TPU v7x, 256 devices: a whole 4x4x8 slice. The times are simulated.
256 devices in a mesh: grp: 8 (over z_lo, core), dev: 32 (over y, z_hi, x).
Axes of the slice: x: 4, y: 4, z: 8 (z_hi: 2, z_lo: 4; z = z_hi * 4 + z_lo), core: 2. Of those that a mesh axis runs over, the one named last changes fastest.
Arguments:
- patches: bfloat16 [8192, 4, 768], P(('grp', 'dev')), may hold values from -6 to 6
- tile_region: int32 [8, 1024], P('grp', 'dev'), may hold values from 0 to 31, as said below
- region_slide: int32 [8, 32], P('grp', 'dev'), may hold values from 0 to 3, never falling along the last dimension, each value on 1 to 16 neighbouring positions
- bin_label: int32 [8, 4], P('grp'), may hold values from 0 to 3
- censored: int32 [8, 4], P('grp'), may hold values 0 or 1
- patch_w: bfloat16 [768, 384], replicated, may hold values from -0.21875 to 0.21875
- tile_qkv: bfloat16 [384, 1152], replicated, may hold values from -0.3125 to 0.3125
- tile_out: bfloat16 [384, 384], replicated, may hold values from -0.3125 to 0.3125
- tile_up: bfloat16 [384, 1536], replicated, may hold values from -0.3125 to 0.3125
- tile_down: bfloat16 [1536, 384], replicated, may hold values from -0.15625 to 0.15625
- region_qkv: bfloat16 [384, 1152], replicated, may hold values from -0.3125 to 0.3125
- region_out: bfloat16 [384, 384], replicated, may hold values from -0.3125 to 0.3125
- region_up: bfloat16 [384, 1536], replicated, may hold values from -0.3125 to 0.3125
- region_down: bfloat16 [1536, 384], replicated, may hold values from -0.15625 to 0.15625
- slide_in: bfloat16 [384, 192], replicated, may hold values from -0.3125 to 0.3125
- slide_qkv: bfloat16 [192, 576], replicated, may hold values from -0.4375 to 0.4375
- slide_out: bfloat16 [192, 192], replicated, may hold values from -0.4375 to 0.4375
- slide_up: bfloat16 [192, 192], replicated, may hold values from -0.4375 to 0.4375
- slide_down: bfloat16 [192, 192], replicated, may hold values from -0.4375 to 0.4375
- slide_head: bfloat16 [192, 4], replicated, may hold values from -0.4375 to 0.4375
Outputs:
- slide_losses: float32 [8, 4], P('grp')
- tile_grads: float32 [2064384], P(('grp', 'dev'))
- region_grads: float32 [1769472], P(('grp', 'dev'))
- slide_grads: float32 [295680], P(('grp', 'dev'))
Inputs may be any that keep to these rules, and one draw needn't show every extreme that they name: `tile_region`: every region of a group holds between 1 and 64 of the group's tiles, and in every group some region holds exactly 64.
All inputs are finite; a program needn't handle non-finite values. No bound on the sum of `censored` on one device may be relied on, other than what follows from the above.
Results may differ from a plain program's by a relative error of at most 0.03.
Values may be sent and summed in bfloat16 or wider, within the bound.
No kernel may reach another device: no remote copies, remote signals or barrier semaphores. Data moves between devices by JAX's collectives and lax.ppermute only.
A program may use at most 128 MiB of HBM per device.

v0:
```python
import math

import jax
import jax.numpy as jnp
from jax import lax
from jax.sharding import PartitionSpec as P

D = 384
HEADS = 6
SLOTS = 64
H_SL = 3
NBINS = 4
SL_GRP = 4


def layer_norm(values):
    average = jnp.mean(values, axis=-1, keepdims=True)
    centred = values - average
    variance = jnp.mean(centred * centred, axis=-1, keepdims=True)
    return centred * lax.rsqrt(variance + 1e-06)


def encoder(stream, allowed, w_qkv, w_out, w_up, w_down, head_count):
    batches, length, feature = stream.shape
    head_size = feature // head_count
    normed = layer_norm(stream).astype(jnp.bfloat16)
    packed = jnp.einsum("bsd,de->bse", normed, w_qkv, preferred_element_type=jnp.float32).astype(
        jnp.bfloat16
    )
    packed = packed.reshape(batches, length, 3, head_count, head_size)
    scores = jnp.einsum(
        "bqhe,bkhe->bhqk", packed[:, :, 0], packed[:, :, 1], preferred_element_type=jnp.float32
    ) / math.sqrt(head_size)
    scores = jnp.where(allowed[:, None], scores, -1e30)
    attend = jax.nn.softmax(scores, axis=-1).astype(jnp.bfloat16)
    mixture = jnp.einsum(
        "bhqk,bkhe->bqhe", attend, packed[:, :, 2], preferred_element_type=jnp.float32
    ).astype(jnp.bfloat16)
    mixture = mixture.reshape(batches, length, feature)
    stream = stream + jnp.einsum("bsd,de->bse", mixture, w_out, preferred_element_type=jnp.float32)
    normed = layer_norm(stream).astype(jnp.bfloat16)
    hidden = jax.nn.gelu(
        jnp.einsum("bsd,de->bse", normed, w_up, preferred_element_type=jnp.float32)
    ).astype(jnp.bfloat16)
    return stream + jnp.einsum("bsd,de->bse", hidden, w_down, preferred_element_type=jnp.float32)


def tile_embed(patch_block, patch_w, w_qkv, w_out, w_up, w_down):
    tile_count, length, pixels = patch_block.shape
    tokens = jnp.einsum("npc,cd->npd", patch_block, patch_w, preferred_element_type=jnp.float32)
    allowed = jnp.ones((tile_count, 1, length), bool)
    tokens = encoder(tokens, allowed, w_qkv, w_out, w_up, w_down, HEADS)
    return jnp.mean(layer_norm(tokens), axis=1).astype(jnp.bfloat16)


def region_embed(tokens, usable, w_qkv, w_out, w_up, w_down):
    stream = encoder(
        tokens.astype(jnp.float32), usable[:, None, :], w_qkv, w_out, w_up, w_down, HEADS
    )
    normed = layer_norm(stream)
    weight = usable.astype(jnp.float32)
    pooled = jnp.sum(normed * weight[:, :, None], axis=1) / jnp.sum(weight, axis=1)[:, None]
    return pooled.astype(jnp.bfloat16)


def slide_loss(embedding, slides, labels, censor_row, slide_in, w_qkv, w_out, w_up, w_down, w_head):
    rows = jnp.dot(embedding, slide_in, preferred_element_type=jnp.float32)[None]
    allowed = (slides[:, None] == slides[None, :])[None]
    rows = encoder(rows, allowed, w_qkv, w_out, w_up, w_down, H_SL)
    normed = layer_norm(rows)[0]
    member = (slides[None, :] == jnp.arange(SL_GRP, dtype=jnp.int32)[:, None]).astype(jnp.float32)
    pooled = (
        jnp.dot(member, normed, precision=lax.Precision.HIGHEST) / jnp.sum(member, axis=1)[:, None]
    )
    logits = jnp.dot(pooled.astype(jnp.bfloat16), w_head, preferred_element_type=jnp.float32)
    log_hazard = jax.nn.log_sigmoid(logits)
    log_stay = jax.nn.log_sigmoid(-logits)
    log_surv = jnp.cumsum(log_stay, axis=-1)
    log_before = log_surv - log_stay
    choose = (labels[:, None] == jnp.arange(NBINS, dtype=jnp.int32)[None, :]).astype(jnp.float32)
    observed = jnp.sum(choose * (log_before + log_hazard), axis=1)
    survived = jnp.sum(choose * log_surv, axis=1)
    weight = censor_row.astype(jnp.float32)
    return -(1.0 - weight) * observed - weight * survived


def slot_table(assign, regions):
    tile_count = assign.shape[0]
    onehot = (assign[:, None] == jnp.arange(regions, dtype=jnp.int32)[None, :]).astype(jnp.int32)
    before = jnp.cumsum(onehot, axis=0) - onehot
    position = jnp.sum(before * onehot, axis=1)
    counts = jnp.sum(onehot, axis=0)
    lookup = jnp.full((regions, SLOTS), tile_count, jnp.int32)
    lookup = lookup.at[assign, position].set(jnp.arange(tile_count, dtype=jnp.int32))
    return (lookup, counts)


def flatten(gradients):
    return jnp.concatenate([gradient.astype(jnp.float32).reshape(-1) for gradient in gradients])


def body(
    patches,
    tile_region,
    region_slide,
    bin_label,
    censored,
    patch_w,
    tile_qkv,
    tile_out,
    tile_up,
    tile_down,
    region_qkv,
    region_out,
    region_up,
    region_down,
    slide_in,
    slide_qkv,
    slide_out,
    slide_up,
    slide_down,
    slide_head,
):
    tile_params = (patch_w, tile_qkv, tile_out, tile_up, tile_down)
    region_params = (region_qkv, region_out, region_up, region_down)
    slide_params = (slide_in, slide_qkv, slide_out, slide_up, slide_down, slide_head)
    member_index = lax.axis_index("dev")
    scaling = 1.0 / (bin_label.shape[1] * lax.axis_size("grp"))
    embeds, tile_pullback = jax.vjp(lambda *params: tile_embed(patches, *params), *tile_params)
    group_assign, group_slides = (
        lax.all_gather(tile_region, "dev", axis=1, tiled=True),
        lax.all_gather(region_slide, "dev", axis=1, tiled=True),
    )
    group_rows = lax.all_gather(embeds, "dev", axis=0, tiled=True)
    region_total = group_slides.shape[1]
    region_local = region_slide.shape[1]
    tile_total = group_assign.shape[1]
    lookup_all, counts_all = slot_table(group_assign[0], region_total)
    first_region = member_index * region_local
    lookup = lax.dynamic_slice_in_dim(lookup_all, first_region, region_local, 0)
    counts = lax.dynamic_slice_in_dim(counts_all, first_region, region_local, 0)
    usable = jnp.arange(SLOTS, dtype=jnp.int32)[None, :] < counts[:, None]
    padded = jnp.concatenate([group_rows, jnp.zeros((1, D), jnp.bfloat16)], axis=0)
    region_tokens = padded[lookup]
    region_embs, region_pullback = jax.vjp(
        lambda tokens, *params: region_embed(tokens, usable, *params), region_tokens, *region_params
    )
    all_regions = lax.all_gather(region_embs, "dev", axis=0, tiled=True)
    losses, slide_pullback = jax.vjp(
        lambda emb_rows, *params: slide_loss(
            emb_rows, group_slides[0], bin_label[0], censored[0], *params
        ),
        all_regions,
        *slide_params
    )
    slide_cots = slide_pullback(jnp.full(losses.shape, scaling, jnp.float32))
    own_cot = lax.dynamic_slice_in_dim(slide_cots[0], first_region, region_local, 0)
    region_cots = region_pullback(own_cot)
    slot_cot = region_cots[0].reshape(-1, D)
    spread = jnp.zeros((tile_total + 1, D), jnp.bfloat16)
    spread = spread.at[lookup.reshape(-1)].set(slot_cot)[:tile_total]
    tile_cot = (
        lax.psum_scatter(spread, "dev", scatter_dimension=0, tiled=True)
        .astype(jnp.float32)
        .astype(jnp.bfloat16)
    )
    tile_grads = tile_pullback(tile_cot)
    tile_flat = flatten(tile_grads)
    region_flat = flatten(region_cots[1:])
    slide_flat = flatten(slide_cots[1:])
    keeping = (member_index == 0).astype(jnp.float32)
    totals = (tile_flat, region_flat, slide_flat * keeping)
    reduced = (
        lax.psum_scatter(totals[0], ("grp", "dev"), scatter_dimension=0, tiled=True),
        lax.psum_scatter(totals[1], ("grp", "dev"), scatter_dimension=0, tiled=True),
        lax.psum_scatter(totals[2], ("grp", "dev"), scatter_dimension=0, tiled=True),
    )
    slide_result = reduced[2]
    return (losses[None, :], reduced[0], reduced[1], slide_result)


def solution(mesh):
    placed = (
        P(("grp", "dev"), None, None),
        P("grp", "dev"),
        P("grp", "dev"),
        P("grp", None),
        P("grp", None),
        P(),
        P(),
        P(),
        P(),
        P(),
        P(),
        P(),
        P(),
        P(),
        P(),
        P(),
        P(),
        P(),
        P(),
        P(),
    )
    return jax.shard_map(
        body,
        mesh=mesh,
        in_specs=placed,
        out_specs=(P("grp", None), P(("grp", "dev")), P(("grp", "dev")), P(("grp", "dev"))),
        check_vma=False,
    )
```

profile of v0, /device:TPU:32, one launch (start us, length us, event | category | flops | bytes accessed | tf_op | source)
XLA Modules:
  0.0 781.9 jit_solution(17429410486698957842)
XLA Ops:
  8.9 1.3 dynamic-slice
  12.3 24.7 %all-reduce.15 = (s32[1024]{0:T(1024)S(1)}, s32[32]{0:T(128)S(1)}) all-reduce(s32[1024]{0:T(1024)S(1)} %bitcast_dynamic-update-slice_fusion, s32[32]{0:T(128)S(1)} %bitcast_dynamic-update-slice_fusion.1), channel_id=1, replica_groups=mesh['grp'=8,'dev'=32] {'dev'}, use_global_device_ids=true, to_apply=%add.11 | all-reduce | flops 1056 | bytes 8448
  37.0 9.0 %reduce-window.6 = s32[32,8,128]{2,1,0:T(8,128)S(1)} reduce-window(s32[32,8,128]{2,1,0:T(8,128)S(1)} %fusion.91, s32[]{:T(128)} %constant.142.clone.1), window={size=1x1x128 pad=0_0x0_0x127_0}, to_apply=%region_9.10 | reduce-window | flops 4161536 | bytes 262148 | tf_op jit(solution)/shard_map/reduce-window
  48.5 1.2 fusion.166
  51.3 4.3 scatter_custom_fusion.1
  61.0 1.2 fusion.193
  66.3 112.3 %all_gather.13 = bf16[1024,384]{1,0:T(8,128)(2,1)S(1)} all-gather(bf16[32,384]{1,0:T(8,128)(2,1)S(1)} %multiply_convert_fusion.5), channel_id=1, replica_groups=mesh['grp'=8,'dev'=32] {'dev'}, dimensions={0}, use_global_device_ids=true | all-gather | bytes 811008 | tf_op jit(solution)/shard_map/all_gather | solution.py:134
  178.6 1.0 concatenate.24
  179.6 1.9 gather_fusion
  184.2 1.3 fusion.195
  186.3 1.4 fusion.196
  192.0 107.9 %all-gather.1 = bf16[32,1,384]{2,1,0:T(2,128)(2,1)S(1)} all-gather(bf16[1,1,384]{2,1,0:T(2,128)(2,1)S(1)} %reshape.1251), channel_id=2, replica_groups=mesh['grp'=8,'dev'=32] {'dev'}, dimensions={0}, use_global_device_ids=true | all-gather | bytes 25344 | tf_op jit(solution)/shard_map/all_gather | solution.py:148
  302.3 1.5 reshape.1181
  303.9 1.4 fusion.190
  305.3 2.1 fusion.199
  307.5 1.3 multiply_divide_fusion.2
  308.7 1.0 fusion.48
  310.4 1.2 fusion.200
  312.3 1.1 fusion.179
  314.0 1.1 fusion.201
  315.4 1.3 multiply_bitcast_fusion.1
  318.4 1.3 fusion.157
  323.8 1.1 fusion.127
  324.9 1.2 multiply_reduce_fusion.15
  327.7 1.0 fusion.203
  329.5 1.0 multiply_reduce_fusion.13
  330.5 1.0 fusion.50
  334.1 1.6 reshape.1189
  335.8 1.1 multiply_reduce_fusion.14
  338.4 1.1 fusion.143
  341.2 1.9 fusion.77
  345.8 1.3 fusion.40
  348.4 1.4 scatter_custom_fusion
  349.7 1.0 slice.61
  350.9 1.6 convolution_convert_fusion.1
  352.6 2.5 convolution_convert_fusion.2
  355.3 1.1 convolution_convert_fusion.7
  356.4 1.4 convolution_convert_fusion
  361.9 1.6 reshape.1203
  363.5 3.7 reshape.1202
  367.4 1.8 reshape.1200
  370.3 1.7 constant_dynamic-update-slice_fusion.10
  372.0 1.0 reshape.1205
  373.0 1.0 reshape.1206
  374.0 1.0 reshape.1207
  375.1 1.0 reshape.1208
  376.4 1.7 constant_dynamic-update-slice_fusion.8
  380.6 18.4 %maximum_convert_fusion = f32[1769472]{0:T(1024)} fusion(bf16[589824]{0:T(1024)(128)(2,1)S(1)} %copy-done.5, bf16[589824]{0:T(1024)(128)(2,1)} %reshape.1202, bf16[147456]{0:T(1024)(128)(2,1)S(1)} %reshape.1201, bf16[442368]{0:T(1024)(128)(2,1)S(1)} %copy-done.11), kind=kLoop, calls=%fused_computation.6 | loop fusion | flops 14155776 | bytes 10616832 | tf_op jit(solution)/shard_map/concatenate | solution.py:99
  399.1 1.1 convert_multiply_fusion
  402.3 195.1 %reduce-scatter.2.cloned.1.call-done = bf16[32,384]{1,0:T(8,128)(2,1)} async-done(((bf16[1024,384]{1,0:T(8,128)(2,1)}), bf16[32,384]{1,0:T(8,128)(2,1)}) %reduce-scatter.2.cloned.1.call-update) | async-done | bytes 24592 | tf_op jit(solution)/shard_map/reduce_scatter | solution.py:163
  601.6 1.5 multiply_reduce_fusion
  608.0 1.0 fusion.11
  609.0 1.6 fusion.5
  610.6 1.6 fusion.3
  614.4 1.9 reshape.1196
  616.4 1.3 reshape.1198
  617.8 2.3 reshape.1199
  620.1 2.2 constant_dynamic-update-slice_fusion
  623.0 1.2 constant_dynamic-update-slice_fusion.3
  624.2 1.2 constant_dynamic-update-slice_fusion.2
  625.3 144.6 %all-reduce.21 = f32[2064384]{0:T(1024)} all-reduce(bf16[2064384]{0:T(1024)(128)(2,1)} %constant_dynamic-update-slice_fusion.2), channel_id=4, replica_groups=mesh['grp'=8,'dev'=32] {'grp','dev'}, use_global_device_ids=true, to_apply=%region_60.62.clone | all-reduce | flops 2064384 | bytes 12386304
  769.9 1.5 dynamic-slice.2
  771.4 1.4 dynamic-slice.3
  772.8 1.4 dynamic-slice.4
  (516 shorter events, 66.2 us)
Async XLA Ops:
  8.0 56.0 %copy-start = (bf16[1536,384]{1,0:T(8,128)(2,1)S(1)}, bf16[1536,384]{1,0:T(8,128)(2,1)}, u32[]{:S(2)}) copy-start(bf16[1536,384]{1,0:T(8,128)(2,1)} %param.30) | copy-start | bytes 3538948
  8.0 43.1 %copy-start.162 = (s32[2]{0:T(128)S(1)}, s32[2]{0:T(128)}, u32[]{:S(2)}) copy-start(s32[2]{0:T(128)} %constant.182) | copy-start | bytes 28
  8.0 43.1 %copy-start.161 = (s32[2]{0:T(128)S(1)}, s32[2]{0:T(128)}, u32[]{:S(2)}) copy-start(s32[2]{0:T(128)} %constant.179) | copy-start | bytes 28
  8.0 48.2 %copy-start.34 = (bf16[768,384]{1,0:T(8,128)(2,1)S(1)}, bf16[768,384]{1,0:T(8,128)(2,1)}, u32[]{:S(2)}) copy-start(bf16[768,384]{1,0:T(8,128)(2,1)} %param.26) | copy-start | bytes 1769476
  8.1 48.2 %copy-start.63 = (bf16[32,4,768]{2,1,0:T(4,128)(2,1)S(1)}, bf16[32,4,768]{2,1,0:T(4,128)(2,1)}, u32[]{:S(2)}) copy-start(bf16[32,4,768]{2,1,0:T(4,128)(2,1)} %param.21) | copy-start | bytes 589828
  8.1 589.3 %reduce-scatter.2.cloned.1.call-start = ((), (), s32[]{:S(2)}) async-start(), calls=%async_computation.1 | async-start | bytes 811008 | tf_op jit(solution)/shard_map/reduce_scatter | solution.py:163
  37.0 19.7 %copy-start.135 = (s32[32]{0:T(128)}, s32[32]{0:T(128)S(1)}, u32[]{:S(2)}) copy-start(s32[32]{0:T(128)S(1)} %get-tuple-element.17) | copy-start | bytes 388
  37.0 19.9 %copy-start.8 = (bf16[384,1152]{1,0:T(8,128)(2,1)S(1)}, bf16[384,1152]{1,0:T(8,128)(2,1)}, u32[]{:S(2)}) copy-start(bf16[384,1152]{1,0:T(8,128)(2,1)} %param.27) | copy-start | bytes 2654212
  47.9 136.3 %copy-start.166 = (pred[64]{0:T(512)(128)(4,1)}, pred[64]{0:T(512)(128)(4,1)S(1)}, u32[]{:S(2)}) copy-start(pred[64]{0:T(512)(128)(4,1)S(1)} %iota_compare_fusion.6) | copy-start | bytes 196
  48.5 142.8 %copy-start.95 = (f32[64]{0:T(128)}, f32[64]{0:T(128)S(1)}, u32[]{:S(2)}) copy-start(f32[64]{0:T(128)S(1)} %fusion.178) | copy-start | bytes 772
  59.4 4.2 copy-start.3
  178.6 3.8 copy-start.6
  184.0 4.5 copy-start.68
  184.0 5.1 copy-start.2
  185.5 4.0 copy-start.136
  186.3 3.9 copy-start.17
  190.2 109.7 %copy-start.33 = (bf16[384,192]{0,1:T(8,128)(2,1)S(1)}, bf16[384,192]{0,1:T(8,128)(2,1)}, u32[]{:S(2)}) copy-start(bf16[384,192]{0,1:T(8,128)(2,1)} %param.35) | copy-start | bytes 442372
  190.2 111.3 %copy-start.22 = (bf16[192,576]{1,0:T(8,128)(2,1)S(1)}, bf16[192,576]{1,0:T(8,128)(2,1)}, u32[]{:S(2)}) copy-start(bf16[192,576]{1,0:T(8,128)(2,1)} %param.36) | copy-start | bytes 663556
  190.6 109.6 %copy-start.86 = (f32[64]{0:T(128)}, f32[64]{0:T(128)S(1)}, u32[]{:S(2)}) copy-start(f32[64]{0:T(128)S(1)} %broadcast_multiply_fusion.6) | copy-start | bytes 772
  299.9 12.4 %copy-start.56 = (bf16[32,1,384]{2,1,0:T(2,128)(2,1)}, bf16[32,1,384]{2,1,0:T(2,128)(2,1)S(1)}, u32[]{:S(2)}) copy-start(bf16[32,1,384]{2,1,0:T(2,128)(2,1)S(1)} %all-gather.1) | copy-start | bytes 73732
  311.6 3.6 copy-start.126
  312.3 6.0 copy-start.142
  323.8 3.8 copy-start.44
  323.8 3.9 copy-start.144
  327.7 13.4 %copy-start.26 = (f32[32,192]{1,0:T(8,128)}, f32[32,192]{1,0:T(8,128)S(1)}, u32[]{:S(2)}) copy-start(f32[32,192]{1,0:T(8,128)S(1)} %add_add_fusion.13) | copy-start | bytes 73732
  329.5 6.3 copy-start.117
  329.5 10.5 %copy-start.87 = (f32[64]{0:T(128)S(1)}, f32[64]{0:T(128)}, u32[]{:S(2)}) copy-start(f32[64]{0:T(128)} %copy-done.86) | copy-start | bytes 772
  329.5 10.5 %copy-start.96 = (f32[64]{0:T(128)S(1)}, f32[64]{0:T(128)}, u32[]{:S(2)}) copy-start(f32[64]{0:T(128)} %copy-done.95) | copy-start | bytes 772
  329.5 11.4 %copy-start.112 = (f32[64]{0:T(128)S(1)}, f32[64]{0:T(128)}, u32[]{:S(2)}) copy-start(f32[64]{0:T(128)} %copy-done.111) | copy-start | bytes 772
  340.1 4.0 copy-start.71
  344.0 4.2 copy-start.24
  350.8 420.6 %all-reduce.20.cloned.1.call-start = ((), (), s32[]{:S(2)}) async-start(), calls=%async_computation.2 | async-start | bytes 16523264
  350.8 4.3 copy-start.25
  350.8 4.3 copy-start.37
  350.8 4.3 copy-start.73
  350.9 4.3 copy-start.90
  350.9 4.3 copy-start.99
  350.9 4.3 copy-start.115
  350.9 4.3 copy-start.125
  350.9 4.3 copy-start.132
  350.9 4.3 copy-start.141
  352.5 3.8 copy-start.94
  352.6 3.8 copy-start.122
  355.2 3.6 copy-start.43
  355.2 3.6 copy-start.118
  355.2 3.9 copy-start.65
  355.3 4.7 copy-start.79
  355.3 4.7 copy-start.127
  355.3 4.7 copy-start.143
  356.4 4.6 copy-start.45
  356.4 4.6 copy-start.67
  356.4 4.6 copy-start.145
  356.4 5.4 copy-start.151
  356.4 5.4 copy-start.165
  363.5 3.7 copy-start.19
  363.5 3.9 copy-start.10
  370.3 10.3 %copy-start.5 = (bf16[589824]{0:T(1024)(128)(2,1)S(1)}, bf16[589824]{0:T(1024)(128)(2,1)}, u32[]{:S(2)}) copy-start(bf16[589824]{0:T(1024)(128)(2,1)} %reshape.1203) | copy-start | bytes 3538948
  376.4 4.2 copy-start.11
  380.6 18.4 %copy-start.23 = (bf16[295680]{0:T(1024)(128)(2,1)S(1)}, bf16[295680]{0:T(1024)(128)(2,1)}, u32[]{:S(2)}) copy-start(bf16[295680]{0:T(1024)(128)(2,1)} %constant_dynamic-update-slice_fusion.1) | copy-start | bytes 1774084
  400.2 198.0 %copy-start.75 = (f32[32,4]{0,1:T(4,128)S(1)}, f32[32,4]{0,1:T(4,128)}, u32[]{:S(2)}) copy-start(f32[32,4]{0,1:T(4,128)} %copy-done.74) | copy-start | bytes 1540
  400.2 198.1 %copy-start.107 = (f32[32,4]{0,1:T(4,128)S(1)}, f32[32,4]{0,1:T(4,128)}, u32[]{:S(2)}) copy-start(f32[32,4]{0,1:T(4,128)} %copy-done.106) | copy-start | bytes 1540
  400.2 198.2 %copy-start.83 = (f32[32,4]{0,1:T(4,128)S(1)}, f32[32,4]{0,1:T(4,128)}, u32[]{:S(2)}) copy-start(f32[32,4]{0,1:T(4,128)} %copy-done.82) | copy-start | bytes 1540
  400.2 198.4 %copy-start.29 = (f32[32,4,1536]{2,0,1:T(8,128)S(1)}, f32[32,4,1536]{2,0,1:T(8,128)}, u32[]{:S(2)}) copy-start(f32[32,4,1536]{2,0,1:T(8,128)} %copy-done.28) | copy-start | bytes 2359300
  625.3 148.9 %copy-start.1 = (bf16[1536,384]{1,0:T(8,128)(2,1)S(1)}, bf16[1536,384]{1,0:T(8,128)(2,1)}, u32[]{:S(2)}) copy-start(bf16[1536,384]{1,0:T(8,128)(2,1)} %param.30) | copy-start | bytes 3538948
  (106 other events, 147.2 us)
Sparse Core Ops, SparseCore 0:
  350.9 246.4 reduce-scatter.1
Sparse Core Ops, SparseCore 1:
  400.3 273.9 all-reduce.19
where the time goes:
time: 791 us; the launch traced here: 782 us
  blocking collectives  389 us (49%)
  waiting for transfers between devices  195 us (25%)
  local copies, waits for them, and re-layouts  70.3 us (9%)
  matrix products  54.2 us (7%)
  other arithmetic  53 us (7%)
  between operations  19.6 us (2%)
    reduce_scatter x1, waiting for transfers between devices, body(): lax.psum_scatter(spread, 'dev', scatter_dimension=0, tiled=True)  195 us
    unnamed x2, blocking collectives  169 us
    all_gather x1, blocking collectives, body(): group_rows = lax.all_gather(embeds, 'dev', axis=0, tiled=True)  112 us
    all_gather x1, blocking collectives, body(): all_regions = lax.all_gather(region_embs, 'dev', axis=0, tiled=True)  108 us
    unnamed x356, local copies, waits for them, and re-layouts  34.4 us
    concatenate x1, other arithmetic, flatten(): jnp.concatenate([gradient.astype(jnp.float32).reshape(-1) for gradient in...  18.4 us
    reshape x15, local copies, waits for them, and re-layouts, flatten(): gradient.astype(jnp.float32).reshape(-1)  18.4 us
  transfers between devices with their start and end apart: 2, of which 1 were waited for; matrix products, arithmetic and copies ran while one was open for 10% of the time, Pallas kernels for 0%

commit v1 on v0

v1 whole, which is shorter than its diff:
```python
import functools
import math

import jax
import jax.numpy as jnp
from jax import lax
from jax.experimental import pallas as pl
from jax.experimental.pallas import tpu as pltpu
from jax.sharding import PartitionSpec as P

D = 384
HEADS = 6
FF = 1536
PATCHES = 4
SLOTS = 64
D_SL = 192
H_SL = 3
NBINS = 4
SL_GRP = 4
HEAD = 64
F32 = jnp.float32
BF16 = jnp.bfloat16
LANES = 128
GELU_C = math.sqrt(2.0 / math.pi)


def mm(a, b):
    return jnp.dot(a, b, preferred_element_type=F32)


def mm_nt(a, b):
    return lax.dot_general(a, b, (((1,), (1,)), ((), ())), preferred_element_type=F32)


def mm_tn(a, b):
    return lax.dot_general(a, b, (((0,), (0,)), ((), ())), preferred_element_type=F32)


def norm_parts(x):
    average = jnp.mean(x, axis=-1, keepdims=True)
    centred = x - average
    variance = jnp.mean(centred * centred, axis=-1, keepdims=True)
    rstd = lax.rsqrt(variance + 1e-06)
    return centred * rstd, rstd


def norm_back(grad, normed, rstd):
    first = jnp.mean(grad, axis=-1, keepdims=True)
    second = jnp.mean(grad * normed, axis=-1, keepdims=True)
    return rstd * (grad - first - normed * second)


def gelu_parts(x):
    t = jnp.tanh(GELU_C * (x + 0.044715 * (x * x * x)))
    value = 0.5 * x * (1.0 + t)
    slope = 0.5 * (1.0 + t) + 0.5 * x * (1.0 - t * t) * (GELU_C * (1.0 + 3.0 * 0.044715 * (x * x)))
    return value, slope


def encode(x, allowed, w_qkv, w_out, w_up, w_down, heads, res):
    packed_ref, attend_ref, mixture_ref, mid_ref, up_ref, out_ref = res
    width = x.shape[1]
    normed, _ = norm_parts(x)
    packed_ref[...] = mm(normed.astype(BF16), w_qkv[...]).astype(BF16)
    send(packed_ref)
    for h in range(heads):
        q = packed_ref[:, h * HEAD : (h + 1) * HEAD]
        k = packed_ref[:, width + h * HEAD : width + (h + 1) * HEAD]
        v = packed_ref[:, 2 * width + h * HEAD : 2 * width + (h + 1) * HEAD]
        scores = jnp.where(allowed, mm_nt(q, k) * 0.125, -1e30)
        scores = jnp.exp(scores - jnp.max(scores, axis=-1, keepdims=True))
        weights = scores / jnp.sum(scores, axis=-1, keepdims=True)
        attend_ref[h] = weights
        mixture_ref[:, h * HEAD : (h + 1) * HEAD] = mm(weights.astype(BF16), v).astype(BF16)
    send(attend_ref)
    send(mixture_ref)
    x1 = x + mm(mixture_ref[...], w_out[...])
    mid_ref[...] = x1
    send(mid_ref)
    normed, _ = norm_parts(x1)
    up = mm(normed.astype(BF16), w_up[...])
    up_ref[...] = up
    send(up_ref)
    hidden, _ = gelu_parts(up)
    out = x1 + mm(hidden.astype(BF16), w_down[...])
    out_ref[...] = out
    send(out_ref)
    return out


def encode_back(grad, x, w_qkv, w_out, w_up, w_down, heads, res, packed_grad, put):
    packed_ref, attend_ref, mixture_ref, mid_ref, up_ref, _ = res
    width = x.shape[1]
    grad_b = grad.astype(BF16)
    hidden, slope = gelu_parts(up_ref[...])
    up_grad = (mm_nt(grad_b, w_down[...]).astype(BF16).astype(F32) * slope).astype(BF16)
    put(3, hidden.astype(BF16), grad_b)
    normed, rstd = norm_parts(mid_ref[...])
    put(2, normed.astype(BF16), up_grad)
    normed_grad = mm_nt(up_grad, w_up[...]).astype(BF16).astype(F32)
    mid_grad = grad + norm_back(normed_grad, normed, rstd)
    mid_b = mid_grad.astype(BF16)
    put(1, mixture_ref[...], mid_b)
    mix_grad = mm_nt(mid_b, w_out[...]).astype(BF16)
    for h in range(heads):
        q = packed_ref[:, h * HEAD : (h + 1) * HEAD]
        k = packed_ref[:, width + h * HEAD : width + (h + 1) * HEAD]
        v = packed_ref[:, 2 * width + h * HEAD : 2 * width + (h + 1) * HEAD]
        head_grad = mix_grad[:, h * HEAD : (h + 1) * HEAD]
        weights = attend_ref[h]
        weights_grad = mm_nt(head_grad, v).astype(BF16).astype(F32)
        v_grad = mm_tn(weights.astype(BF16), head_grad)
        inner = jnp.sum(weights_grad * weights, axis=-1, keepdims=True)
        scores_grad = (weights * (weights_grad - inner) * 0.125).astype(BF16)
        packed_grad[:, h * HEAD : (h + 1) * HEAD] = mm(scores_grad, k).astype(BF16)
        packed_grad[:, width + h * HEAD : width + (h + 1) * HEAD] = mm_tn(scores_grad, q).astype(BF16)
        packed_grad[:, 2 * width + h * HEAD : 2 * width + (h + 1) * HEAD] = v_grad.astype(BF16)
    normed, rstd = norm_parts(x)
    put(0, normed.astype(BF16), packed_grad[...])
    normed_grad = mm_nt(packed_grad[...], w_qkv[...]).astype(BF16).astype(F32)
    return mid_grad + norm_back(normed_grad, normed, rstd)


def put_rows(flat, base, a, b):
    rows, columns = a.shape[1], b.shape[1]
    chunks = columns // 128
    left = a.T
    for c in range(0, chunks, 3):
        part = mm(left, b[:, c * 128 : (c + 3) * 128]).astype(BF16).astype(F32)
        for j in range(3):
            flat[pl.ds(base + c + j, rows, stride=chunks), :] = part[:, j * 128 : (j + 1) * 128]


def same_tile():
    row = lax.broadcasted_iota(jnp.int32, (128, 128), 0)
    column = lax.broadcasted_iota(jnp.int32, (128, 128), 1)
    return lax.rem(row, 32) == lax.rem(column, 32)


class Late:
    def __init__(self, source, buffer, sem):
        self.copy = pltpu.make_async_copy(source, buffer, sem)
        self.buffer, self.here = buffer, False
        self.copy.start()

    def ref(self):
        if not self.here:
            self.copy.wait()
            self.here = True
        return self.buffer

    def __getitem__(self, index):
        return self.ref()[index]


class Early:
    def __init__(self, target, buffer, sem):
        self.copy = pltpu.make_async_copy(buffer, target, sem)
        self.buffer = buffer

    def __getitem__(self, index):
        return self.buffer[index]

    def __setitem__(self, index, value):
        self.buffer[index] = value

    def finish(self):
        self.copy.wait()


def send(ref):
    if isinstance(ref, Early):
        ref.copy.start()


def broadcast_out(block, out, sems):
    copies = [pltpu.make_async_copy(block, out.at[i], sems.at[i]) for i in range(32)]
    for copy in copies:
        copy.start()
    for copy in copies:
        copy.wait()


def tile_forward(where, ids, slide, *refs):
    ins, outs, bufs, obufs, block, sems, osems, bsems = cut(refs, 6, 8, 6, 7, 1, 1, 1, 1)
    late = [Late(r, b, sems[0].at[i]) for i, (r, b) in enumerate(zip(ins, bufs))]
    res = [Early(r, b, osems[0].at[i]) for i, (r, b) in enumerate(zip(outs[1:], obufs))]
    patches, patch_w, w_qkv, w_out, w_up, w_down = late
    x = mm(patches[...], patch_w[...])
    res[0][...] = x
    send(res[0])
    out = encode(x, same_tile(), w_qkv, w_out, w_up, w_down, HEADS, res[1:])
    normed, _ = norm_parts(out)
    total = (normed[0:32] + normed[32:64]) + (normed[64:96] + normed[96:128])
    total = (total * 0.25).astype(BF16)
    message = block[0]
    for c in range(3):
        message[c * 32 : (c + 1) * 32, :] = total[:, c * LANES : (c + 1) * LANES]
    row = lax.broadcasted_iota(jnp.int32, (16, LANES), 0)
    lane = lax.broadcasted_iota(jnp.int32, (16, LANES), 1)
    mine = (lane >= 32 * lax.rem(where[0], 4)) & (lane < 32 * lax.rem(where[0], 4) + 32)
    tail = jnp.where((row == 0) & mine, ids[...].astype(F32), 0.0) + jnp.where(row == 1, slide[...].astype(F32), 0.0)
    message[96:112, :] = tail.astype(BF16)
    broadcast_out(message, outs[0], bsems[0])
    for r in res:
        r.finish()


def cut(refs, *sizes):
    parts, at = [], 0
    for size in sizes:
        parts.append(refs[at : at + size])
        at += size
    assert at == len(refs)
    return parts


def tails_of(tails):
    tails = tails.astype(F32)
    row = lax.broadcasted_iota(jnp.int32, tails.shape, 1)
    ids = jnp.sum(jnp.where(row == 0, tails, 0.0), axis=1)
    slides = jnp.sum(jnp.where(row == 1, tails, 0.0), axis=1)
    to = lax.broadcasted_iota(jnp.int32, (8, 32), 0)
    source = lax.broadcasted_iota(jnp.int32, (8, 32), 1)
    near = (source >= 4 * to) & (source < 4 * to + 4)
    ids = mm(jnp.where(near, 1.0, 0.0).astype(BF16), ids.astype(BF16))
    return ids, slides[:, 0:1]


def slots_of(ids, region):
    member = jnp.where(ids == region.astype(F32), 1.0, 0.0)
    row = lax.broadcasted_iota(jnp.int32, (128, 128), 0)
    column = lax.broadcasted_iota(jnp.int32, (128, 128), 1)
    within = mm(member.astype(BF16), jnp.where(row < column, 1.0, 0.0).astype(BF16))
    sums = jnp.sum(member, axis=1, keepdims=True)
    row8 = lax.broadcasted_iota(jnp.int32, (8, 8), 0)
    column8 = lax.broadcasted_iota(jnp.int32, (8, 8), 1)
    earlier = jnp.where(column8 < row8, 1.0, 0.0).astype(BF16)
    ahead = mm(earlier, jnp.broadcast_to(sums, (8, 128)).astype(BF16))
    count = jnp.sum(sums, axis=0, keepdims=True)
    return member, (within + ahead).astype(jnp.int32), count


def choice(member, slot, b):
    k = lax.broadcasted_iota(jnp.int32, (SLOTS, 128), 0)
    return jnp.where((slot[b : b + 1] == k) & (member[b : b + 1] > 0.0), 1.0, 0.0).astype(BF16)


def region_forward(where, *refs):
    ins, outs, bufs, obufs, block, sems, osems, bsems = cut(refs, 5, 8, 5, 7, 1, 1, 1, 1)
    late = [Late(r, b, sems[0].at[i]) for i, (r, b) in enumerate(zip(ins, bufs))]
    res = [Early(r, b, osems[0].at[i]) for i, (r, b) in enumerate(zip(outs[1:], obufs))]
    rows, w_qkv, w_out, w_up, w_down = late
    ids, _ = tails_of(rows[:, 96:112, :])
    member, slot, count = slots_of(ids, where[0])
    parts = [jnp.zeros((SLOTS, LANES), F32)] * 3
    for b in range(8):
        pick = choice(member, slot, b)
        for c in range(3):
            block_rows = rows[4 * b : 4 * b + 4, 32 * c : 32 * c + 32, :].reshape(128, LANES)
            parts[c] = parts[c] + mm(pick, block_rows)
    for c in range(3):
        res[0][:, c * LANES : (c + 1) * LANES] = parts[c]
    send(res[0])
    key = lax.broadcasted_iota(jnp.int32, (SLOTS, SLOTS), 1).astype(F32)
    out = encode(res[0][...], key < count, w_qkv, w_out, w_up, w_down, HEADS, res[1:])
    normed, _ = norm_parts(out)
    usable = lax.broadcasted_iota(jnp.int32, (SLOTS, 1), 0).astype(F32) < count
    total = jnp.sum(jnp.where(usable, normed, 0.0), axis=0, keepdims=True)
    embed = (total / count).astype(BF16).astype(F32)
    message = block[0]
    message[...] = jnp.zeros((8, LANES), F32)
    for c in range(3):
        message[c : c + 1, :] = embed[:, c * LANES : (c + 1) * LANES]
    broadcast_out(message, outs[0], bsems[0])
    for r in res:
        r.finish()


def slide_step(embeds, slide_row, slide_col, label, censor, slide_in, w_qkv, w_out, w_up, w_down, head, losses, grads, res, packed_grad, scaling):
    emb = embeds[...]
    x = mm(emb, slide_in[...])
    out = encode(x, slide_col == slide_row, w_qkv, w_out, w_up, w_down, H_SL, res)
    normed, rstd = norm_parts(out)
    sums, sizes, masks = [], [], []
    for s in range(SL_GRP):
        mask = jnp.where(slide_col == float(s), 1.0, 0.0)
        size = jnp.sum(mask, axis=0, keepdims=True)
        masks.append(mask)
        sizes.append(size)
        sums.append(jnp.sum(mask * normed, axis=0, keepdims=True) / size)
    pooled = jnp.concatenate(sums, axis=0).astype(BF16)
    logits = mm(pooled, head[...])
    soft = jnp.log1p(jnp.exp(-jnp.abs(logits)))
    log_hazard = -(jnp.maximum(-logits, 0.0) + soft)
    log_stay = -(jnp.maximum(logits, 0.0) + soft)
    bin_at = lax.broadcasted_iota(jnp.int32, (SL_GRP, NBINS), 1)
    at = (bin_at == label[...]).astype(F32)
    before = (bin_at < label[...]).astype(F32)
    held = censor[...].astype(F32)
    past = jnp.sum(before * log_stay, axis=1, keepdims=True)
    seen = past + jnp.sum(at * log_hazard, axis=1, keepdims=True)
    lived = past + jnp.sum(at * log_stay, axis=1, keepdims=True)
    losses[...] = -(1.0 - held) * seen - held * lived
    chance = 1.0 / (1.0 + jnp.exp(-logits))
    logit_grad = (scaling * (before * chance + at * (chance - (1.0 - held)))).astype(BF16)
    grads[5][...] = mm_tn(pooled, logit_grad).astype(BF16)
    pooled_grad = mm_nt(logit_grad, head[...]).astype(BF16).astype(F32)
    grad = jnp.zeros_like(normed)
    for s in range(SL_GRP):
        grad = grad + masks[s] * (pooled_grad[s : s + 1] / sizes[s])
    grad = norm_back(grad, normed, rstd)

    def put(i, a, b):
        grads[i + 1][...] = mm_tn(a, b).astype(BF16)

    grad = encode_back(grad, x, w_qkv, w_out, w_up, w_down, H_SL, res, packed_grad, put).astype(BF16)
    grads[0][...] = mm_tn(emb, grad).astype(BF16)
    return mm_nt(grad, slide_in[...]).astype(BF16)


def region_backward(scaling, where, label, censor, *refs):
    ins, outs, bufs, obufs, extra, sems, osems = cut(refs, 19, 15, 19, 15, 9, 1, 1)
    order = list(range(8)) + [18, 13, 17, 16, 14, 15, 9, 8, 10, 11, 12]
    late = dict()
    for i in list(dict.fromkeys(order)):
        late[i] = Late(ins[i], bufs[i], sems[0].at[i])
    early = [Early(r, b, osems[0].at[i]) for i, (r, b) in enumerate(zip(outs, obufs))]
    message, tails = late[0], late[1]
    slide_weights = [late[i] for i in range(2, 8)]
    w_qkv, w_out, w_up, w_down = [late[i] for i in range(8, 12)]
    x_ref, res = late[12], [late[i] for i in range(13, 19)]
    losses, spread, pairs, slide_grads = early[0], early[1], early[2:9], early[9:15]
    packed_grad, slide_packed_grad, embeds = extra[:3]
    ids, slide_col = tails_of(tails[...])
    rows32 = lax.broadcasted_iota(jnp.int32, (32, 32), 0)
    columns32 = lax.broadcasted_iota(jnp.int32, (32, 32), 1)
    slide_row = jnp.sum(jnp.where(rows32 == columns32, slide_col, 0.0), axis=0, keepdims=True)
    arrived = message[...]
    at = lax.broadcasted_iota(jnp.int32, arrived.shape, 1)
    for c in range(3):
        part = jnp.sum(jnp.where(at == c, arrived, 0.0), axis=1)
        embeds[:, c * LANES : (c + 1) * LANES] = part.astype(BF16)
    cots = slide_step(
        embeds, slide_row, slide_col, label, censor, *slide_weights, losses, slide_grads, extra[3:9], slide_packed_grad, scaling
    ).astype(F32)
    for g in [losses] + slide_grads:
        send(g)
    mine = lax.broadcasted_iota(jnp.int32, (32, 1), 0) == where[0]
    own = jnp.sum(jnp.where(mine, cots, 0.0), axis=0, keepdims=True)
    member, slot, count = slots_of(ids, where[0])
    usable = lax.broadcasted_iota(jnp.int32, (SLOTS, 1), 0).astype(F32) < count
    grad = jnp.where(usable, own / count, 0.0)
    normed, rstd = norm_parts(res[5][...])
    grad = norm_back(grad, normed, rstd)

    def put(i, a, b):
        at = {3: 0, 2: 2, 1: 4, 0: 5}[i]
        if i != 1:
            pairs[at][...] = a
            send(pairs[at])
            at += 1
        pairs[at][...] = b
        send(pairs[at])

    grad = encode_back(grad, x_ref[...], w_qkv, w_out, w_up, w_down, HEADS, res, packed_grad, put).astype(BF16)
    for b in range(8):
        spread[b * 128 : (b + 1) * 128, :] = mm_tn(choice(member, slot, b), grad).astype(BF16)
    send(spread)
    for e in early:
        e.finish()


def two_halves(flat, rows, core, halves, stage, sems, extra=None):
    run = 32 * rows
    copies = []
    for side in range(2):
        which = core if side == 0 else 1 - core
        for z in range(4):
            start = pl.multiple_of((2 * z + which) * run, 32)
            stage[side, z * run : (z + 1) * run, :] = flat[pl.ds(start, run), :].astype(BF16)
            part = pl.ds(z * run, run)
            copies.append(pltpu.make_async_copy(stage.at[side, part, :], halves[side].at[part, :], sems.at[side, z]))
            copies[-1].start()
        if extra is not None:
            stage[side, 4 * run : 4 * run + 80, :] = extra.ref()[which]
            part = pl.ds(4 * run, 80)
            copies.append(pltpu.make_async_copy(stage.at[side, part, :], halves[side].at[part, :], sems.at[side, 4]))
            copies[-1].start()
    for copy in copies:
        copy.wait()


def region_weights(core, *refs):
    ins, halves, bufs, flat, stage, sems, osems = cut(refs, 8, 2, 8, 1, 1, 1, 1)
    late = [Late(r, b, sems[0].at[i]) for i, (r, b) in enumerate(zip(ins, bufs))]
    hidden, grad, second, up_grad, mixture, mid_grad, first, packed_grad = late
    put_rows(flat[0], 9216, hidden[...], grad[...])
    put_rows(flat[0], 4608, second[...], up_grad[...])
    put_rows(flat[0], 3456, mixture[...], mid_grad[...])
    put_rows(flat[0], 0, first[...], packed_grad[...])
    two_halves(flat[0], 54, core[0], halves, stage[0], osems[0])


def tile_backward(core, ids, *refs):
    ins, halves, bufs, packed_grad, flat, stage, sems, osems = cut(refs, 14, 2, 14, 1, 1, 1, 1, 1)
    late = [Late(ins[i], bufs[i], sems[0].at[i]) for i in (0, 13, 6, 12, 11, 5, 10, 4, 9, 8, 3, 7, 1, 2)]
    late = dict(zip((0, 13, 6, 12, 11, 5, 10, 4, 9, 8, 3, 7, 1, 2), late))
    arrived, patches, slide_rows = late[0], late[1], late[2]
    w_qkv, w_out, w_up, w_down = [late[i] for i in range(3, 7)]
    x_ref, res = late[7], [late[i] for i in range(8, 14)]
    rows32 = lax.broadcasted_iota(jnp.int32, (32, 32), 0)
    columns32 = lax.broadcasted_iota(jnp.int32, (32, 32), 1)
    assign = jnp.sum(jnp.where(rows32 == columns32, ids[...].astype(F32), 0.0), axis=1, keepdims=True)
    cot = jnp.zeros((32, D), F32)
    for r in range(32):
        cot = cot + jnp.where(assign == float(r), arrived[r].astype(F32), 0.0)
    cot = cot * 0.25
    grad = jnp.concatenate([cot] * PATCHES, axis=0)
    normed, rstd = norm_parts(res[5][...])
    grad = norm_back(grad, normed, rstd)
    bases = (2304, 5760, 6912, 11520)

    def put(i, a, b):
        put_rows(flat[0], bases[i], a, b)

    grad = encode_back(grad, x_ref[...], w_qkv, w_out, w_up, w_down, HEADS, res, packed_grad[0], put)
    put_rows(flat[0], 0, patches[...], grad.astype(BF16))
    two_halves(flat[0], 63, core[0], halves, stage[0], osems[0], slide_rows)


def fold(rows, pad, tail, *refs):
    mine, got = refs[:2]
    refs = refs[2:]
    if tail:
        out, extra = refs[:2]
        refs = refs[2:]
    else:
        out = refs[0]
        refs = refs[1:]
    a, b, total, stage, chunks, sems, osems = refs[:7]
    run = 32 * rows
    arriving = []
    for z in range(4 + tail):
        part = pl.ds(z * run, run if z < 4 else 80)
        for side, (source, buffer) in enumerate(((mine, a), (got, b))):
            arriving.append(pltpu.make_async_copy(source.at[part, :], buffer.at[part, :], sems.at[side, z]))
            arriving[-1].start()
    for z in range(4):
        arriving[2 * z].wait()
        arriving[2 * z + 1].wait()
        part = pl.ds(z * run, run)
        total[part, :] = a[part, :].astype(F32) + b[part, :].astype(F32)
    leaving = []
    if tail:
        arriving[8].wait()
        arriving[9].wait()
        part = pl.ds(4 * run, 80)
        refs[7][...] = (a[part, :].astype(F32) + b[part, :].astype(F32)).astype(BF16)
        leaving.append(pltpu.make_async_copy(refs[7], extra, osems.at[16]))
        leaving[-1].start()
    if pad:
        stage[8 * rows :, :] = jnp.zeros((pad, LANES), F32)
    for y in range(4):
        for x in range(4):
            for z in range(4):
                for h in range(2):
                    source = (z * 32 + y * 8 + h * 4 + x) * rows
                    target = (z * 2 + h) * rows
                    stage[target : target + rows, :] = total[source : source + rows, :]
            chunks[y * 4 + x] = stage[...].astype(BF16)
            leaving.append(pltpu.make_async_copy(chunks.at[y * 4 + x], out.at[y * 4 + x], osems.at[y * 4 + x]))
            leaving[-1].start()
    for copy in leaving:
        copy.wait()


def merge(tile_in, region_in, slide_in, out, tile_buf, region_buf, slide_buf, total, region_total, slide_total, stage, chunks, sems, osems):
    tile_late = Late(tile_in, tile_buf, sems.at[0])
    region_late = Late(region_in, region_buf, sems.at[1])
    slide_late = Late(slide_in, slide_buf, sems.at[2])
    slide_total[...] = slide_late[...].astype(F32)

    def added(late, target, rows):
        for start in range(0, rows, 48 if rows % 48 == 0 else 64):
            size = 48 if rows % 48 == 0 else 64
            value = late[0, start : start + size, :].astype(F32)
            for i in range(1, 16):
                value = value + late[i, start : start + size, :].astype(F32)
            target[start : start + size, :] = value

    added(region_late, region_total, 432)
    added(tile_late, total, 512)
    leaving = []
    for i in range(8):
        stage[0:63, :] = total[i * 63 : (i + 1) * 63, :]
        stage[63:64, :] = jnp.zeros((1, LANES), F32)
        stage[64:118, :] = region_total[i * 54 : (i + 1) * 54, :]
        stage[118:128, :] = slide_total[i * 10 : (i + 1) * 10, :]
        chunks[i] = stage[...].astype(BF16)
        leaving.append(pltpu.make_async_copy(chunks.at[i], out.at[i], osems.at[i]))
        leaving[-1].start()
    for copy in leaving:
        copy.wait()


def call(kernel, outs, scratch, inputs, scalars=0, whole=0):
    specs = [pl.BlockSpec(memory_space=pltpu.SMEM)] * scalars
    specs += [pl.BlockSpec(memory_space=pltpu.VMEM)] * whole
    specs += [pl.BlockSpec(memory_space=pl.ANY)] * (len(inputs) - scalars - whole)
    return pl.pallas_call(
        kernel,
        out_shape=[jax.ShapeDtypeStruct(shape, kind) for shape, kind in outs],
        in_specs=specs,
        out_specs=[pl.BlockSpec(memory_space=pl.ANY)] * len(outs),
        scratch_shapes=[pltpu.VMEM(*item) if isinstance(item, tuple) else item for item in scratch],
        compiler_params=pltpu.CompilerParams(vmem_limit_bytes=60 * 1024 * 1024),
    )(*inputs)


def like(arrays):
    return [(a.shape, a.dtype) for a in arrays]


def semaphores(*shape):
    return pltpu.SemaphoreType.DMA(shape)


def residuals(tokens, width, hidden, heads):
    return [
        ((tokens, 3 * width), BF16),
        ((heads, tokens, tokens), F32),
        ((tokens, width), BF16),
        ((tokens, width), F32),
        ((tokens, hidden), F32),
        ((tokens, width), F32),
    ]


def index_of(z, core, y, z_hi, x):
    return (z * 2 + core) * 32 + y * 8 + z_hi * 4 + x


PLANES = [[index_of(z, c, y, h, x) for y in range(4) for x in range(4)] for z in range(4) for c in range(2) for h in range(2)]
COLUMNS = [[index_of(z, c, y, h, x) for z in range(4) for h in range(2)] for c in range(2) for y in range(4) for x in range(4)]
OTHER_CORE = [(g, g + 1 - 2 * (g % 2)) for g in range(8)]
ALL = ("grp", "dev")


def exchange(array, groups):
    return lax.all_to_all(array, ALL, 0, 0, axis_index_groups=groups)


def folded(mine, other, rows, pad, tail):
    got = lax.ppermute(other, "grp", OTHER_CORE)
    height = 128 * rows + 80 * tail
    chunk = 8 * rows + pad
    return call(
        functools.partial(fold, rows, pad, tail),
        [((16, chunk, LANES), BF16)] + [((80, LANES), BF16)] * tail,
        [((height, LANES), BF16)] * 2
        + [((128 * rows, LANES), F32), ((chunk, LANES), F32), ((16, chunk, LANES), BF16)]
        + [semaphores(2, 5), semaphores(17)]
        + [((80, LANES), BF16)] * tail,
        (mine, got),
    )


def body(
    patches,
    tile_region,
    region_slide,
    bin_label,
    censored,
    patch_w,
    tile_qkv,
    tile_out,
    tile_up,
    tile_down,
    region_qkv,
    region_out,
    region_up,
    region_down,
    slide_in,
    slide_qkv,
    slide_out,
    slide_up,
    slide_down,
    slide_head,
):
    member_index = lax.axis_index("dev").astype(jnp.int32)
    where = member_index.reshape(1)
    core = lax.rem(lax.axis_index("grp").astype(jnp.int32), 2).reshape(1)
    scaling = 1.0 / (bin_label.shape[1] * lax.axis_size("grp"))
    tokens = patches.transpose(1, 0, 2).reshape(128, 768)
    ids = jnp.tile(tile_region, (1, 4))
    tile_res = [((128, D), F32)] + residuals(128, D, FF, HEADS)
    ins = (tokens, patch_w, tile_qkv, tile_out, tile_up, tile_down)
    message, *tile_kept = call(
        tile_forward,
        [((32, 112, LANES), BF16)] + tile_res,
        like(ins) + tile_res + [((112, LANES), BF16), semaphores(6), semaphores(7), semaphores(32)],
        (where, ids, region_slide) + ins,
        scalars=1,
        whole=2,
    )
    rows = lax.all_to_all(message, "dev", 0, 0)
    region_res = [((SLOTS, D), F32)] + residuals(SLOTS, D, FF, HEADS)
    ins = (rows, region_qkv, region_out, region_up, region_down)
    message, *region_kept = call(
        region_forward,
        [((32, 8, LANES), F32)] + region_res,
        like(ins) + region_res + [((8, LANES), F32), semaphores(5), semaphores(7), semaphores(32)],
        (where,) + ins,
        scalars=1,
    )
    all_regions = lax.all_to_all(message, "dev", 0, 0)
    slide_weights = (slide_in, slide_qkv, slide_out, slide_up, slide_down, slide_head)
    pairs = [
        ((SLOTS, FF), BF16),
        ((SLOTS, D), BF16),
        ((SLOTS, D), BF16),
        ((SLOTS, FF), BF16),
        ((SLOTS, D), BF16),
        ((SLOTS, D), BF16),
        ((SLOTS, 3 * D), BF16),
    ]
    outs = [((SL_GRP, 1), F32), ((1024, D), BF16)] + pairs + like(slide_weights)
    ins = (all_regions, rows[:, 96:112, :]) + slide_weights + (region_qkv, region_out, region_up, region_down) + tuple(region_kept)
    losses, spread, *rest = call(
        functools.partial(region_backward, scaling),
        outs,
        like(ins)
        + outs
        + [((SLOTS, 3 * D), BF16), ((32, 3 * D_SL), BF16), ((32, D), BF16)]
        + residuals(32, D_SL, D_SL, H_SL)
        + [semaphores(19), semaphores(15)],
        (where, bin_label.reshape(SL_GRP, 1), censored.reshape(SL_GRP, 1)) + ins,
        scalars=1,
        whole=2,
    )
    arrived = lax.all_to_all(spread.reshape(32, 32, D), "dev", 0, 0)
    hidden, down_grad, second, up_grad, mid_grad, first, packed_grad = rest[:7]
    ins = (hidden, down_grad, second, up_grad, region_kept[3], mid_grad, first, packed_grad)
    mine, other = call(
        region_weights,
        [((6912, LANES), BF16)] * 2,
        like(ins) + [((13824, LANES), F32), ((2, 6912, LANES), BF16), semaphores(8), semaphores(2, 5)],
        (core,) + ins,
        scalars=1,
    )
    (region_chunks,) = folded(mine, other, 54, 0, 0)
    region_parts = exchange(region_chunks, PLANES)
    slide_flat = jnp.concatenate([g.astype(F32).reshape(-1) for g in rest[7:]]).reshape(4, 2, 4, 2, 4, 1155)
    y, x = member_index // 8, lax.rem(member_index, 4)
    zero = jnp.zeros((), jnp.int32)
    slide_rows = lax.dynamic_slice(slide_flat, (zero, zero, y, zero, x, zero), (4, 2, 1, 2, 1, 1155))
    slide_rows = slide_rows.reshape(4, 2, 2, 1155).transpose(1, 0, 2, 3)
    slide_rows = jnp.pad(slide_rows, ((0, 0), (0, 0), (0, 0), (0, 125))).astype(BF16).reshape(2, 80, LANES)
    ins = (arrived, tokens, slide_rows, tile_qkv, tile_out, tile_up, tile_down) + tuple(tile_kept)
    mine, other = call(
        tile_backward,
        [((8144, LANES), BF16)] * 2,
        like(ins)
        + [((128, 3 * D), BF16), ((16128, LANES), F32), ((2, 8144, LANES), BF16), semaphores(14), semaphores(2, 5)],
        (core, tile_region) + ins,
        scalars=1,
        whole=1,
    )
    tile_chunks, slide_sums = folded(mine, other, 63, 8, 1)
    tile_parts = exchange(tile_chunks, PLANES)
    ins = (tile_parts, region_parts, slide_sums)
    (last,) = call(
        merge,
        [((8, 128, LANES), BF16)],
        like(ins)
        + [((512, LANES), F32), ((432, LANES), F32), ((80, LANES), F32), ((128, LANES), F32), ((8, 128, LANES), BF16)]
        + [semaphores(3), semaphores(8)],
        ins,
    )
    total = jnp.sum(exchange(last, COLUMNS).astype(F32), axis=0)
    tile_result = total[0:63].reshape(8064)
    region_result = total[64:118].reshape(6912)
    slide_result = total[118:128].reshape(1280)[:1155] * 0.5
    return (losses.reshape(1, SL_GRP), tile_result, region_result, slide_result)


def solution(mesh):
    placed = (P(ALL, None, None), P("grp", "dev"), P("grp", "dev"), P("grp", None), P("grp", None)) + (P(),) * 15
    return jax.shard_map(
        body,
        mesh=mesh,
        in_specs=placed,
        out_specs=(P("grp", None), P(ALL), P(ALL), P(ALL)),
        check_vma=False,
    )
```

time: 791 us -> 219 us (0.28); the launches traced: 782 us -> 219 us
  blocking collectives: 389 us -> 74.5 us
  waiting for transfers between devices: 195 us -> 49.7 us
  Pallas kernels: 0 us -> 55 us
  matrix products: 54.2 us -> 0 us
  other arithmetic: 53 us -> 1.27 us
  local copies, waits for them, and re-layouts: 70.3 us -> 19.4 us
  between operations: 19.6 us -> 1.6 us
  starting transfers between devices: 0.08 us -> 17.2 us
    all_gather x2 -> x0, blocking collectives: 220 us -> none  [the longest x1 112 us: body(): group_rows = lax.all_gather(embeds, 'dev', axis=0, tiled=True)]
    reduce_scatter x1 -> x0, waiting for transfers between devices: 195 us -> none  [body(): lax.psum_scatter(spread, 'dev', scatter_dimension=0, tiled=True)]
    unnamed x2 -> x0, blocking collectives: 169 us -> none
    all_to_all x0 -> x2, blocking collectives: none -> 74.5 us  [the longest x1 41.8 us: body(): rows = lax.all_to_all(message, 'dev', 0, 0)]
    pallas_call x0 -> x8, Pallas kernels: none -> 55 us  [call(): pl.pallas_call(kernel, out_shape=[jax.ShapeDtypeStruct(shape, kind) for s...]
    dot_general x61 -> x0, matrix products: 50.1 us -> none  [the longest x9 9.95 us: encoder(): jnp.einsum('bsd,de->bse', hidden, w_down, preferred_element_type=jnp.floa...]
    all_to_all x0 -> x4, waiting for transfers between devices: none -> 49.7 us  [the longest x2 33.8 us: exchange(): return lax.all_to_all(array, ALL, 0, 0, axis_index_groups=groups)]
    unnamed x356 -> x33, local copies, waits for them, and re-layouts: 34.4 us -> 5.33 us
  transfers between devices with their start and end apart: 2 -> 6, of which waited for: 1 -> 4; matrix products, arithmetic and copies ran while one was open for 10% -> 6% of each run, Pallas kernels for 0% -> 12%
where the time goes in v1:
time: 219 us
  blocking collectives  74.5 us (34%)
  Pallas kernels  55 us (25%)
  waiting for transfers between devices  49.7 us (23%)
  local copies, waits for them, and re-layouts  19.4 us (9%)
  starting transfers between devices  17.2 us (8%)
    pallas_call x8, Pallas kernels, call(): pl.pallas_call(kernel, out_shape=[jax.ShapeDtypeStruct(shape, kind) for s...  55 us
    all_to_all x1, blocking collectives, body(): rows = lax.all_to_all(message, 'dev', 0, 0)  41.8 us
    all_to_all x2, waiting for transfers between devices, exchange(): return lax.all_to_all(array, ALL, 0, 0, axis_index_groups=groups)  33.8 us
    all_to_all x1, blocking collectives, exchange(): return lax.all_to_all(array, ALL, 0, 0, axis_index_groups=groups)  32.7 us
    all_to_all x1, waiting for transfers between devices, body(): all_regions = lax.all_to_all(message, 'dev', 0, 0)  8.08 us
    all_to_all x1, waiting for transfers between devices, body(): arrived = lax.all_to_all(spread.reshape(32, 32, D), 'dev', 0, 0)  7.82 us
    all_to_all x2, starting transfers between devices, exchange(): return lax.all_to_all(array, ALL, 0, 0, axis_index_groups=groups)  7.69 us
    unnamed x33, local copies, waits for them, and re-layouts  5.33 us
  transfers between devices with their start and end apart: 6, of which 4 were waited for; matrix products, arithmetic and copies ran while one was open for 6% of the time, Pallas kernels for 12%

profile of v1, /device:TPU:32, one launch (start us, length us, event | category | flops | bytes accessed | tf_op | source)
XLA Modules:
  0.0 218.6 jit_solution(15821558453057795704)
XLA Ops:
  1.3 0.7 tile.12
  1.9 0.6 tile.13.ids
  2.5 1.6 copy.35
  4.2 7.5 %shard_map.219 = (bf16[32,112,128]{2,1,0:T(8,128)(2,1)}, f32[128,384]{1,0:T(8,128)}, bf16[128,1152]{1,0:T(8,128)(2,1)}, f32[6,128,128]{2,1,0:T(8,128)}, bf16[128...) custom-call(s32[1]{0:T(128)} %bitcast.where, s32[1,128]{1,0:T(1,128)} %tile.13.ids, ...), custom_call_target="tpu_custom_call" | custom-call | tf_op jit(solution)/shard_map/pallas_call | solution.py:511
  11.7 41.8 %all_to_all.30.refs_0_ = bf16[32,112,128]{2,1,0:T(8,128)(2,1)} all-to-all(bf16[32,112,128]{2,1,0:T(8,128)(2,1)} %get-tuple-element.41), channel_id=1, replica_groups=mesh['grp'=8,'dev'=32] {'dev'}, dimensions={0} | all-to-all | bytes 1835008 | tf_op jit(solution)/shard_map/all_to_all | solution.py:607
  53.5 0.0 copy-start.12
  53.5 0.0 copy-start.9
  53.5 6.4 %shard_map.220 = (f32[32,8,128]{2,1,0:T(8,128)}, f32[64,384]{1,0:T(8,128)}, bf16[64,1152]{1,0:T(8,128)(2,1)}, f32[6,64,64]{2,1,0:T(8,128)}, bf16[64,384]{1,0:T(8...) custom-call(s32[1]{0:T(128)} %bitcast.where, bf16[32,112,128]{2,1,0:T(8,128)(2,1)} %all_to_all.30.refs_0_, ...), custom_call_target="tpu_custom_call" | custom-call | tf_op jit(solution)/shard_map/pallas_call | solution.py:511
  59.9 4.8 %all-to-all-start.1 = ((f32[32,8,128]{2,1,0:T(8,128)}), f32[32,8,128]{2,1,0:T(8,128)S(1)}, u32[]{:S(2)}, u32[]{:S(2)}) async-start(f32[32,8,128]{2,1,0:T(8,128)} %get-tuple-element.42), calls=%async_computation.1 | async-start | bytes 262144 | tf_op jit(solution)/shard_map/all_to_all | solution.py:617
  64.7 0.0 copy-done.11
  64.7 0.7 copy.36.label
  65.3 0.0 copy-done.12
  65.4 0.7 copy.37.censor
  66.0 0.0 copy-done.9
  66.0 0.8 copy.39.refs_7_
  66.8 0.0 copy-done.6
  66.8 0.8 copy.38.refs_2_
  67.6 1.6 slice.20.refs_1_
  69.2 8.1 %all-to-all-done.1.refs_0_ = f32[32,8,128]{2,1,0:T(8,128)S(1)} async-done(((f32[32,8,128]{2,1,0:T(8,128)}), f32[32,8,128]{2,1,0:T(8,128)S(1)}, u32[]{:S(2)}, u32[]{:S(2)}) %all-to-all-start.1) | async-done | bytes 131104 | tf_op jit(solution)/shard_map/all_to_all | solution.py:617
  77.3 0.7 copy-done.3
  77.9 12.5 %shard_map.221 = (f32[4,1]{1,0:T(4,128)}, bf16[1024,384]{1,0:T(8,128)(2,1)}, bf16[64,1536]{1,0:T(8,128)(2,1)}, bf16[64,384]{1,0:T(8,128)(2,1)}, bf16[64,384]{1,0...) custom-call(s32[1]{0:T(128)} %bitcast.where, ...), custom_call_target="tpu_custom_call" | custom-call | tf_op jit(solution)/shard_map/pallas_call | solution.py:511
  90.5 0.0 copy-start.8
  90.5 0.0 copy-start.7
  90.5 0.0 copy-start.5
  90.5 0.0 copy-start.4
  90.5 1.0 reshape.93
  91.5 4.3 %all-to-all-start.2 = ((bf16[32,32,384]{2,1,0:T(8,128)(2,1)}), bf16[32,32,384]{2,1,0:T(8,128)(2,1)S(1)}, u32[]{:S(2)}, u32[]{:S(2)}) async-start(bf16[32,32,384]{2,1,0:T(8,128)(2,1)} %bitcast.23), calls=%async_computation.2 | async-start | bytes 1572864 | tf_op jit(solution)/shard_map/all_to_all | solution.py:642
  95.8 1.7 reshape.90
  97.5 0.0 copy-done.8
  97.5 0.2 reshape.91
  97.6 0.0 copy-done.7
  97.6 0.2 reshape.92
  97.8 0.0 copy-done.5
  97.8 0.3 reshape.88
  98.1 0.0 copy-done.4
  98.1 0.3 reshape.89
  98.4 4.9 %shard_map.224 = (bf16[6912,128]{1,0:T(8,128)(2,1)}, bf16[6912,128]{1,0:T(8,128)(2,1)}) custom-call(s32[1]{0:T(128)} %bitcast.6.core, bf16[64,1536]{1,0:T(8,128)(2,1)} %get-tuple-element.68.refs_0_, bf16[64,384]{1,0:T(8,128)(2,1)} %get-tuple-element.69.refs_1_, bf16[64,384]{1,0:T(8,128)(2,1)} %get-tuple-element.70.refs_2_, ...), custom_call_target="tpu_custom_call" | custom-call | tf_op jit(solution)/shard_map/pallas_call | solution.py:511
  103.3 0.1 collective-permute-start.1
  103.4 0.9 constant_dynamic-update-slice_fusion.3
  104.3 1.8 reshape.102
  106.2 1.0 dynamic-slice_convert_fusion
  107.3 0.6 reshape.97.refs_2_
  107.9 7.8 %all-to-all-done.2.refs_0_ = bf16[32,32,384]{2,1,0:T(8,128)(2,1)S(1)} async-done(((bf16[32,32,384]{2,1,0:T(8,128)(2,1)}), bf16[32,32,384]{2,1,0:T(8,128)(2,1)S(1)}, u32[]{:S(2)}, u32[]{:S(2)}) %all-to-all-start.2) | async-done | bytes 786464 | tf_op jit(solution)/shard_map/all_to_all | solution.py:642
  115.7 0.9 copy-done.1
  116.6 12.8 %shard_map.222 = (bf16[8144,128]{1,0:T(8,128)(2,1)}, bf16[8144,128]{1,0:T(8,128)(2,1)}) custom-call(s32[1]{0:T(128)} %bitcast.6.core, s32[1,32]{1,0:T(1,128)} %ids.1, bf16[32,32,384]{2,1,0:T(8,128)(2,1)} %copy-done.1, bf16[128,768]{1,0:T(8,128)(2,1)} %bitcast.22, bf16[2,80,128]{2,1,0:T(8,128)(2,1)} %reshape.97.refs_2_, bf16[384,1152]{1,0:T(8,128)(2,1)} %refs_3_.7, ...), custom_call_target="tpu_custom_call" | custom-call | tf_op jit(solution)/shard_map/pallas_call | solution.py:511
  129.4 0.3 collective-permute-start
  129.8 0.0 collective-permute-done.1.refs_1_
  129.8 0.0 copy-start.2
  129.8 1.2 copy-done.2
  131.0 3.7 %shard_map.225 = bf16[16,432,128]{2,1,0:T(8,128)(2,1)} custom-call(bf16[6912,128]{1,0:T(8,128)(2,1)} %get-tuple-element.75.refs_0_, bf16[6912,128]{1,0:T(8,128)(2,1)} %copy-done.2), custom_call_target="tpu_custom_call" | custom-call | tf_op jit(solution)/shard_map/pallas_call | solution.py:511
  134.7 4.3 %all-to-all-start.4 = ((bf16[16,432,128]{2,1,0:T(8,128)(2,1)}), bf16[16,432,128]{2,1,0:T(8,128)(2,1)S(1)}, u32[]{:S(2)}, u32[]{:S(2)}) async-start(bf16[16,432,128]{2,1,0:T(8,128)(2,1)} %shard_map.225), calls=%async_computation.4 | async-start | bytes 3538944 | tf_op jit(solution)/shard_map/all_to_all | solution.py:551
  139.0 0.0 collective-permute-done.refs_1_
  139.0 3.8 %shard_map.223 = (bf16[16,512,128]{2,1,0:T(8,128)(2,1)}, bf16[80,128]{1,0:T(8,128)(2,1)}) custom-call(bf16[8144,128]{1,0:T(8,128)(2,1)} %get-tuple-element.65.refs_0_, bf16[8144,128]{1,0:T(8,128)(2,1)} %collective-permute-done.refs_1_), custom_call_target="tpu_custom_call" | custom-call | tf_op jit(solution)/shard_map/pallas_call | solution.py:511
  142.8 25.8 %all-to-all-done.4.region_in = bf16[16,432,128]{2,1,0:T(8,128)(2,1)S(1)} async-done(((bf16[16,432,128]{2,1,0:T(8,128)(2,1)}), bf16[16,432,128]{2,1,0:T(8,128)(2,1)S(1)}, u32[]{:S(2)}, u32[]{:S(2)}) %all-to-all-start.4) | async-done | bytes 1769504 | tf_op jit(solution)/shard_map/all_to_all | solution.py:551
  168.6 32.7 %all_to_all.31.tile_in = bf16[16,512,128]{2,1,0:T(8,128)(2,1)} all-to-all(bf16[16,512,128]{2,1,0:T(8,128)(2,1)} %get-tuple-element.67), channel_id=1, replica_groups={{0,1,2,3,8,9,10,11,16,17,18,19,24,25,26,27},{4,5,6,7,12,13,14,15,20,21,..., dimensions={0} | all-to-all | bytes 4194304 | tf_op jit(solution)/shard_map/all_to_all | solution.py:551
  201.2 0.0 copy-done
  201.2 3.4 %shard_map.226 = bf16[8,128,128]{2,1,0:T(8,128)(2,1)} custom-call(bf16[16,512,128]{2,1,0:T(8,128)(2,1)} %all_to_all.31.tile_in, bf16[16,432,128]{2,1,0:T(8,128)(2,1)} %copy-done, bf16[80,128]{1,0:T(8,128)(2,1)} %get-tuple-element.77.slide_in), custom_call_target="tpu_custom_call" | custom-call | tf_op jit(solution)/shard_map/pallas_call | solution.py:511
  204.7 3.4 %all-to-all-start.5 = ((bf16[8,128,128]{2,1,0:T(8,128)(2,1)}), bf16[8,128,128]{2,1,0:T(8,128)(2,1)S(1)}, u32[]{:S(2)}, u32[]{:S(2)}) async-start(bf16[8,128,128]{2,1,0:T(8,128)(2,1)} %shard_map.226), calls=%async_computation.5 | async-start | bytes 524288 | tf_op jit(solution)/shard_map/all_to_all | solution.py:551
  208.1 0.0 copy-done.10
  208.1 0.6 reduce
  208.7 8.0 %all-to-all-done.5 = bf16[8,128,128]{2,1,0:T(8,128)(2,1)S(1)} async-done(((bf16[8,128,128]{2,1,0:T(8,128)(2,1)}), bf16[8,128,128]{2,1,0:T(8,128)(2,1)S(1)}, u32[]{:S(2)}, u32[]{:S(2)}) %all-to-all-start.5) | async-done | bytes 262176 | tf_op jit(solution)/shard_map/all_to_all | solution.py:551
  216.8 0.6 slice_bitcast_fusion.1
  217.4 0.6 slice_bitcast_fusion
  218.0 0.6 slice_multiply_fusion
  (15 shorter events, 0.2 us)
Async XLA Ops:
  53.5 11.2 %copy-start.11 = (s32[1,4]{1,0:T(1,128)S(1)}, s32[1,4]{1,0:T(1,128)}, u32[]{:S(2)}) copy-start(s32[1,4]{1,0:T(1,128)} %param.23) | copy-start | bytes 52
  53.5 11.9 %copy-start.12 = (s32[1,4]{1,0:T(1,128)S(1)}, s32[1,4]{1,0:T(1,128)}, u32[]{:S(2)}) copy-start(s32[1,4]{1,0:T(1,128)} %param.24) | copy-start | bytes 52
  53.5 12.5 %copy-start.9 = (bf16[192,4]{0,1:T(4,128)(2,1)S(1)}, bf16[192,4]{0,1:T(4,128)(2,1)}, u32[]{:S(2)}) copy-start(bf16[192,4]{0,1:T(4,128)(2,1)} %param.39) | copy-start | bytes 4612
  53.5 13.3 %copy-start.6 = (bf16[384,192]{0,1:T(8,128)(2,1)S(1)}, bf16[384,192]{0,1:T(8,128)(2,1)}, u32[]{:S(2)}) copy-start(bf16[384,192]{0,1:T(8,128)(2,1)} %param.34) | copy-start | bytes 442372
  59.9 17.4 %all-to-all-start.1 = ((f32[32,8,128]{2,1,0:T(8,128)}), f32[32,8,128]{2,1,0:T(8,128)S(1)}, u32[]{:S(2)}, u32[]{:S(2)}) async-start(f32[32,8,128]{2,1,0:T(8,128)} %get-tuple-element.42), calls=%async_computation.1 | async-start | bytes 262144 | tf_op jit(solution)/shard_map/all_to_all | solution.py:617
  77.3 0.7 copy-start.3
  90.5 7.0 %copy-start.8 = (bf16[192,192]{1,0:T(8,128)(2,1)S(1)}, bf16[192,192]{1,0:T(8,128)(2,1)}, u32[]{:S(2)}) copy-start(bf16[192,192]{1,0:T(8,128)(2,1)} %get-tuple-element.55) | copy-start | bytes 221188
  90.5 7.2 %copy-start.7 = (bf16[192,192]{1,0:T(8,128)(2,1)S(1)}, bf16[192,192]{1,0:T(8,128)(2,1)}, u32[]{:S(2)}) copy-start(bf16[192,192]{1,0:T(8,128)(2,1)} %get-tuple-element.56) | copy-start | bytes 221188
  90.5 7.3 %copy-start.5 = (bf16[384,192]{1,0:T(8,128)(2,1)S(1)}, bf16[384,192]{1,0:T(8,128)(2,1)}, u32[]{:S(2)}) copy-start(bf16[384,192]{1,0:T(8,128)(2,1)} %get-tuple-element.52) | copy-start | bytes 442372
  90.5 7.6 %copy-start.4 = (bf16[192,576]{1,0:T(8,128)(2,1)S(1)}, bf16[192,576]{1,0:T(8,128)(2,1)}, u32[]{:S(2)}) copy-start(bf16[192,576]{1,0:T(8,128)(2,1)} %get-tuple-element.53) | copy-start | bytes 663556
  91.5 24.2 %all-to-all-start.2 = ((bf16[32,32,384]{2,1,0:T(8,128)(2,1)}), bf16[32,32,384]{2,1,0:T(8,128)(2,1)S(1)}, u32[]{:S(2)}, u32[]{:S(2)}) async-start(bf16[32,32,384]{2,1,0:T(8,128)(2,1)} %bitcast.23), calls=%async_computation.2 | async-start | bytes 1572864 | tf_op jit(solution)/shard_map/all_to_all | solution.py:642
  103.3 26.5 %collective-permute-start.1 = (bf16[6912,128]{1,0:T(8,128)(2,1)}, bf16[6912,128]{1,0:T(8,128)(2,1)S(1)}, u32[]{:S(2)}, u32[]{:S(2)}) collective-permute-start(bf16[6912,128]{1,0:T(8,128)(2,1)} %get-tuple-element.76), channel_id=1, source_target_pairs={{0,32},{32,0},{64,96},{96,64},{128,160},{160,128},{192,224},{224,1... | collective-permute-start | bytes 5308424 | tf_op jit(solution)/shard_map/ppermute | solution.py:555
  115.7 0.9 copy-start.1
  129.4 9.6 %collective-permute-start = (bf16[8144,128]{1,0:T(8,128)(2,1)}, bf16[8144,128]{1,0:T(8,128)(2,1)}, u32[]{:S(2)}, u32[]{:S(2)}) collective-permute-start(bf16[8144,128]{1,0:T(8,128)(2,1)} %get-tuple-element.66), channel_id=1, source_target_pairs={{0,32},{32,0},{64,96},{96,64},{128,160},{160,128},{192,224},{224,1... | collective-permute-start | bytes 6254600 | tf_op jit(solution)/shard_map/ppermute | solution.py:555
  129.8 1.2 copy-start.2
  134.7 33.9 %all-to-all-start.4 = ((bf16[16,432,128]{2,1,0:T(8,128)(2,1)}), bf16[16,432,128]{2,1,0:T(8,128)(2,1)S(1)}, u32[]{:S(2)}, u32[]{:S(2)}) async-start(bf16[16,432,128]{2,1,0:T(8,128)(2,1)} %shard_map.225), calls=%async_computation.4 | async-start | bytes 3538944 | tf_op jit(solution)/shard_map/all_to_all | solution.py:551
  168.6 32.7 %copy-start = (bf16[16,432,128]{2,1,0:T(8,128)(2,1)}, bf16[16,432,128]{2,1,0:T(8,128)(2,1)S(1)}, u32[]{:S(2)}) copy-start(bf16[16,432,128]{2,1,0:T(8,128)(2,1)S(1)} %all-to-all-done.4.region_in) | copy-start | bytes 5308420
  201.2 6.8 %copy-start.10 = (f32[4,1]{1,0:T(4,128)S(1)}, f32[4,1]{1,0:T(4,128)}, u32[]{:S(2)}) copy-start(f32[4,1]{1,0:T(4,128)} %get-tuple-element.50) | copy-start | bytes 52
  204.7 12.1 %all-to-all-start.5 = ((bf16[8,128,128]{2,1,0:T(8,128)(2,1)}), bf16[8,128,128]{2,1,0:T(8,128)(2,1)S(1)}, u32[]{:S(2)}, u32[]{:S(2)}) async-start(bf16[8,128,128]{2,1,0:T(8,128)(2,1)} %shard_map.226), calls=%async_computation.5 | async-start | bytes 524288 | tf_op jit(solution)/shard_map/all_to_all | solution.py:551

commit v2 on v1

--- a/solution.py
+++ b/solution.py
@@ -21,6 +21,7 @@
 F32 = jnp.float32
 BF16 = jnp.bfloat16
 LANES = 128
+US = 550_000_000
 GELU_C = math.sqrt(2.0 / math.pi)
 
 
@@ -173,6 +174,14 @@
         ref.copy.start()
 
 
+def leave(pairs, sems):
+    copies = [pltpu.make_async_copy(a, b, sems.at[i]) for i, (a, b) in enumerate(pairs)]
+    for copy in copies:
+        copy.start()
+    for copy in copies:
+        copy.wait()
+
+
 def broadcast_out(block, out, sems):
     copies = [pltpu.make_async_copy(block, out.at[i], sems.at[i]) for i in range(32)]
     for copy in copies:
@@ -199,9 +208,10 @@
     row = lax.broadcasted_iota(jnp.int32, (16, LANES), 0)
     lane = lax.broadcasted_iota(jnp.int32, (16, LANES), 1)
     mine = (lane >= 32 * lax.rem(where[0], 4)) & (lane < 32 * lax.rem(where[0], 4) + 32)
-    tail = jnp.where((row == 0) & mine, ids[...].astype(F32), 0.0) + jnp.where(row == 1, slide[...].astype(F32), 0.0)
+    four = jnp.concatenate([ids[...].astype(F32)] * 4, axis=1)
+    tail = jnp.where((row == 0) & mine, four, 0.0) + jnp.where(row == 1, slide[...].astype(F32), 0.0)
     message[96:112, :] = tail.astype(BF16)
-    broadcast_out(message, outs[0], bsems[0])
+    leave([(message, outs[0])], bsems[0])
     for r in res:
         r.finish()
 
@@ -247,10 +257,22 @@
 
 
 def region_forward(where, *refs):
-    ins, outs, bufs, obufs, block, sems, osems, bsems = cut(refs, 5, 8, 5, 7, 1, 1, 1, 1)
-    late = [Late(r, b, sems[0].at[i]) for i, (r, b) in enumerate(zip(ins, bufs))]
-    res = [Early(r, b, osems[0].at[i]) for i, (r, b) in enumerate(zip(outs[1:], obufs))]
-    rows, w_qkv, w_out, w_up, w_down = late
+    ins, outs, bufs, rows, obufs, block, sems, osems, bsems, rsems = cut(refs, 5, 9, 4, 1, 7, 1, 1, 1, 1, 1)
+    rows = rows[0]
+    h = lax.rem(where[0] // 4, 2)
+    arriving = []
+    for i in range(16):
+        base = i // 4 * 8 + i % 4
+        for side, z in enumerate((h, 1 - h)):
+            source = ins[0].at[i, 112 * side : 112 * side + 112, :]
+            arriving.append(pltpu.make_async_copy(source, rows.at[base + 4 * z], rsems[0].at[2 * i + side]))
+            arriving[-1].start()
+    w_qkv, w_out, w_up, w_down = [Late(r, b, sems[0].at[i]) for i, (r, b) in enumerate(zip(ins[1:], bufs))]
+    res = [Early(r, b, osems[0].at[i]) for i, (r, b) in enumerate(zip(outs[2:], obufs))]
+    for copy in arriving:
+        copy.wait()
+    tails = pltpu.make_async_copy(rows.at[:, 96:112, :], outs[1], bsems[0].at[32])
+    tails.start()
     ids, _ = tails_of(rows[:, 96:112, :])
     member, slot, count = slots_of(ids, where[0])
     parts = [jnp.zeros((SLOTS, LANES), F32)] * 3
@@ -273,6 +295,7 @@
     for c in range(3):
         message[c : c + 1, :] = embed[:, c * LANES : (c + 1) * LANES]
     broadcast_out(message, outs[0], bsems[0])
+    tails.wait()
     for r in res:
         r.finish()
 
@@ -403,7 +426,7 @@
 
 
 def tile_backward(core, ids, *refs):
-    ins, halves, bufs, packed_grad, flat, stage, sems, osems = cut(refs, 14, 2, 14, 1, 1, 1, 1, 1)
+    ins, _, halves, bufs, packed_grad, flat, stage, sems, osems = cut(refs, 14, 1, 2, 14, 1, 1, 1, 1, 1)
     late = [Late(ins[i], bufs[i], sems[0].at[i]) for i in (0, 13, 6, 12, 11, 5, 10, 4, 9, 8, 3, 7, 1, 2)]
     late = dict(zip((0, 13, 6, 12, 11, 5, 10, 4, 9, 8, 3, 7, 1, 2), late))
     arrived, patches, slide_rows = late[0], late[1], late[2]
@@ -504,10 +527,12 @@
         copy.wait()
 
 
-def call(kernel, outs, scratch, inputs, scalars=0, whole=0):
+def call(kernel, macs, outs, scratch, inputs, scalars=0, whole=0):
     specs = [pl.BlockSpec(memory_space=pltpu.SMEM)] * scalars
     specs += [pl.BlockSpec(memory_space=pltpu.VMEM)] * whole
     specs += [pl.BlockSpec(memory_space=pl.ANY)] * (len(inputs) - scalars - whole)
+    moved = sum(math.prod(a.shape) * a.dtype.itemsize for a in inputs) + sum(math.prod(a) * jnp.dtype(k).itemsize for a, k in outs)
+    cost = pl.CostEstimate(flops=2 * macs, bytes_accessed=moved, transcendentals=0)
     return pl.pallas_call(
         kernel,
         out_shape=[jax.ShapeDtypeStruct(shape, kind) for shape, kind in outs],
@@ -515,6 +540,7 @@
         out_specs=[pl.BlockSpec(memory_space=pl.ANY)] * len(outs),
         scratch_shapes=[pltpu.VMEM(*item) if isinstance(item, tuple) else item for item in scratch],
         compiler_params=pltpu.CompilerParams(vmem_limit_bytes=60 * 1024 * 1024),
+        cost_estimate=cost,
     )(*inputs)
 
 
@@ -544,6 +570,7 @@
 PLANES = [[index_of(z, c, y, h, x) for y in range(4) for x in range(4)] for z in range(4) for c in range(2) for h in range(2)]
 COLUMNS = [[index_of(z, c, y, h, x) for z in range(4) for h in range(2)] for c in range(2) for y in range(4) for x in range(4)]
 OTHER_CORE = [(g, g + 1 - 2 * (g % 2)) for g in range(8)]
+OTHER_PLANE = [(d, d + 4 - 8 * (d // 4 % 2)) for d in range(32)]
 ALL = ("grp", "dev")
 
 
@@ -557,6 +584,7 @@
     chunk = 8 * rows + pad
     return call(
         functools.partial(fold, rows, pad, tail),
+        4 * US,
         [((16, chunk, LANES), BF16)] + [((80, LANES), BF16)] * tail,
         [((height, LANES), BF16)] * 2
         + [((128 * rows, LANES), F32), ((chunk, LANES), F32), ((16, chunk, LANES), BF16)]
@@ -593,25 +621,30 @@
     core = lax.rem(lax.axis_index("grp").astype(jnp.int32), 2).reshape(1)
     scaling = 1.0 / (bin_label.shape[1] * lax.axis_size("grp"))
     tokens = patches.transpose(1, 0, 2).reshape(128, 768)
-    ids = jnp.tile(tile_region, (1, 4))
     tile_res = [((128, D), F32)] + residuals(128, D, FF, HEADS)
     ins = (tokens, patch_w, tile_qkv, tile_out, tile_up, tile_down)
     message, *tile_kept = call(
         tile_forward,
-        [((32, 112, LANES), BF16)] + tile_res,
-        like(ins) + tile_res + [((112, LANES), BF16), semaphores(6), semaphores(7), semaphores(32)],
-        (where, ids, region_slide) + ins,
+        7 * US,
+        [((112, LANES), BF16)] + tile_res,
+        like(ins) + tile_res + [((112, LANES), BF16), semaphores(6), semaphores(7), semaphores(1)],
+        (where, tile_region, region_slide) + ins,
         scalars=1,
         whole=2,
     )
-    rows = lax.all_to_all(message, "dev", 0, 0)
+    both = jnp.concatenate([message, lax.ppermute(message, "dev", OTHER_PLANE)], axis=0)
+    rows = exchange(jnp.broadcast_to(both[None], (16, 224, LANES)), PLANES)
     region_res = [((SLOTS, D), F32)] + residuals(SLOTS, D, FF, HEADS)
-    ins = (rows, region_qkv, region_out, region_up, region_down)
-    message, *region_kept = call(
+    ins = (region_qkv, region_out, region_up, region_down)
+    message, tails, *region_kept = call(
         region_forward,
-        [((32, 8, LANES), F32)] + region_res,
-        like(ins) + region_res + [((8, LANES), F32), semaphores(5), semaphores(7), semaphores(32)],
-        (where,) + ins,
+        6 * US,
+        [((32, 8, LANES), F32), ((32, 16, LANES), BF16)] + region_res,
+        like(ins)
+        + [((32, 112, LANES), BF16)]
+        + region_res
+        + [((8, LANES), F32), semaphores(4), semaphores(7), semaphores(33), semaphores(32)],
+        (where, rows) + ins,
         scalars=1,
     )
     all_regions = lax.all_to_all(message, "dev", 0, 0)
@@ -626,9 +659,10 @@
         ((SLOTS, 3 * D), BF16),
     ]
     outs = [((SL_GRP, 1), F32), ((1024, D), BF16)] + pairs + like(slide_weights)
-    ins = (all_regions, rows[:, 96:112, :]) + slide_weights + (region_qkv, region_out, region_up, region_down) + tuple(region_kept)
+    ins = (all_regions, tails) + slide_weights + (region_qkv, region_out, region_up, region_down) + tuple(region_kept)
     losses, spread, *rest = call(
         functools.partial(region_backward, scaling),
+        12 * US,
         outs,
         like(ins)
         + outs
@@ -644,6 +678,7 @@
     ins = (hidden, down_grad, second, up_grad, region_kept[3], mid_grad, first, packed_grad)
     mine, other = call(
         region_weights,
+        5 * US,
         [((6912, LANES), BF16)] * 2,
         like(ins) + [((13824, LANES), F32), ((2, 6912, LANES), BF16), semaphores(8), semaphores(2, 5)],
         (core,) + ins,
@@ -660,10 +695,11 @@
     ins = (arrived, tokens, slide_rows, tile_qkv, tile_out, tile_up, tile_down) + tuple(tile_kept)
     mine, other = call(
         tile_backward,
+        13 * US,
         [((8144, LANES), BF16)] * 2,
         like(ins)
         + [((128, 3 * D), BF16), ((16128, LANES), F32), ((2, 8144, LANES), BF16), semaphores(14), semaphores(2, 5)],
-        (core, tile_region) + ins,
+        (core, tile_region) + ins + (region_chunks,),
         scalars=1,
         whole=1,
     )
@@ -672,6 +708,7 @@
     ins = (tile_parts, region_parts, slide_sums)
     (last,) = call(
         merge,
+        3 * US,
         [((8, 128, LANES), BF16)],
         like(ins)
         + [((512, LANES), F32), ((432, LANES), F32), ((80, LANES), F32), ((128, LANES), F32), ((8, 128, LANES), BF16)]

time: 219 us -> 208 us (0.950)
  blocking collectives: 74.5 us -> 54.7 us
  starting transfers between devices: 17.2 us -> 27.3 us
  local copies, waits for them, and re-layouts: 19.4 us -> 11.3 us
  waiting for transfers between devices: 49.7 us -> 55 us
    all_to_all x1 -> x0, blocking collectives: 41.8 us -> none  [body(): rows = lax.all_to_all(message, 'dev', 0, 0)]
    all_to_all x1 -> x2, blocking collectives: 32.7 us -> 54.7 us  [exchange(): return lax.all_to_all(array, ALL, 0, 0, axis_index_groups=groups)]
    ppermute x0 -> x1, starting transfers between devices: none -> 6.38 us  [body(): lax.ppermute(message, 'dev', OTHER_PLANE)]
    all_to_all x1, starting transfers between devices: 4.78 us -> 8.24 us  [body(): all_regions = lax.all_to_all(message, 'dev', 0, 0)]
  transfers between devices with their start and end apart: 6 -> 7, of which waited for: 4 -> 7; matrix products, arithmetic and copies ran while one was open for 6% -> 4% of each run, Pallas kernels for 12% -> 6%
where the time goes in v2:
time: 208 us; the launch traced here: 207 us
  Pallas kernels  55.3 us (27%)
  waiting for transfers between devices  55 us (26%)
  blocking collectives  54.7 us (26%)
  starting transfers between devices  27.3 us (13%)
  local copies, waits for them, and re-layouts  11.3 us (5%)
    pallas_call x8, Pallas kernels, call(): pl.pallas_call(kernel, out_shape=[jax.ShapeDtypeStruct(shape, kind) for s...  55.3 us
    all_to_all x2, blocking collectives, exchange(): return lax.all_to_all(array, ALL, 0, 0, axis_index_groups=groups)  54.7 us
    all_to_all x2, waiting for transfers between devices, exchange(): return lax.all_to_all(array, ALL, 0, 0, axis_index_groups=groups)  33.7 us
    all_to_all x1, waiting for transfers between devices, body(): all_regions = lax.all_to_all(message, 'dev', 0, 0)  9.67 us
    all_to_all x1, starting transfers between devices, body(): all_regions = lax.all_to_all(message, 'dev', 0, 0)  8.24 us
    all_to_all x2, starting transfers between devices, exchange(): return lax.all_to_all(array, ALL, 0, 0, axis_index_groups=groups)  8.07 us
    all_to_all x1, waiting for transfers between devices, body(): arrived = lax.all_to_all(spread.reshape(32, 32, D), 'dev', 0, 0)  7.5 us
    ppermute x1, starting transfers between devices, body(): lax.ppermute(message, 'dev', OTHER_PLANE)  6.38 us
  transfers between devices with their start and end apart: 7, of which 7 were waited for; matrix products, arithmetic and copies ran while one was open for 4% of the time, Pallas kernels for 6%

profile of v2, /device:TPU:32, one launch (start us, length us, event | category | flops | bytes accessed | tf_op | source)
XLA Modules:
  0.0 207.2 jit_solution(1035999152676663107)
XLA Ops:
  1.3 1.6 copy.35
  2.9 6.9 %shard_map.219 = (bf16[112,128]{1,0:T(8,128)(2,1)}, f32[128,384]{1,0:T(8,128)}, bf16[128,1152]{1,0:T(8,128)(2,1)}, f32[6,128,128]{2,1,0:T(8,128)}, bf16[128,384]...) custom-call(s32[1]{0:T(128)} %bitcast.where, s32[1,32]{1,0:T(1,128)} %ids.3, ...), custom_call_target="tpu_custom_call" | custom-call | flops 7699999744 | bytes 6516872 | tf_op jit(solution)/shard_map/pallas_call | solution.py:536
  9.8 6.4 %collective-permute-start = (bf16[112,128]{1,0:T(8,128)(2,1)}, bf16[112,128]{1,0:T(8,128)(2,1)S(1)}, u32[]{:S(2)}, u32[]{:S(2)}) collective-permute-start(bf16[112,128]{1,0:T(8,128)(2,1)} %get-tuple-element.42), channel_id=1, source_target_pairs={{0,4},{1,5},{2,6},{3,7},{4,0},{5,1},{6,2},{7,3},{8,12},{9,13},{10,... | collective-permute-start | bytes 86024 | tf_op jit(solution)/shard_map/ppermute | solution.py:635
  16.2 2.1 collective-permute-done
  18.2 0.8 pad_maximum_fusion
  19.0 0.1 broadcast_in_dim.2
  19.1 22.0 %all_to_all.30.refs_0_ = bf16[16,224,128]{2,1,0:T(8,128)(2,1)} all-to-all(bf16[16,224,128]{2,1,0:T(8,128)(2,1)S(1)} %broadcast_in_dim.2), channel_id=1, replica_groups={{0,1,2,3,8,9,10,11,16,17,18,19,24,25,26,27},{4,5,6,7,12,13,14,15,20,21,..., dimensions={0} | all-to-all | bytes 1835008 | tf_op jit(solution)/shard_map/all_to_all | solution.py:578
  41.1 0.0 copy-start.11
  41.1 0.0 copy-start.12
  41.1 7.3 %shard_map.220 = (f32[32,8,128]{2,1,0:T(8,128)}, bf16[32,16,128]{2,1,0:T(8,128)(2,1)}, f32[64,384]{1,0:T(8,128)}, bf16[64,1152]{1,0:T(8,128)(2,1)}, f32[6,64,64]...) custom-call(s32[1]{0:T(128)} %bitcast.where, ...), custom_call_target="tpu_custom_call" | custom-call | flops 6600000000 | bytes 5701636 | tf_op jit(solution)/shard_map/pallas_call | solution.py:536
  48.5 8.2 %all-to-all-start.1 = ((f32[32,8,128]{2,1,0:T(8,128)}), f32[32,8,128]{2,1,0:T(8,128)S(1)}, u32[]{:S(2)}, u32[]{:S(2)}) async-start(f32[32,8,128]{2,1,0:T(8,128)} %get-tuple-element.43), calls=%async_computation.1 | async-start | bytes 262144 | tf_op jit(solution)/shard_map/all_to_all | solution.py:650
  56.7 0.0 copy-done.11
  56.7 0.7 copy.36.label
  57.4 0.0 copy-done.12
  57.4 0.7 copy.37.censor
  58.1 0.0 copy-done.3
  58.1 0.8 copy.38.refs_2_
  58.9 0.0 copy-done.9
  58.9 0.8 copy.39.refs_7_
  59.6 9.7 %all-to-all-done.1.refs_0_ = f32[32,8,128]{2,1,0:T(8,128)S(1)} async-done(((f32[32,8,128]{2,1,0:T(8,128)}), f32[32,8,128]{2,1,0:T(8,128)S(1)}, u32[]{:S(2)}, u32[]{:S(2)}) %all-to-all-start.1) | async-done | bytes 131104 | tf_op jit(solution)/shard_map/all_to_all | solution.py:650
  69.3 0.6 copy-done.4
  69.9 12.6 %shard_map.221 = (f32[4,1]{1,0:T(4,128)}, bf16[1024,384]{1,0:T(8,128)(2,1)}, bf16[64,1536]{1,0:T(8,128)(2,1)}, bf16[64,384]{1,0:T(8,128)(2,1)}, bf16[64,384]{1,0...) custom-call(s32[1]{0:T(128)} %bitcast.where, ...), custom_call_target="tpu_custom_call" | custom-call | flops 13200000000 | bytes 7490612 | tf_op jit(solution)/shard_map/pallas_call | solution.py:536
  82.5 0.0 copy-start.2
  82.5 0.0 copy-start.7
  82.5 0.0 copy-start.6
  82.6 4.2 %all-to-all-start.2 = ((bf16[32,32,384]{2,1,0:T(8,128)(2,1)}), bf16[32,32,384]{2,1,0:T(8,128)(2,1)S(1)}, u32[]{:S(2)}, u32[]{:S(2)}) async-start(bf16[32,32,384]{2,1,0:T(8,128)(2,1)} %bitcast.20), calls=%async_computation.2 | async-start | bytes 1572864 | tf_op jit(solution)/shard_map/all_to_all | solution.py:676
  86.8 1.2 reshape.83
  88.0 0.0 copy-done.2
  88.0 0.3 reshape.84
  88.3 0.0 copy-done.7
  88.3 0.2 reshape.85
  88.5 0.0 copy-done.6
  88.5 0.2 reshape.86
  88.6 0.0 copy-start.5
  88.6 0.0 copy-start.8
  88.7 4.9 %shard_map.222 = (bf16[6912,128]{1,0:T(8,128)(2,1)}, bf16[6912,128]{1,0:T(8,128)(2,1)}) custom-call(s32[1]{0:T(128)} %bitcast.5.core, bf16[64,1536]{1,0:T(8,128)(2,1)} %get-tuple-element.67.refs_0_, bf16[64,384]{1,0:T(8,128)(2,1)} %get-tuple-element.68.refs_1_, bf16[64,384]{1,0:T(8,128)(2,1)} %get-tuple-element.69.refs_2_, ...), custom_call_target="tpu_custom_call" | custom-call | flops 5500000256 | bytes 4325380 | tf_op jit(solution)/shard_map/pallas_call | solution.py:536
  93.5 0.1 collective-permute-start.1
  93.7 0.0 copy-done.5
  93.7 0.2 reshape.87
  93.8 0.0 copy-done.8
  93.9 0.1 reshape.88
  94.0 0.9 reshape.97
  95.0 0.1 dynamic-slice_convert_fusion
  95.2 0.6 reshape.92.refs_2_
  95.8 1.9 collective-permute-done.1.refs_1_
  97.7 3.6 %shard_map.223.refs_14_ = bf16[16,432,128]{2,1,0:T(8,128)(2,1)} custom-call(bf16[6912,128]{1,0:T(8,128)(2,1)} %get-tuple-element.74.refs_0_, bf16[6912,128]{1,0:T(8,128)(2,1)} %collective-permute-done.1.refs_1_), custom_call_target="tpu_custom_call" | custom-call | flops 4400000000 | bytes 5308416 | tf_op jit(solution)/shard_map/pallas_call | solution.py:536
  101.3 7.5 %all-to-all-done.2.refs_0_ = bf16[32,32,384]{2,1,0:T(8,128)(2,1)S(1)} async-done(((bf16[32,32,384]{2,1,0:T(8,128)(2,1)}), bf16[32,32,384]{2,1,0:T(8,128)(2,1)S(1)}, u32[]{:S(2)}, u32[]{:S(2)}) %all-to-all-start.2) | async-done | bytes 786464 | tf_op jit(solution)/shard_map/all_to_all | solution.py:676
  108.8 0.9 copy-done.1
  109.7 12.8 %shard_map.224 = (bf16[8144,128]{1,0:T(8,128)(2,1)}, bf16[8144,128]{1,0:T(8,128)(2,1)}) custom-call(s32[1]{0:T(128)} %bitcast.5.core, s32[1,32]{1,0:T(1,128)} %ids.3, bf16[32,32,384]{2,1,0:T(8,128)(2,1)} %copy-done.1, bf16[128,768]{1,0:T(8,128)(2,1)} %bitcast.23, bf16[2,80,128]{2,1,0:T(8,128)(2,1)} %reshape.92.refs_2_, bf16[384,1152]{1,0:T(8,128)(2,1)} %refs_3_.7, ...), custom_call_target="tpu_custom_call" | custom-call | flops 14300000256 | bytes 12664964 | tf_op jit(solution)/shard_map/pallas_call | solution.py:536
  122.5 0.3 collective-permute-start.2
  122.8 4.3 %all-to-all-start.4 = ((bf16[16,432,128]{2,1,0:T(8,128)(2,1)}), bf16[16,432,128]{2,1,0:T(8,128)(2,1)S(1)}, u32[]{:S(2)}, u32[]{:S(2)}) async-start(bf16[16,432,128]{2,1,0:T(8,128)(2,1)} %shard_map.223.refs_14_), calls=%async_computation.4 | async-start | bytes 3538944 | tf_op jit(solution)/shard_map/all_to_all | solution.py:578
  127.1 0.2 collective-permute-done.2.refs_1_
  127.3 3.8 %shard_map.225 = (bf16[16,512,128]{2,1,0:T(8,128)(2,1)}, bf16[80,128]{1,0:T(8,128)(2,1)}) custom-call(bf16[8144,128]{1,0:T(8,128)(2,1)} %get-tuple-element.76.refs_0_, bf16[8144,128]{1,0:T(8,128)(2,1)} %collective-permute-done.2.refs_1_), custom_call_target="tpu_custom_call" | custom-call | flops 4400000000 | bytes 6287360 | tf_op jit(solution)/shard_map/pallas_call | solution.py:536
  131.1 25.6 %all-to-all-done.4.region_in = bf16[16,432,128]{2,1,0:T(8,128)(2,1)S(1)} async-done(((bf16[16,432,128]{2,1,0:T(8,128)(2,1)}), bf16[16,432,128]{2,1,0:T(8,128)(2,1)S(1)}, u32[]{:S(2)}, u32[]{:S(2)}) %all-to-all-start.4) | async-done | bytes 1769504 | tf_op jit(solution)/shard_map/all_to_all | solution.py:578
  156.6 32.7 %all_to_all.31.tile_in = bf16[16,512,128]{2,1,0:T(8,128)(2,1)} all-to-all(bf16[16,512,128]{2,1,0:T(8,128)(2,1)} %get-tuple-element.78), channel_id=1, replica_groups={{0,1,2,3,8,9,10,11,16,17,18,19,24,25,26,27},{4,5,6,7,12,13,14,15,20,21,..., dimensions={0} | all-to-all | bytes 4194304 | tf_op jit(solution)/shard_map/all_to_all | solution.py:578
  189.3 0.0 copy-done
  189.3 3.4 %shard_map.226 = bf16[8,128,128]{2,1,0:T(8,128)(2,1)} custom-call(bf16[16,512,128]{2,1,0:T(8,128)(2,1)} %all_to_all.31.tile_in, bf16[16,432,128]{2,1,0:T(8,128)(2,1)} %copy-done, bf16[80,128]{1,0:T(8,128)(2,1)} %get-tuple-element.79.slide_in), custom_call_target="tpu_custom_call" | custom-call | flops 3300000000 | bytes 4149248 | tf_op jit(solution)/shard_map/pallas_call | solution.py:536
  192.7 3.8 %all-to-all-start.5 = ((bf16[8,128,128]{2,1,0:T(8,128)(2,1)}), bf16[8,128,128]{2,1,0:T(8,128)(2,1)S(1)}, u32[]{:S(2)}, u32[]{:S(2)}) async-start(bf16[8,128,128]{2,1,0:T(8,128)(2,1)} %shard_map.226), calls=%async_computation.5 | async-start | bytes 524288 | tf_op jit(solution)/shard_map/all_to_all | solution.py:578
  196.5 0.0 copy-done.10
  196.6 0.6 reduce
  197.2 8.2 %all-to-all-done.5 = bf16[8,128,128]{2,1,0:T(8,128)(2,1)S(1)} async-done(((bf16[8,128,128]{2,1,0:T(8,128)(2,1)}), bf16[8,128,128]{2,1,0:T(8,128)(2,1)S(1)}, u32[]{:S(2)}, u32[]{:S(2)}) %all-to-all-start.5) | async-done | bytes 262176 | tf_op jit(solution)/shard_map/all_to_all | solution.py:578
  205.4 0.6 slice_bitcast_fusion
  206.0 0.6 slice_bitcast_fusion.1
  206.6 0.6 slice_multiply_fusion
  (16 shorter events, 0.2 us)
Async XLA Ops:
  9.8 8.4 %collective-permute-start = (bf16[112,128]{1,0:T(8,128)(2,1)}, bf16[112,128]{1,0:T(8,128)(2,1)S(1)}, u32[]{:S(2)}, u32[]{:S(2)}) collective-permute-start(bf16[112,128]{1,0:T(8,128)(2,1)} %get-tuple-element.42), channel_id=1, source_target_pairs={{0,4},{1,5},{2,6},{3,7},{4,0},{5,1},{6,2},{7,3},{8,12},{9,13},{10,... | collective-permute-start | bytes 86024 | tf_op jit(solution)/shard_map/ppermute | solution.py:635
  41.1 15.6 %copy-start.11 = (s32[1,4]{1,0:T(1,128)S(1)}, s32[1,4]{1,0:T(1,128)}, u32[]{:S(2)}) copy-start(s32[1,4]{1,0:T(1,128)} %param.23) | copy-start | bytes 52
  41.1 16.3 %copy-start.12 = (s32[1,4]{1,0:T(1,128)S(1)}, s32[1,4]{1,0:T(1,128)}, u32[]{:S(2)}) copy-start(s32[1,4]{1,0:T(1,128)} %param.24) | copy-start | bytes 52
  41.1 16.9 %copy-start.3 = (bf16[384,192]{0,1:T(8,128)(2,1)S(1)}, bf16[384,192]{0,1:T(8,128)(2,1)}, u32[]{:S(2)}) copy-start(bf16[384,192]{0,1:T(8,128)(2,1)} %param.34) | copy-start | bytes 442372
  41.1 17.8 %copy-start.9 = (bf16[192,4]{0,1:T(4,128)(2,1)S(1)}, bf16[192,4]{0,1:T(4,128)(2,1)}, u32[]{:S(2)}) copy-start(bf16[192,4]{0,1:T(4,128)(2,1)} %param.39) | copy-start | bytes 4612
  48.5 20.9 %all-to-all-start.1 = ((f32[32,8,128]{2,1,0:T(8,128)}), f32[32,8,128]{2,1,0:T(8,128)S(1)}, u32[]{:S(2)}, u32[]{:S(2)}) async-start(f32[32,8,128]{2,1,0:T(8,128)} %get-tuple-element.43), calls=%async_computation.1 | async-start | bytes 262144 | tf_op jit(solution)/shard_map/all_to_all | solution.py:650
  69.3 0.6 copy-start.4
  82.5 5.5 %copy-start.2 = (bf16[192,576]{1,0:T(8,128)(2,1)S(1)}, bf16[192,576]{1,0:T(8,128)(2,1)}, u32[]{:S(2)}) copy-start(bf16[192,576]{1,0:T(8,128)(2,1)} %get-tuple-element.55) | copy-start | bytes 663556
  82.5 5.8 %copy-start.7 = (bf16[192,192]{1,0:T(8,128)(2,1)S(1)}, bf16[192,192]{1,0:T(8,128)(2,1)}, u32[]{:S(2)}) copy-start(bf16[192,192]{1,0:T(8,128)(2,1)} %get-tuple-element.56) | copy-start | bytes 221188
  82.5 5.9 %copy-start.6 = (bf16[192,192]{1,0:T(8,128)(2,1)S(1)}, bf16[192,192]{1,0:T(8,128)(2,1)}, u32[]{:S(2)}) copy-start(bf16[192,192]{1,0:T(8,128)(2,1)} %get-tuple-element.57) | copy-start | bytes 221188
  82.6 26.2 %all-to-all-start.2 = ((bf16[32,32,384]{2,1,0:T(8,128)(2,1)}), bf16[32,32,384]{2,1,0:T(8,128)(2,1)S(1)}, u32[]{:S(2)}, u32[]{:S(2)}) async-start(bf16[32,32,384]{2,1,0:T(8,128)(2,1)} %bitcast.20), calls=%async_computation.2 | async-start | bytes 1572864 | tf_op jit(solution)/shard_map/all_to_all | solution.py:676
  88.6 5.1 %copy-start.5 = (bf16[192,192]{1,0:T(8,128)(2,1)S(1)}, bf16[192,192]{1,0:T(8,128)(2,1)}, u32[]{:S(2)}) copy-start(bf16[192,192]{1,0:T(8,128)(2,1)} %get-tuple-element.58) | copy-start | bytes 221188
  88.6 5.2 %copy-start.8 = (bf16[192,4]{1,0:T(8,128)(2,1)S(1)}, bf16[192,4]{1,0:T(8,128)(2,1)}, u32[]{:S(2)}) copy-start(bf16[192,4]{1,0:T(8,128)(2,1)} %get-tuple-element.59) | copy-start | bytes 4612
  93.5 4.1 %collective-permute-start.1 = (bf16[6912,128]{1,0:T(8,128)(2,1)}, bf16[6912,128]{1,0:T(8,128)(2,1)}, u32[]{:S(2)}, u32[]{:S(2)}) collective-permute-start(bf16[6912,128]{1,0:T(8,128)(2,1)} %get-tuple-element.75), channel_id=1, source_target_pairs={{0,32},{32,0},{64,96},{96,64},{128,160},{160,128},{192,224},{224,1... | collective-permute-start | bytes 5308424 | tf_op jit(solution)/shard_map/ppermute | solution.py:582
  108.8 0.9 copy-start.1
  122.5 4.8 %collective-permute-start.2 = (bf16[8144,128]{1,0:T(8,128)(2,1)}, bf16[8144,128]{1,0:T(8,128)(2,1)}, u32[]{:S(2)}, u32[]{:S(2)}) collective-permute-start(bf16[8144,128]{1,0:T(8,128)(2,1)} %get-tuple-element.77), channel_id=1, source_target_pairs={{0,32},{32,0},{64,96},{96,64},{128,160},{160,128},{192,224},{224,1... | collective-permute-start | bytes 6254600 | tf_op jit(solution)/shard_map/ppermute | solution.py:582
  122.8 33.8 %all-to-all-start.4 = ((bf16[16,432,128]{2,1,0:T(8,128)(2,1)}), bf16[16,432,128]{2,1,0:T(8,128)(2,1)S(1)}, u32[]{:S(2)}, u32[]{:S(2)}) async-start(bf16[16,432,128]{2,1,0:T(8,128)(2,1)} %shard_map.223.refs_14_), calls=%async_computation.4 | async-start | bytes 3538944 | tf_op jit(solution)/shard_map/all_to_all | solution.py:578
  156.6 32.7 %copy-start = (bf16[16,432,128]{2,1,0:T(8,128)(2,1)}, bf16[16,432,128]{2,1,0:T(8,128)(2,1)S(1)}, u32[]{:S(2)}) copy-start(bf16[16,432,128]{2,1,0:T(8,128)(2,1)S(1)} %all-to-all-done.4.region_in) | copy-start | bytes 5308420
  189.3 7.3 %copy-start.10 = (f32[4,1]{1,0:T(4,128)S(1)}, f32[4,1]{1,0:T(4,128)}, u32[]{:S(2)}) copy-start(f32[4,1]{1,0:T(4,128)} %get-tuple-element.52) | copy-start | bytes 52
  192.7 12.6 %all-to-all-start.5 = ((bf16[8,128,128]{2,1,0:T(8,128)(2,1)}), bf16[8,128,128]{2,1,0:T(8,128)(2,1)S(1)}, u32[]{:S(2)}, u32[]{:S(2)}) async-start(bf16[8,128,128]{2,1,0:T(8,128)(2,1)} %shard_map.226), calls=%async_computation.5 | async-start | bytes 524288 | tf_op jit(solution)/shard_map/all_to_all | solution.py:578

commit v3 on v2

--- a/solution.py
+++ b/solution.py
@@ -491,8 +491,9 @@
                     source = (z * 32 + y * 8 + h * 4 + x) * rows
                     target = (z * 2 + h) * rows
                     stage[target : target + rows, :] = total[source : source + rows, :]
-            chunks[y * 4 + x] = stage[...].astype(BF16)
-            leaving.append(pltpu.make_async_copy(chunks.at[y * 4 + x], out.at[y * 4 + x], osems.at[y * 4 + x]))
+            to = y * 4 + x if tail else x * 4 + y
+            chunks[to] = stage[...].astype(BF16)
+            leaving.append(pltpu.make_async_copy(chunks.at[to], out.at[to], osems.at[to]))
             leaving[-1].start()
     for copy in leaving:
         copy.wait()
@@ -505,15 +506,15 @@
     slide_total[...] = slide_late[...].astype(F32)
 
     def added(late, target, rows):
-        for start in range(0, rows, 48 if rows % 48 == 0 else 64):
-            size = 48 if rows % 48 == 0 else 64
+        size = 64
+        for start in range(0, rows, size):
             value = late[0, start : start + size, :].astype(F32)
             for i in range(1, 16):
                 value = value + late[i, start : start + size, :].astype(F32)
             target[start : start + size, :] = value
 
-    added(region_late, region_total, 432)
     added(tile_late, total, 512)
+    region_total[...] = region_late[...].astype(F32)
     leaving = []
     for i in range(8):
         stage[0:63, :] = total[i * 63 : (i + 1) * 63, :]
@@ -568,10 +569,16 @@
 
 
 PLANES = [[index_of(z, c, y, h, x) for y in range(4) for x in range(4)] for z in range(4) for c in range(2) for h in range(2)]
+ROWS = [[index_of(z, c, y, h, x) for x in range(4)] for z in range(4) for c in range(2) for h in range(2) for y in range(4)]
+FILES = [[index_of(z, c, y, h, x) for y in range(4)] for z in range(4) for c in range(2) for h in range(2) for x in range(4)]
 COLUMNS = [[index_of(z, c, y, h, x) for z in range(4) for h in range(2)] for c in range(2) for y in range(4) for x in range(4)]
 OTHER_CORE = [(g, g + 1 - 2 * (g % 2)) for g in range(8)]
 OTHER_PLANE = [(d, d + 4 - 8 * (d // 4 % 2)) for d in range(32)]
 ALL = ("grp", "dev")
+
+
+def scattered(array, groups):
+    return lax.psum_scatter(array, ALL, scatter_dimension=0, tiled=False, axis_index_groups=groups)
 
 
 def exchange(array, groups):
@@ -685,7 +692,8 @@
         scalars=1,
     )
     (region_chunks,) = folded(mine, other, 54, 0, 0)
-    region_parts = exchange(region_chunks, PLANES)
+    region_parts = scattered(region_chunks.reshape(4, 1728, LANES), ROWS)
+    region_parts = scattered(region_parts.reshape(4, 432, LANES), FILES)
     slide_flat = jnp.concatenate([g.astype(F32).reshape(-1) for g in rest[7:]]).reshape(4, 2, 4, 2, 4, 1155)
     y, x = member_index // 8, lax.rem(member_index, 4)
     zero = jnp.zeros((), jnp.int32)

time: 208 us -> 227 us (1.091)
  waiting for transfers between devices: 55 us -> 89 us
  blocking collectives: 54.7 us -> 22 us
  between operations: 1.61 us -> 15 us
  starting transfers between devices: 27.3 us -> 30.7 us
    reduce_scatter x0 -> x2, waiting for transfers between devices: none -> 40.4 us  [scattered(): lax.psum_scatter(array, ALL, scatter_dimension=0, tiled=False, axis_index...]
    all_to_all x2 -> x1, blocking collectives: 54.7 us -> 22 us  [exchange(): return lax.all_to_all(array, ALL, 0, 0, axis_index_groups=groups)]
    all_to_all x2, waiting for transfers between devices: 33.7 us -> 23.3 us  [exchange(): return lax.all_to_all(array, ALL, 0, 0, axis_index_groups=groups)]
    ppermute x2, waiting for transfers between devices: 2.04 us -> 6.17 us  [folded(): got = lax.ppermute(other, 'grp', OTHER_CORE)]
    all_to_all x2, starting transfers between devices: 8.07 us -> 11.6 us  [exchange(): return lax.all_to_all(array, ALL, 0, 0, axis_index_groups=groups)]
    unnamed x33 -> x35, local copies, waits for them, and re-layouts: 3.17 us -> 4.6 us
  transfers between devices with their start and end apart: 7 -> 9, of which waited for: 7 -> 9; matrix products, arithmetic and copies ran while one was open for 4% -> 3% of each run, Pallas kernels for 6% -> 6%
where the time goes in v3:
time: 227 us; the launch traced here: 226 us
  waiting for transfers between devices  89 us (39%)
  Pallas kernels  54.9 us (24%)
  starting transfers between devices  30.7 us (14%)
  blocking collectives  22 us (10%)
  between operations  15 us (7%)
  local copies, waits for them, and re-layouts  12.7 us (6%)
    pallas_call x8, Pallas kernels, call(): pl.pallas_call(kernel, out_shape=[jax.ShapeDtypeStruct(shape, kind) for s...  54.9 us
    reduce_scatter x2, waiting for transfers between devices, scattered(): lax.psum_scatter(array, ALL, scatter_dimension=0, tiled=False, axis_index...  40.4 us
    all_to_all x2, waiting for transfers between devices, exchange(): return lax.all_to_all(array, ALL, 0, 0, axis_index_groups=groups)  23.3 us
    all_to_all x1, blocking collectives, exchange(): return lax.all_to_all(array, ALL, 0, 0, axis_index_groups=groups)  22 us
    all_to_all x2, starting transfers between devices, exchange(): return lax.all_to_all(array, ALL, 0, 0, axis_index_groups=groups)  11.6 us
    all_to_all x1, waiting for transfers between devices, body(): all_regions = lax.all_to_all(message, 'dev', 0, 0)  9.65 us
    all_to_all x1, starting transfers between devices, body(): all_regions = lax.all_to_all(message, 'dev', 0, 0)  8.24 us
    all_to_all x1, waiting for transfers between devices, body(): arrived = lax.all_to_all(spread.reshape(32, 32, D), 'dev', 0, 0)  7.39 us
  transfers between devices with their start and end apart: 9, of which 9 were waited for; matrix products, arithmetic and copies ran while one was open for 3% of the time, Pallas kernels for 6%

profile of v3, /device:TPU:32, one launch (start us, length us, event | category | flops | bytes accessed | tf_op | source)
XLA Modules:
  0.0 226.4 jit_solution(12150952599047333277)
XLA Ops:
  7.8 1.6 copy.35
  9.5 6.9 %shard_map.219 = (bf16[112,128]{1,0:T(8,128)(2,1)}, f32[128,384]{1,0:T(8,128)}, bf16[128,1152]{1,0:T(8,128)(2,1)}, f32[6,128,128]{2,1,0:T(8,128)}, bf16[128,384]...) custom-call(s32[1]{0:T(128)} %bitcast.where, s32[1,32]{1,0:T(1,128)} %ids.3, ...), custom_call_target="tpu_custom_call" | custom-call | flops 7699999744 | bytes 6516872 | tf_op jit(solution)/shard_map/pallas_call | solution.py:537
  16.3 6.4 %collective-permute-start = (bf16[112,128]{1,0:T(8,128)(2,1)}, bf16[112,128]{1,0:T(8,128)(2,1)S(1)}, u32[]{:S(2)}, u32[]{:S(2)}) collective-permute-start(bf16[112,128]{1,0:T(8,128)(2,1)} %get-tuple-element.42), channel_id=1, source_target_pairs={{0,4},{1,5},{2,6},{3,7},{4,0},{5,1},{6,2},{7,3},{8,12},{9,13},{10,... | collective-permute-start | bytes 86024 | tf_op jit(solution)/shard_map/ppermute | solution.py:642
  22.7 2.1 collective-permute-done
  24.8 0.8 pad_maximum_fusion
  25.5 0.1 broadcast_in_dim.2
  25.6 22.0 %all_to_all.25.refs_0_ = bf16[16,224,128]{2,1,0:T(8,128)(2,1)} all-to-all(bf16[16,224,128]{2,1,0:T(8,128)(2,1)S(1)} %broadcast_in_dim.2), channel_id=1, replica_groups={{0,1,2,3,8,9,10,11,16,17,18,19,24,25,26,27},{4,5,6,7,12,13,14,15,20,21,..., dimensions={0} | all-to-all | bytes 1835008 | tf_op jit(solution)/shard_map/all_to_all | solution.py:585
  47.7 7.3 %shard_map.220 = (f32[32,8,128]{2,1,0:T(8,128)}, bf16[32,16,128]{2,1,0:T(8,128)(2,1)}, f32[64,384]{1,0:T(8,128)}, bf16[64,1152]{1,0:T(8,128)(2,1)}, f32[6,64,64]...) custom-call(s32[1]{0:T(128)} %bitcast.where, ...), custom_call_target="tpu_custom_call" | custom-call | flops 6600000000 | bytes 5701636 | tf_op jit(solution)/shard_map/pallas_call | solution.py:537
  55.0 8.2 %all-to-all-start.1 = ((f32[32,8,128]{2,1,0:T(8,128)}), f32[32,8,128]{2,1,0:T(8,128)S(1)}, u32[]{:S(2)}, u32[]{:S(2)}) async-start(f32[32,8,128]{2,1,0:T(8,128)} %get-tuple-element.43), calls=%async_computation.1 | async-start | bytes 262144 | tf_op jit(solution)/shard_map/all_to_all | solution.py:657
  63.3 0.0 copy-done.11
  63.3 0.7 copy.36.label
  63.9 0.0 copy-done.12
  63.9 0.7 copy.37.censor
  64.6 0.0 copy-done.3
  64.6 0.8 copy.38.refs_2_
  65.4 0.0 copy-done.9
  65.4 0.8 copy.39.refs_7_
  66.2 9.6 %all-to-all-done.1.refs_0_ = f32[32,8,128]{2,1,0:T(8,128)S(1)} async-done(((f32[32,8,128]{2,1,0:T(8,128)}), f32[32,8,128]{2,1,0:T(8,128)S(1)}, u32[]{:S(2)}, u32[]{:S(2)}) %all-to-all-start.1) | async-done | bytes 131104 | tf_op jit(solution)/shard_map/all_to_all | solution.py:657
  75.8 0.7 copy-done.4
  76.5 12.5 %shard_map.221 = (f32[4,1]{1,0:T(4,128)}, bf16[1024,384]{1,0:T(8,128)(2,1)}, bf16[64,1536]{1,0:T(8,128)(2,1)}, bf16[64,384]{1,0:T(8,128)(2,1)}, bf16[64,384]{1,0...) custom-call(s32[1]{0:T(128)} %bitcast.where, ...), custom_call_target="tpu_custom_call" | custom-call | flops 13200000000 | bytes 7490612 | tf_op jit(solution)/shard_map/pallas_call | solution.py:537
  89.0 0.0 copy-start.2
  89.0 0.0 copy-start.7
  89.0 0.0 copy-start.6
  89.1 4.1 %all-to-all-start.2 = ((bf16[32,32,384]{2,1,0:T(8,128)(2,1)}), bf16[32,32,384]{2,1,0:T(8,128)(2,1)S(1)}, u32[]{:S(2)}, u32[]{:S(2)}) async-start(bf16[32,32,384]{2,1,0:T(8,128)(2,1)} %bitcast.24), calls=%async_computation.2 | async-start | bytes 1572864 | tf_op jit(solution)/shard_map/all_to_all | solution.py:683
  93.1 0.2 reduce-scatter.3.cloned.1.call-start
  93.3 1.2 reshape.86
  94.5 0.0 copy-done.2
  94.6 0.3 reshape.87
  94.8 0.0 copy-done.7
  94.9 0.2 reshape.88
  95.0 0.0 copy-done.6
  95.0 0.2 reshape.89
  95.2 4.9 %shard_map.222 = (bf16[6912,128]{1,0:T(8,128)(2,1)}, bf16[6912,128]{1,0:T(8,128)(2,1)}) custom-call(s32[1]{0:T(128)} %bitcast.5.core, bf16[64,1536]{1,0:T(8,128)(2,1)} %get-tuple-element.67.refs_0_, bf16[64,384]{1,0:T(8,128)(2,1)} %get-tuple-element.68.refs_1_, bf16[64,384]{1,0:T(8,128)(2,1)} %get-tuple-element.69.refs_2_, ...), custom_call_target="tpu_custom_call" | custom-call | flops 5500000256 | bytes 4325380 | tf_op jit(solution)/shard_map/pallas_call | solution.py:537
  100.1 0.1 collective-permute-start.1
  100.3 0.2 reshape.90
  100.5 0.0 copy-done.8
  100.5 0.1 reshape.91
  100.6 0.9 reshape.101
  101.6 0.1 dynamic-slice_convert_fusion
  101.8 0.6 reshape.95.refs_2_
  102.4 1.9 collective-permute-done.1.refs_1_
  104.3 3.6 %shard_map.223.refs_14_ = bf16[16,432,128]{2,1,0:T(8,128)(2,1)} custom-call(bf16[6912,128]{1,0:T(8,128)(2,1)} %get-tuple-element.74.refs_0_, bf16[6912,128]{1,0:T(8,128)(2,1)} %collective-permute-done.1.refs_1_), custom_call_target="tpu_custom_call" | custom-call | flops 4400000000 | bytes 5308416 | tf_op jit(solution)/shard_map/pallas_call | solution.py:537
  107.9 7.4 %all-to-all-done.2.refs_0_ = bf16[32,32,384]{2,1,0:T(8,128)(2,1)S(1)} async-done(((bf16[32,32,384]{2,1,0:T(8,128)(2,1)}), bf16[32,32,384]{2,1,0:T(8,128)(2,1)S(1)}, u32[]{:S(2)}, u32[]{:S(2)}) %all-to-all-start.2) | async-done | bytes 786464 | tf_op jit(solution)/shard_map/all_to_all | solution.py:683
  115.3 0.9 copy-done.1
  116.2 12.9 %shard_map.224 = (bf16[8144,128]{1,0:T(8,128)(2,1)}, bf16[8144,128]{1,0:T(8,128)(2,1)}) custom-call(s32[1]{0:T(128)} %bitcast.5.core, s32[1,32]{1,0:T(1,128)} %ids.3, bf16[32,32,384]{2,1,0:T(8,128)(2,1)} %copy-done.1, bf16[128,768]{1,0:T(8,128)(2,1)} %bitcast.28, bf16[2,80,128]{2,1,0:T(8,128)(2,1)} %reshape.95.refs_2_, bf16[384,1152]{1,0:T(8,128)(2,1)} %refs_3_.7, ...), custom_call_target="tpu_custom_call" | custom-call | flops 14300000256 | bytes 12664964 | tf_op jit(solution)/shard_map/pallas_call | solution.py:537
  129.0 0.1 collective-permute-start.2
  129.1 0.0 reduce-scatter.3.cloned.1.call-update
  129.2 4.3 %collective-permute-done.2.refs_1_ = bf16[8144,128]{1,0:T(8,128)(2,1)S(1)} collective-permute-done((bf16[8144,128]{1,0:T(8,128)(2,1)}, bf16[8144,128]{1,0:T(8,128)(2,1)S(1)}, u32[]{:S(2)}, u32[]{:S(2)}) %collective-permute-start.2) | collective-permute-done | bytes 2084896 | tf_op jit(solution)/shard_map/ppermute | solution.py:589
  133.5 1.4 copy-done.13
  134.9 4.1 %shard_map.225 = (bf16[16,512,128]{2,1,0:T(8,128)(2,1)}, bf16[80,128]{1,0:T(8,128)(2,1)}) custom-call(bf16[8144,128]{1,0:T(8,128)(2,1)} %get-tuple-element.76.refs_0_, bf16[8144,128]{1,0:T(8,128)(2,1)} %copy-done.13), custom_call_target="tpu_custom_call" | custom-call | flops 4400000000 | bytes 6287360 | tf_op jit(solution)/shard_map/pallas_call | solution.py:537
  139.0 4.0 %all-to-all-start.3 = ((bf16[16,512,128]{2,1,0:T(8,128)(2,1)}), bf16[16,512,128]{2,1,0:T(8,128)(2,1)S(1)}, u32[]{:S(2)}, u32[]{:S(2)}) async-start(bf16[16,512,128]{2,1,0:T(8,128)(2,1)} %get-tuple-element.78), calls=%async_computation.3 | async-start | bytes 4194304 | tf_op jit(solution)/shard_map/all_to_all | solution.py:585
  143.0 0.0 reduce-scatter.5.cloned.1.call-start
  143.1 25.3 %reduce-scatter.3.cloned.1.call-done = bf16[1,1728,128]{2,1,0:T(8,128)(2,1)} async-done(((bf16[4,1728,128]{2,1,0:T(8,128)(2,1)}), bf16[1,1728,128]{2,1,0:T(8,128)(2,1)}) %reduce-scatter.3.cloned.1.call-update) | async-done | bytes 442384 | tf_op jit(solution)/shard_map/reduce_scatter | solution.py:581
  168.4 0.0 reduce-scatter.5.cloned.1.call-update
  168.4 15.2 %all-to-all-done.3.tile_in = bf16[16,512,128]{2,1,0:T(8,128)(2,1)S(1)} async-done(((bf16[16,512,128]{2,1,0:T(8,128)(2,1)}), bf16[16,512,128]{2,1,0:T(8,128)(2,1)S(1)}, u32[]{:S(2)}, u32[]{:S(2)}) %all-to-all-start.3) | async-done | bytes 2097184 | tf_op jit(solution)/shard_map/all_to_all | solution.py:585
  183.7 15.1 %reduce-scatter.5.cloned.1.call-done = bf16[1,432,128]{2,1,0:T(8,128)(2,1)} async-done(((bf16[4,432,128]{2,1,0:T(8,128)(2,1)}), bf16[1,432,128]{2,1,0:T(8,128)(2,1)}) %reduce-scatter.5.cloned.1.call-update) | async-done | bytes 110608 | tf_op jit(solution)/shard_map/reduce_scatter | solution.py:581
  198.8 0.0 copy-done
  198.8 2.7 %shard_map.226 = bf16[8,128,128]{2,1,0:T(8,128)(2,1)} custom-call(bf16[16,512,128]{2,1,0:T(8,128)(2,1)} %copy-done, bf16[432,128]{1,0:T(8,128)(2,1)} %bitcast.33, bf16[80,128]{1,0:T(8,128)(2,1)} %get-tuple-element.79.slide_in), custom_call_target="tpu_custom_call" | custom-call | flops 3300000000 | bytes 2490368 | tf_op jit(solution)/shard_map/pallas_call | solution.py:537
  201.5 7.5 %all-to-all-start.4 = ((bf16[8,128,128]{2,1,0:T(8,128)(2,1)}), bf16[8,128,128]{2,1,0:T(8,128)(2,1)S(1)}, u32[]{:S(2)}, u32[]{:S(2)}) async-start(bf16[8,128,128]{2,1,0:T(8,128)(2,1)} %shard_map.226), calls=%async_computation.6 | async-start | bytes 524288 | tf_op jit(solution)/shard_map/all_to_all | solution.py:585
  209.0 0.6 reduce
  209.6 8.0 %all-to-all-done.4 = bf16[8,128,128]{2,1,0:T(8,128)(2,1)S(1)} async-done(((bf16[8,128,128]{2,1,0:T(8,128)(2,1)}), bf16[8,128,128]{2,1,0:T(8,128)(2,1)S(1)}, u32[]{:S(2)}, u32[]{:S(2)}) %all-to-all-start.4) | async-done | bytes 262176 | tf_op jit(solution)/shard_map/all_to_all | solution.py:585
  217.7 0.6 slice_bitcast_fusion
  218.3 0.6 slice_bitcast_fusion.1
  218.9 0.6 slice_multiply_fusion
  (23 shorter events, 0.2 us)
Async XLA Ops:
  16.3 8.4 %collective-permute-start = (bf16[112,128]{1,0:T(8,128)(2,1)}, bf16[112,128]{1,0:T(8,128)(2,1)S(1)}, u32[]{:S(2)}, u32[]{:S(2)}) collective-permute-start(bf16[112,128]{1,0:T(8,128)(2,1)} %get-tuple-element.42), channel_id=1, source_target_pairs={{0,4},{1,5},{2,6},{3,7},{4,0},{5,1},{6,2},{7,3},{8,12},{9,13},{10,... | collective-permute-start | bytes 86024 | tf_op jit(solution)/shard_map/ppermute | solution.py:642
  47.7 15.6 %copy-start.11 = (s32[1,4]{1,0:T(1,128)S(1)}, s32[1,4]{1,0:T(1,128)}, u32[]{:S(2)}) copy-start(s32[1,4]{1,0:T(1,128)} %param.23) | copy-start | bytes 52
  47.7 16.3 %copy-start.12 = (s32[1,4]{1,0:T(1,128)S(1)}, s32[1,4]{1,0:T(1,128)}, u32[]{:S(2)}) copy-start(s32[1,4]{1,0:T(1,128)} %param.24) | copy-start | bytes 52
  47.7 16.9 %copy-start.3 = (bf16[384,192]{0,1:T(8,128)(2,1)S(1)}, bf16[384,192]{0,1:T(8,128)(2,1)}, u32[]{:S(2)}) copy-start(bf16[384,192]{0,1:T(8,128)(2,1)} %param.34) | copy-start | bytes 442372
  47.7 17.8 %copy-start.9 = (bf16[192,4]{0,1:T(4,128)(2,1)S(1)}, bf16[192,4]{0,1:T(4,128)(2,1)}, u32[]{:S(2)}) copy-start(bf16[192,4]{0,1:T(4,128)(2,1)} %param.39) | copy-start | bytes 4612
  55.0 20.9 %all-to-all-start.1 = ((f32[32,8,128]{2,1,0:T(8,128)}), f32[32,8,128]{2,1,0:T(8,128)S(1)}, u32[]{:S(2)}, u32[]{:S(2)}) async-start(f32[32,8,128]{2,1,0:T(8,128)} %get-tuple-element.43), calls=%async_computation.1 | async-start | bytes 262144 | tf_op jit(solution)/shard_map/all_to_all | solution.py:657
  75.8 0.7 copy-start.4
  89.0 5.5 %copy-start.2 = (bf16[192,576]{1,0:T(8,128)(2,1)S(1)}, bf16[192,576]{1,0:T(8,128)(2,1)}, u32[]{:S(2)}) copy-start(bf16[192,576]{1,0:T(8,128)(2,1)} %get-tuple-element.55) | copy-start | bytes 663556
  89.0 5.8 %copy-start.7 = (bf16[192,192]{1,0:T(8,128)(2,1)S(1)}, bf16[192,192]{1,0:T(8,128)(2,1)}, u32[]{:S(2)}) copy-start(bf16[192,192]{1,0:T(8,128)(2,1)} %get-tuple-element.56) | copy-start | bytes 221188
  89.0 6.0 %copy-start.6 = (bf16[192,192]{1,0:T(8,128)(2,1)S(1)}, bf16[192,192]{1,0:T(8,128)(2,1)}, u32[]{:S(2)}) copy-start(bf16[192,192]{1,0:T(8,128)(2,1)} %get-tuple-element.57) | copy-start | bytes 221188
  89.1 26.2 %all-to-all-start.2 = ((bf16[32,32,384]{2,1,0:T(8,128)(2,1)}), bf16[32,32,384]{2,1,0:T(8,128)(2,1)S(1)}, u32[]{:S(2)}, u32[]{:S(2)}) async-start(bf16[32,32,384]{2,1,0:T(8,128)(2,1)} %bitcast.24), calls=%async_computation.2 | async-start | bytes 1572864 | tf_op jit(solution)/shard_map/all_to_all | solution.py:683
  93.1 75.3 %reduce-scatter.3.cloned.1.call-start = ((), (), s32[]{:S(2)}) async-start(), calls=%async_computation.7 | async-start | bytes 2211840 | tf_op jit(solution)/shard_map/reduce_scatter | solution.py:581
  95.2 5.1 %copy-start.5 = (bf16[192,192]{1,0:T(8,128)(2,1)S(1)}, bf16[192,192]{1,0:T(8,128)(2,1)}, u32[]{:S(2)}) copy-start(bf16[192,192]{1,0:T(8,128)(2,1)} %get-tuple-element.58) | copy-start | bytes 221188
  95.2 5.3 %copy-start.8 = (bf16[192,4]{1,0:T(8,128)(2,1)S(1)}, bf16[192,4]{1,0:T(8,128)(2,1)}, u32[]{:S(2)}) copy-start(bf16[192,4]{1,0:T(8,128)(2,1)} %get-tuple-element.59) | copy-start | bytes 4612
  100.1 4.1 %collective-permute-start.1 = (bf16[6912,128]{1,0:T(8,128)(2,1)}, bf16[6912,128]{1,0:T(8,128)(2,1)}, u32[]{:S(2)}, u32[]{:S(2)}) collective-permute-start(bf16[6912,128]{1,0:T(8,128)(2,1)} %get-tuple-element.75), channel_id=1, source_target_pairs={{0,32},{32,0},{64,96},{96,64},{128,160},{160,128},{192,224},{224,1... | collective-permute-start | bytes 5308424 | tf_op jit(solution)/shard_map/ppermute | solution.py:589
  115.3 0.9 copy-start.1
  129.0 4.4 %collective-permute-start.2 = (bf16[8144,128]{1,0:T(8,128)(2,1)}, bf16[8144,128]{1,0:T(8,128)(2,1)S(1)}, u32[]{:S(2)}, u32[]{:S(2)}) collective-permute-start(bf16[8144,128]{1,0:T(8,128)(2,1)} %get-tuple-element.77), channel_id=1, source_target_pairs={{0,32},{32,0},{64,96},{96,64},{128,160},{160,128},{192,224},{224,1... | collective-permute-start | bytes 6254600 | tf_op jit(solution)/shard_map/ppermute | solution.py:589
  133.5 1.4 copy-start.13
  139.0 44.7 %all-to-all-start.3 = ((bf16[16,512,128]{2,1,0:T(8,128)(2,1)}), bf16[16,512,128]{2,1,0:T(8,128)(2,1)S(1)}, u32[]{:S(2)}, u32[]{:S(2)}) async-start(bf16[16,512,128]{2,1,0:T(8,128)(2,1)} %get-tuple-element.78), calls=%async_computation.3 | async-start | bytes 4194304 | tf_op jit(solution)/shard_map/all_to_all | solution.py:585
  143.0 55.7 %reduce-scatter.5.cloned.1.call-start = ((), (), s32[]{:S(2)}) async-start(), calls=%async_computation.8 | async-start | bytes 552960 | tf_op jit(solution)/shard_map/reduce_scatter | solution.py:581
  183.7 15.1 %copy-start = (bf16[16,512,128]{2,1,0:T(8,128)(2,1)}, bf16[16,512,128]{2,1,0:T(8,128)(2,1)S(1)}, u32[]{:S(2)}) copy-start(bf16[16,512,128]{2,1,0:T(8,128)(2,1)S(1)} %all-to-all-done.3.tile_in) | copy-start | bytes 6291460
  198.8 10.2 %copy-start.10 = (f32[4,1]{1,0:T(4,128)S(1)}, f32[4,1]{1,0:T(4,128)}, u32[]{:S(2)}) copy-start(f32[4,1]{1,0:T(4,128)} %get-tuple-element.52) | copy-start | bytes 52
  201.5 16.2 %all-to-all-start.4 = ((bf16[8,128,128]{2,1,0:T(8,128)(2,1)}), bf16[8,128,128]{2,1,0:T(8,128)(2,1)S(1)}, u32[]{:S(2)}, u32[]{:S(2)}) async-start(bf16[8,128,128]{2,1,0:T(8,128)(2,1)} %shard_map.226), calls=%async_computation.6 | async-start | bytes 524288 | tf_op jit(solution)/shard_map/all_to_all | solution.py:585
Sparse Core Ops, SparseCore 0:
  129.3 39.0 reduce-scatter.2
  171.1 27.6 reduce-scatter.4

commit v4 on v2

--- a/solution.py
+++ b/solution.py
@@ -498,22 +498,36 @@
         copy.wait()
 
 
-def merge(tile_in, region_in, slide_in, out, tile_buf, region_buf, slide_buf, total, region_total, slide_total, stage, chunks, sems, osems):
+def gate(source, unread, target):
+    pass
+
+
+def plane_sum(parts, out, buffer, total, sems):
+    copies = [pltpu.make_async_copy(parts.at[:, i * 144 : (i + 1) * 144, :], buffer.at[:, i * 144 : (i + 1) * 144, :], sems.at[i]) for i in range(3)]
+    for copy in copies:
+        copy.start()
+    for i in range(3):
+        copies[i].wait()
+        for start in range(i * 144, (i + 1) * 144, 48):
+            value = buffer[0, start : start + 48, :].astype(F32)
+            for j in range(1, 16):
+                value = value + buffer[j, start : start + 48, :].astype(F32)
+            total[start : start + 48, :] = value
+    leave([(total, out)], sems)
+
+
+def merge(tile_in, region_in, slide_in, out, tile_buf, region_buf, slide_buf, total, slide_total, stage, chunks, sems, osems):
     tile_late = Late(tile_in, tile_buf, sems.at[0])
     region_late = Late(region_in, region_buf, sems.at[1])
     slide_late = Late(slide_in, slide_buf, sems.at[2])
     slide_total[...] = slide_late[...].astype(F32)
 
-    def added(late, target, rows):
-        for start in range(0, rows, 48 if rows % 48 == 0 else 64):
-            size = 48 if rows % 48 == 0 else 64
-            value = late[0, start : start + size, :].astype(F32)
-            for i in range(1, 16):
-                value = value + late[i, start : start + size, :].astype(F32)
-            target[start : start + size, :] = value
-
-    added(region_late, region_total, 432)
-    added(tile_late, total, 512)
+    for start in range(0, 512, 64):
+        value = tile_late[0, start : start + 64, :].astype(F32)
+        for i in range(1, 16):
+            value = value + tile_late[i, start : start + 64, :].astype(F32)
+        total[start : start + 64, :] = value
+    region_total = region_late.ref()
     leaving = []
     for i in range(8):
         stage[0:63, :] = total[i * 63 : (i + 1) * 63, :]
@@ -686,6 +700,13 @@
     )
     (region_chunks,) = folded(mine, other, 54, 0, 0)
     region_parts = exchange(region_chunks, PLANES)
+    (region_sums,) = call(
+        plane_sum,
+        2 * US,
+        [((432, LANES), F32)],
+        like((region_parts,)) + [((432, LANES), F32), semaphores(3)],
+        (region_parts,),
+    )
     slide_flat = jnp.concatenate([g.astype(F32).reshape(-1) for g in rest[7:]]).reshape(4, 2, 4, 2, 4, 1155)
     y, x = member_index // 8, lax.rem(member_index, 4)
     zero = jnp.zeros((), jnp.int32)
@@ -703,15 +724,22 @@
         scalars=1,
         whole=1,
     )
+    other = pl.pallas_call(
+        gate,
+        out_shape=jax.ShapeDtypeStruct(other.shape, other.dtype),
+        in_specs=[pl.BlockSpec(memory_space=pl.ANY)] * 2,
+        out_specs=pl.BlockSpec(memory_space=pl.ANY),
+        input_output_aliases={0: 0},
+    )(other, region_parts)
     tile_chunks, slide_sums = folded(mine, other, 63, 8, 1)
     tile_parts = exchange(tile_chunks, PLANES)
-    ins = (tile_parts, region_parts, slide_sums)
+    ins = (tile_parts, region_sums, slide_sums)
     (last,) = call(
         merge,
         3 * US,
         [((8, 128, LANES), BF16)],
         like(ins)
-        + [((512, LANES), F32), ((432, LANES), F32), ((80, LANES), F32), ((128, LANES), F32), ((8, 128, LANES), BF16)]
+        + [((512, LANES), F32), ((80, LANES), F32), ((128, LANES), F32), ((8, 128, LANES), BF16)]
         + [semaphores(3), semaphores(8)],
         ins,
     )

time: 208 us -> 209 us (level)
  blocking collectives: 54.7 us -> 22 us
  waiting for transfers between devices: 55 us -> 78.7 us
  starting transfers between devices: 27.3 us -> 32.1 us
  local copies, waits for them, and re-layouts: 11.3 us -> 15.3 us
    all_to_all x2 -> x1, blocking collectives: 54.7 us -> 22 us  [exchange(): return lax.all_to_all(array, ALL, 0, 0, axis_index_groups=groups)]
    all_to_all x2 -> x3, waiting for transfers between devices: 33.7 us -> 51.5 us  [exchange(): return lax.all_to_all(array, ALL, 0, 0, axis_index_groups=groups)]
    ppermute x2, waiting for transfers between devices: 2.04 us -> 7.68 us  [folded(): got = lax.ppermute(other, 'grp', OTHER_CORE)]
    all_to_all x2 -> x3, starting transfers between devices: 8.07 us -> 13.2 us  [exchange(): return lax.all_to_all(array, ALL, 0, 0, axis_index_groups=groups)]
    unnamed x33 -> x37, local copies, waits for them, and re-layouts: 3.17 us -> 7.12 us
    pallas_call x8 -> x9, Pallas kernels: 55.3 us -> 56.8 us  [call(): pl.pallas_call(kernel, out_shape=[jax.ShapeDtypeStruct(shape, kind) for s...]
  transfers between devices with their start and end apart: 7 -> 8, of which waited for: 7 -> 8; matrix products, arithmetic and copies ran while one was open for 4% -> 4% of each run, Pallas kernels for 6% -> 11%
where the time goes in v4:
time: 209 us
  waiting for transfers between devices  78.7 us (38%)
  Pallas kernels  56.8 us (27%)
  starting transfers between devices  32.1 us (15%)
  blocking collectives  22 us (11%)
  local copies, waits for them, and re-layouts  15.3 us (7%)
    pallas_call x9, Pallas kernels, call(): pl.pallas_call(kernel, out_shape=[jax.ShapeDtypeStruct(shape, kind) for s...  56.8 us
    all_to_all x3, waiting for transfers between devices, exchange(): return lax.all_to_all(array, ALL, 0, 0, axis_index_groups=groups)  51.5 us
    all_to_all x1, blocking collectives, exchange(): return lax.all_to_all(array, ALL, 0, 0, axis_index_groups=groups)  22 us
    all_to_all x3, starting transfers between devices, exchange(): return lax.all_to_all(array, ALL, 0, 0, axis_index_groups=groups)  13.2 us
    all_to_all x1, waiting for transfers between devices, body(): all_regions = lax.all_to_all(message, 'dev', 0, 0)  9.66 us
    all_to_all x1, starting transfers between devices, body(): all_regions = lax.all_to_all(message, 'dev', 0, 0)  8.24 us
    all_to_all x1, waiting for transfers between devices, body(): arrived = lax.all_to_all(spread.reshape(32, 32, D), 'dev', 0, 0)  7.8 us
    ppermute x2, waiting for transfers between devices, folded(): got = lax.ppermute(other, 'grp', OTHER_CORE)  7.68 us
  transfers between devices with their start and end apart: 8, of which 8 were waited for; matrix products, arithmetic and copies ran while one was open for 4% of the time, Pallas kernels for 11%

profile of v4, /device:TPU:32, one launch (start us, length us, event | category | flops | bytes accessed | tf_op | source)
XLA Modules:
  0.0 208.5 jit_solution(10999349748849293383)
XLA Ops:
  1.3 1.6 copy.36
  2.9 6.9 %shard_map.219 = (bf16[112,128]{1,0:T(8,128)(2,1)}, f32[128,384]{1,0:T(8,128)}, bf16[128,1152]{1,0:T(8,128)(2,1)}, f32[6,128,128]{2,1,0:T(8,128)}, bf16[128,384]...) custom-call(s32[1]{0:T(128)} %bitcast.where, s32[1,32]{1,0:T(1,128)} %ids.3, ...), custom_call_target="tpu_custom_call" | custom-call | flops 7699999744 | bytes 6516872 | tf_op jit(solution)/shard_map/pallas_call | solution.py:550
  9.8 6.4 %collective-permute-start = (bf16[112,128]{1,0:T(8,128)(2,1)}, bf16[112,128]{1,0:T(8,128)(2,1)S(1)}, u32[]{:S(2)}, u32[]{:S(2)}) collective-permute-start(bf16[112,128]{1,0:T(8,128)(2,1)} %get-tuple-element.42), channel_id=1, source_target_pairs={{0,4},{1,5},{2,6},{3,7},{4,0},{5,1},{6,2},{7,3},{8,12},{9,13},{10,... | collective-permute-start | bytes 86024 | tf_op jit(solution)/shard_map/ppermute | solution.py:649
  16.2 2.1 collective-permute-done
  18.2 0.8 pad_maximum_fusion
  19.0 0.1 broadcast_in_dim.2
  19.1 22.0 %all_to_all.30.refs_0_ = bf16[16,224,128]{2,1,0:T(8,128)(2,1)} all-to-all(bf16[16,224,128]{2,1,0:T(8,128)(2,1)S(1)} %broadcast_in_dim.2), channel_id=1, replica_groups={{0,1,2,3,8,9,10,11,16,17,18,19,24,25,26,27},{4,5,6,7,12,13,14,15,20,21,..., dimensions={0} | all-to-all | bytes 1835008 | tf_op jit(solution)/shard_map/all_to_all | solution.py:592
  41.1 7.3 %shard_map.220 = (f32[32,8,128]{2,1,0:T(8,128)}, bf16[32,16,128]{2,1,0:T(8,128)(2,1)}, f32[64,384]{1,0:T(8,128)}, bf16[64,1152]{1,0:T(8,128)(2,1)}, f32[6,64,64]...) custom-call(s32[1]{0:T(128)} %bitcast.where, ...), custom_call_target="tpu_custom_call" | custom-call | flops 6600000000 | bytes 5701636 | tf_op jit(solution)/shard_map/pallas_call | solution.py:550
  48.5 8.2 %all-to-all-start.1 = ((f32[32,8,128]{2,1,0:T(8,128)}), f32[32,8,128]{2,1,0:T(8,128)S(1)}, u32[]{:S(2)}, u32[]{:S(2)}) async-start(f32[32,8,128]{2,1,0:T(8,128)} %get-tuple-element.43), calls=%async_computation.1 | async-start | bytes 262144 | tf_op jit(solution)/shard_map/all_to_all | solution.py:664
  56.7 0.0 copy-done.12
  56.8 0.7 copy.37.label
  57.4 0.0 copy-done.13
  57.4 0.7 copy.38.censor
  58.1 0.0 copy-done.4
  58.1 0.8 copy.39.refs_2_
  58.9 0.0 copy-done.10
  58.9 0.8 copy.40.refs_7_
  59.7 9.7 %all-to-all-done.1.refs_0_ = f32[32,8,128]{2,1,0:T(8,128)S(1)} async-done(((f32[32,8,128]{2,1,0:T(8,128)}), f32[32,8,128]{2,1,0:T(8,128)S(1)}, u32[]{:S(2)}, u32[]{:S(2)}) %all-to-all-start.1) | async-done | bytes 131104 | tf_op jit(solution)/shard_map/all_to_all | solution.py:664
  69.3 0.6 copy-done.5
  70.0 12.6 %shard_map.221 = (f32[4,1]{1,0:T(4,128)}, bf16[1024,384]{1,0:T(8,128)(2,1)}, bf16[64,1536]{1,0:T(8,128)(2,1)}, bf16[64,384]{1,0:T(8,128)(2,1)}, bf16[64,384]{1,0...) custom-call(s32[1]{0:T(128)} %bitcast.where, ...), custom_call_target="tpu_custom_call" | custom-call | flops 13200000000 | bytes 7490612 | tf_op jit(solution)/shard_map/pallas_call | solution.py:550
  82.5 0.0 copy-start.3
  82.6 4.2 %all-to-all-start.2 = ((bf16[32,32,384]{2,1,0:T(8,128)(2,1)}), bf16[32,32,384]{2,1,0:T(8,128)(2,1)S(1)}, u32[]{:S(2)}, u32[]{:S(2)}) async-start(bf16[32,32,384]{2,1,0:T(8,128)(2,1)} %bitcast.20), calls=%async_computation.2 | async-start | bytes 1572864 | tf_op jit(solution)/shard_map/all_to_all | solution.py:690
  86.8 1.2 reshape.83
  88.0 0.0 copy-done.3
  88.0 0.3 reshape.84
  88.3 0.0 copy-start.8
  88.3 0.0 copy-start.7
  88.3 0.0 copy-start.6
  88.3 0.0 copy-start.9
  88.4 4.9 %shard_map.222 = (bf16[6912,128]{1,0:T(8,128)(2,1)}, bf16[6912,128]{1,0:T(8,128)(2,1)}) custom-call(s32[1]{0:T(128)} %bitcast.5.core, bf16[64,1536]{1,0:T(8,128)(2,1)} %get-tuple-element.67.refs_0_, bf16[64,384]{1,0:T(8,128)(2,1)} %get-tuple-element.68.refs_1_, bf16[64,384]{1,0:T(8,128)(2,1)} %get-tuple-element.69.refs_2_, ...), custom_call_target="tpu_custom_call" | custom-call | flops 5500000256 | bytes 4325380 | tf_op jit(solution)/shard_map/pallas_call | solution.py:550
  93.2 0.1 collective-permute-start.1
  93.4 0.0 copy-done.8
  93.4 0.2 reshape.85
  93.5 0.0 copy-done.7
  93.5 0.2 reshape.86
  93.7 0.0 copy-done.6
  93.7 0.2 reshape.87
  93.9 0.1 reshape.88
  94.0 3.3 %collective-permute-done.1.refs_1_ = bf16[6912,128]{1,0:T(8,128)(2,1)} collective-permute-done((bf16[6912,128]{1,0:T(8,128)(2,1)}, bf16[6912,128]{1,0:T(8,128)(2,1)}, u32[]{:S(2)}, u32[]{:S(2)}) %collective-permute-start.1) | collective-permute-done | bytes 1769504 | tf_op jit(solution)/shard_map/ppermute | solution.py:596
  97.4 3.7 %shard_map.223.refs_14_ = bf16[16,432,128]{2,1,0:T(8,128)(2,1)} custom-call(bf16[6912,128]{1,0:T(8,128)(2,1)} %get-tuple-element.74.refs_0_, bf16[6912,128]{1,0:T(8,128)(2,1)} %collective-permute-done.1.refs_1_), custom_call_target="tpu_custom_call" | custom-call | flops 4400000000 | bytes 5308416 | tf_op jit(solution)/shard_map/pallas_call | solution.py:550
  101.0 7.8 %all-to-all-done.2.refs_0_ = bf16[32,32,384]{2,1,0:T(8,128)(2,1)S(1)} async-done(((bf16[32,32,384]{2,1,0:T(8,128)(2,1)}), bf16[32,32,384]{2,1,0:T(8,128)(2,1)S(1)}, u32[]{:S(2)}, u32[]{:S(2)}) %all-to-all-start.2) | async-done | bytes 786464 | tf_op jit(solution)/shard_map/all_to_all | solution.py:690
  108.8 0.9 copy-done.2
  109.7 4.3 %all-to-all-start.3 = ((bf16[16,432,128]{2,1,0:T(8,128)(2,1)}), bf16[16,432,128]{2,1,0:T(8,128)(2,1)S(1)}, u32[]{:S(2)}, u32[]{:S(2)}) async-start(bf16[16,432,128]{2,1,0:T(8,128)(2,1)} %shard_map.223.refs_14_), calls=%async_computation.3 | async-start | bytes 3538944 | tf_op jit(solution)/shard_map/all_to_all | solution.py:592
  114.0 0.9 reshape.97
  115.0 0.1 dynamic-slice_convert_fusion
  115.2 0.6 reshape.92.refs_2_
  115.8 12.8 %shard_map.224 = (bf16[8144,128]{1,0:T(8,128)(2,1)}, bf16[8144,128]{1,0:T(8,128)(2,1)}) custom-call(s32[1]{0:T(128)} %bitcast.5.core, s32[1,32]{1,0:T(1,128)} %ids.3, bf16[32,32,384]{2,1,0:T(8,128)(2,1)} %copy-done.2, bf16[128,768]{1,0:T(8,128)(2,1)} %bitcast.23, bf16[2,80,128]{2,1,0:T(8,128)(2,1)} %reshape.92.refs_2_, bf16[384,1152]{1,0:T(8,128)(2,1)} %refs_3_.7, ...), custom_call_target="tpu_custom_call" | custom-call | flops 14300000256 | bytes 12664964 | tf_op jit(solution)/shard_map/pallas_call | solution.py:550
  128.7 10.8 %all-to-all-done.3.unread.parts = bf16[16,432,128]{2,1,0:T(8,128)(2,1)S(1)} async-done(((bf16[16,432,128]{2,1,0:T(8,128)(2,1)}), bf16[16,432,128]{2,1,0:T(8,128)(2,1)S(1)}, u32[]{:S(2)}, u32[]{:S(2)}) %all-to-all-start.3) | async-done | bytes 1769504 | tf_op jit(solution)/shard_map/all_to_all | solution.py:592
  139.5 1.2 copy-done
  140.7 0.0 collective-permute-start.2
  140.7 4.3 %collective-permute-done.2.refs_1_ = bf16[8144,128]{1,0:T(8,128)(2,1)S(1)} collective-permute-done((bf16[8144,128]{1,0:T(8,128)(2,1)}, bf16[8144,128]{1,0:T(8,128)(2,1)S(1)}, u32[]{:S(2)}, u32[]{:S(2)}) %collective-permute-start.2) | collective-permute-done | bytes 2084896 | tf_op jit(solution)/shard_map/ppermute | solution.py:596
  145.1 1.3 copy-done.14
  146.4 3.8 %shard_map.226 = (bf16[16,512,128]{2,1,0:T(8,128)(2,1)}, bf16[80,128]{1,0:T(8,128)(2,1)}) custom-call(bf16[8144,128]{1,0:T(8,128)(2,1)} %get-tuple-element.76.refs_0_, bf16[8144,128]{1,0:T(8,128)(2,1)} %copy-done.14), custom_call_target="tpu_custom_call" | custom-call | flops 4400000000 | bytes 6287360 | tf_op jit(solution)/shard_map/pallas_call | solution.py:550
  150.2 3.7 %all-to-all-start.4 = ((bf16[16,512,128]{2,1,0:T(8,128)(2,1)}), bf16[16,512,128]{2,1,0:T(8,128)(2,1)S(1)}, u32[]{:S(2)}, u32[]{:S(2)}) async-start(bf16[16,512,128]{2,1,0:T(8,128)(2,1)} %get-tuple-element.78), calls=%async_computation.4 | async-start | bytes 4194304 | tf_op jit(solution)/shard_map/all_to_all | solution.py:592
  153.9 2.2 %shard_map.227.region_in = f32[432,128]{1,0:T(8,128)} custom-call(bf16[16,432,128]{2,1,0:T(8,128)(2,1)} %copy-done), custom_call_target="tpu_custom_call" | custom-call | flops 2200000000 | bytes 1990656 | tf_op jit(solution)/shard_map/pallas_call | solution.py:550
  156.2 31.7 %all-to-all-done.4.tile_in = bf16[16,512,128]{2,1,0:T(8,128)(2,1)S(1)} async-done(((bf16[16,512,128]{2,1,0:T(8,128)(2,1)}), bf16[16,512,128]{2,1,0:T(8,128)(2,1)S(1)}, u32[]{:S(2)}, u32[]{:S(2)}) %all-to-all-start.4) | async-done | bytes 2097184 | tf_op jit(solution)/shard_map/all_to_all | solution.py:592
  187.8 1.3 copy-done.1
  189.2 2.7 %shard_map.228 = bf16[8,128,128]{2,1,0:T(8,128)(2,1)} custom-call(bf16[16,512,128]{2,1,0:T(8,128)(2,1)} %copy-done.1, f32[432,128]{1,0:T(8,128)} %shard_map.227.region_in, bf16[80,128]{1,0:T(8,128)(2,1)} %get-tuple-element.79.slide_in), custom_call_target="tpu_custom_call" | custom-call | flops 3300000000 | bytes 2600960 | tf_op jit(solution)/shard_map/pallas_call | solution.py:550
  191.9 5.2 %all-to-all-start.5 = ((bf16[8,128,128]{2,1,0:T(8,128)(2,1)}), bf16[8,128,128]{2,1,0:T(8,128)(2,1)S(1)}, u32[]{:S(2)}, u32[]{:S(2)}) async-start(bf16[8,128,128]{2,1,0:T(8,128)(2,1)} %shard_map.228), calls=%async_computation.5 | async-start | bytes 524288 | tf_op jit(solution)/shard_map/all_to_all | solution.py:592
  197.1 0.6 reduce
  197.7 9.0 %all-to-all-done.5 = bf16[8,128,128]{2,1,0:T(8,128)(2,1)S(1)} async-done(((bf16[8,128,128]{2,1,0:T(8,128)(2,1)}), bf16[8,128,128]{2,1,0:T(8,128)(2,1)S(1)}, u32[]{:S(2)}, u32[]{:S(2)}) %all-to-all-start.5) | async-done | bytes 262176 | tf_op jit(solution)/shard_map/all_to_all | solution.py:592
  206.7 0.6 slice_bitcast_fusion
  207.3 0.6 slice_bitcast_fusion.1
  207.9 0.6 slice_multiply_fusion
  (23 shorter events, 0.2 us)
Async XLA Ops:
  9.8 8.4 %collective-permute-start = (bf16[112,128]{1,0:T(8,128)(2,1)}, bf16[112,128]{1,0:T(8,128)(2,1)S(1)}, u32[]{:S(2)}, u32[]{:S(2)}) collective-permute-start(bf16[112,128]{1,0:T(8,128)(2,1)} %get-tuple-element.42), channel_id=1, source_target_pairs={{0,4},{1,5},{2,6},{3,7},{4,0},{5,1},{6,2},{7,3},{8,12},{9,13},{10,... | collective-permute-start | bytes 86024 | tf_op jit(solution)/shard_map/ppermute | solution.py:649
  41.1 15.6 %copy-start.12 = (s32[1,4]{1,0:T(1,128)S(1)}, s32[1,4]{1,0:T(1,128)}, u32[]{:S(2)}) copy-start(s32[1,4]{1,0:T(1,128)} %param.23) | copy-start | bytes 52
  41.1 16.3 %copy-start.13 = (s32[1,4]{1,0:T(1,128)S(1)}, s32[1,4]{1,0:T(1,128)}, u32[]{:S(2)}) copy-start(s32[1,4]{1,0:T(1,128)} %param.24) | copy-start | bytes 52
  41.1 16.9 %copy-start.4 = (bf16[384,192]{0,1:T(8,128)(2,1)S(1)}, bf16[384,192]{0,1:T(8,128)(2,1)}, u32[]{:S(2)}) copy-start(bf16[384,192]{0,1:T(8,128)(2,1)} %param.34) | copy-start | bytes 442372
  41.1 17.8 %copy-start.10 = (bf16[192,4]{0,1:T(4,128)(2,1)S(1)}, bf16[192,4]{0,1:T(4,128)(2,1)}, u32[]{:S(2)}) copy-start(bf16[192,4]{0,1:T(4,128)(2,1)} %param.39) | copy-start | bytes 4612
  48.5 20.9 %all-to-all-start.1 = ((f32[32,8,128]{2,1,0:T(8,128)}), f32[32,8,128]{2,1,0:T(8,128)S(1)}, u32[]{:S(2)}, u32[]{:S(2)}) async-start(f32[32,8,128]{2,1,0:T(8,128)} %get-tuple-element.43), calls=%async_computation.1 | async-start | bytes 262144 | tf_op jit(solution)/shard_map/all_to_all | solution.py:664
  69.3 0.6 copy-start.5
  82.5 5.5 %copy-start.3 = (bf16[192,576]{1,0:T(8,128)(2,1)S(1)}, bf16[192,576]{1,0:T(8,128)(2,1)}, u32[]{:S(2)}) copy-start(bf16[192,576]{1,0:T(8,128)(2,1)} %get-tuple-element.55) | copy-start | bytes 663556
  82.6 26.3 %all-to-all-start.2 = ((bf16[32,32,384]{2,1,0:T(8,128)(2,1)}), bf16[32,32,384]{2,1,0:T(8,128)(2,1)S(1)}, u32[]{:S(2)}, u32[]{:S(2)}) async-start(bf16[32,32,384]{2,1,0:T(8,128)(2,1)} %bitcast.20), calls=%async_computation.2 | async-start | bytes 1572864 | tf_op jit(solution)/shard_map/all_to_all | solution.py:690
  88.3 5.1 %copy-start.8 = (bf16[192,192]{1,0:T(8,128)(2,1)S(1)}, bf16[192,192]{1,0:T(8,128)(2,1)}, u32[]{:S(2)}) copy-start(bf16[192,192]{1,0:T(8,128)(2,1)} %get-tuple-element.56) | copy-start | bytes 221188
  88.3 5.2 %copy-start.7 = (bf16[192,192]{1,0:T(8,128)(2,1)S(1)}, bf16[192,192]{1,0:T(8,128)(2,1)}, u32[]{:S(2)}) copy-start(bf16[192,192]{1,0:T(8,128)(2,1)} %get-tuple-element.57) | copy-start | bytes 221188
  88.3 5.4 %copy-start.6 = (bf16[192,192]{1,0:T(8,128)(2,1)S(1)}, bf16[192,192]{1,0:T(8,128)(2,1)}, u32[]{:S(2)}) copy-start(bf16[192,192]{1,0:T(8,128)(2,1)} %get-tuple-element.58) | copy-start | bytes 221188
  88.3 5.5 %copy-start.9 = (bf16[192,4]{1,0:T(8,128)(2,1)S(1)}, bf16[192,4]{1,0:T(8,128)(2,1)}, u32[]{:S(2)}) copy-start(bf16[192,4]{1,0:T(8,128)(2,1)} %get-tuple-element.59) | copy-start | bytes 4612
  93.2 4.1 %collective-permute-start.1 = (bf16[6912,128]{1,0:T(8,128)(2,1)}, bf16[6912,128]{1,0:T(8,128)(2,1)}, u32[]{:S(2)}, u32[]{:S(2)}) collective-permute-start(bf16[6912,128]{1,0:T(8,128)(2,1)} %get-tuple-element.75), channel_id=1, source_target_pairs={{0,32},{32,0},{64,96},{96,64},{128,160},{160,128},{192,224},{224,1... | collective-permute-start | bytes 5308424 | tf_op jit(solution)/shard_map/ppermute | solution.py:596
  108.8 0.9 copy-start.2
  109.7 29.8 %all-to-all-start.3 = ((bf16[16,432,128]{2,1,0:T(8,128)(2,1)}), bf16[16,432,128]{2,1,0:T(8,128)(2,1)S(1)}, u32[]{:S(2)}, u32[]{:S(2)}) async-start(bf16[16,432,128]{2,1,0:T(8,128)(2,1)} %shard_map.223.refs_14_), calls=%async_computation.3 | async-start | bytes 3538944 | tf_op jit(solution)/shard_map/all_to_all | solution.py:592
  139.5 1.2 copy-start
  140.7 4.4 %collective-permute-start.2 = (bf16[8144,128]{1,0:T(8,128)(2,1)}, bf16[8144,128]{1,0:T(8,128)(2,1)S(1)}, u32[]{:S(2)}, u32[]{:S(2)}) collective-permute-start(bf16[8144,128]{1,0:T(8,128)(2,1)} %shard_map.225), channel_id=1, source_target_pairs={{0,32},{32,0},{64,96},{96,64},{128,160},{160,128},{192,224},{224,1... | collective-permute-start | bytes 6254600 | tf_op jit(solution)/shard_map/ppermute | solution.py:596
  145.1 1.4 copy-start.14
  150.2 37.6 %all-to-all-start.4 = ((bf16[16,512,128]{2,1,0:T(8,128)(2,1)}), bf16[16,512,128]{2,1,0:T(8,128)(2,1)S(1)}, u32[]{:S(2)}, u32[]{:S(2)}) async-start(bf16[16,512,128]{2,1,0:T(8,128)(2,1)} %get-tuple-element.78), calls=%async_computation.4 | async-start | bytes 4194304 | tf_op jit(solution)/shard_map/all_to_all | solution.py:592
  187.8 1.3 copy-start.1
  189.2 7.9 %copy-start.11 = (f32[4,1]{1,0:T(4,128)S(1)}, f32[4,1]{1,0:T(4,128)}, u32[]{:S(2)}) copy-start(f32[4,1]{1,0:T(4,128)} %get-tuple-element.52) | copy-start | bytes 52
  191.9 14.8 %all-to-all-start.5 = ((bf16[8,128,128]{2,1,0:T(8,128)(2,1)}), bf16[8,128,128]{2,1,0:T(8,128)(2,1)S(1)}, u32[]{:S(2)}, u32[]{:S(2)}) async-start(bf16[8,128,128]{2,1,0:T(8,128)(2,1)} %shard_map.228), calls=%async_computation.5 | async-start | bytes 524288 | tf_op jit(solution)/shard_map/all_to_all | solution.py:592

commit v5 on v4

--- a/solution.py
+++ b/solution.py
@@ -155,8 +155,8 @@
 
 
 class Early:
-    def __init__(self, target, buffer, sem):
-        self.copy = pltpu.make_async_copy(buffer, target, sem)
+    def __init__(self, target, buffer, sem, part=None):
+        self.copy = pltpu.make_async_copy(buffer if part is None else buffer.at[part], target, sem)
         self.buffer = buffer
 
     def __getitem__(self, index):
@@ -183,7 +183,7 @@
 
 
 def broadcast_out(block, out, sems):
-    copies = [pltpu.make_async_copy(block, out.at[i], sems.at[i]) for i in range(32)]
+    copies = [pltpu.make_async_copy(block, out.at[i], sems.at[i]) for i in range(16)]
     for copy in copies:
         copy.start()
     for copy in copies:
@@ -251,9 +251,20 @@
     return member, (within + ahead).astype(jnp.int32), count
 
 
-def choice(member, slot, b):
+def both_slots(ids, device):
+    first = device - 4 * lax.rem(device // 4, 2)
+    return first, [slots_of(ids, first + 4 * b) for b in range(2)]
+
+
+def choice(slots, i):
     k = lax.broadcasted_iota(jnp.int32, (SLOTS, 128), 0)
-    return jnp.where((slot[b : b + 1] == k) & (member[b : b + 1] > 0.0), 1.0, 0.0).astype(BF16)
+    parts = [jnp.where((slot[i : i + 1] == k) & (member[i : i + 1] > 0.0), 1.0, 0.0) for member, slot, _ in slots]
+    return jnp.concatenate(parts, axis=0).astype(BF16)
+
+
+def usable_of(slots):
+    k = lax.broadcasted_iota(jnp.int32, (SLOTS, 1), 0).astype(F32)
+    return [k < count for _, _, count in slots]
 
 
 def region_forward(where, *refs):
@@ -274,26 +285,29 @@
     tails = pltpu.make_async_copy(rows.at[:, 96:112, :], outs[1], bsems[0].at[32])
     tails.start()
     ids, _ = tails_of(rows[:, 96:112, :])
-    member, slot, count = slots_of(ids, where[0])
-    parts = [jnp.zeros((SLOTS, LANES), F32)] * 3
+    _, slots = both_slots(ids, where[0])
+    parts = [jnp.zeros((2 * SLOTS, LANES), F32)] * 3
     for b in range(8):
-        pick = choice(member, slot, b)
+        pick = choice(slots, b)
         for c in range(3):
             block_rows = rows[4 * b : 4 * b + 4, 32 * c : 32 * c + 32, :].reshape(128, LANES)
             parts[c] = parts[c] + mm(pick, block_rows)
     for c in range(3):
         res[0][:, c * LANES : (c + 1) * LANES] = parts[c]
     send(res[0])
-    key = lax.broadcasted_iota(jnp.int32, (SLOTS, SLOTS), 1).astype(F32)
-    out = encode(res[0][...], key < count, w_qkv, w_out, w_up, w_down, HEADS, res[1:])
+    row = lax.broadcasted_iota(jnp.int32, (2 * SLOTS, 2 * SLOTS), 0)
+    key = lax.broadcasted_iota(jnp.int32, (2 * SLOTS, 2 * SLOTS), 1)
+    at = key.astype(F32)
+    allowed = ((row < SLOTS) & (at < slots[0][2])) | ((row >= SLOTS) & (key >= SLOTS) & (at < slots[1][2] + SLOTS))
+    out = encode(res[0][...], allowed, w_qkv, w_out, w_up, w_down, HEADS, res[1:])
     normed, _ = norm_parts(out)
-    usable = lax.broadcasted_iota(jnp.int32, (SLOTS, 1), 0).astype(F32) < count
-    total = jnp.sum(jnp.where(usable, normed, 0.0), axis=0, keepdims=True)
-    embed = (total / count).astype(BF16).astype(F32)
     message = block[0]
     message[...] = jnp.zeros((8, LANES), F32)
-    for c in range(3):
-        message[c : c + 1, :] = embed[:, c * LANES : (c + 1) * LANES]
+    for b, usable in enumerate(usable_of(slots)):
+        total = jnp.sum(jnp.where(usable, normed[b * SLOTS : (b + 1) * SLOTS], 0.0), axis=0, keepdims=True)
+        embed = (total / slots[b][2]).astype(BF16).astype(F32)
+        for c in range(3):
+            message[3 * b + c : 3 * b + c + 1, :] = embed[:, c * LANES : (c + 1) * LANES]
     broadcast_out(message, outs[0], bsems[0])
     tails.wait()
     for r in res:
@@ -343,55 +357,64 @@
 
 
 def region_backward(scaling, where, label, censor, *refs):
-    ins, outs, bufs, obufs, extra, sems, osems = cut(refs, 19, 15, 19, 15, 9, 1, 1)
+    ins, outs, bufs, obufs, extra, sems, osems = cut(refs, 19, 16, 19, 16, 10, 1, 1)
+    h = lax.rem(where[0] // 4, 2)
     order = list(range(8)) + [18, 13, 17, 16, 14, 15, 9, 8, 10, 11, 12]
     late = dict()
     for i in list(dict.fromkeys(order)):
         late[i] = Late(ins[i], bufs[i], sems[0].at[i])
-    early = [Early(r, b, osems[0].at[i]) for i, (r, b) in enumerate(zip(outs, obufs))]
+    early = []
+    for i, (r, b) in enumerate(zip(outs, obufs)):
+        part = pl.ds(pl.multiple_of(h * SLOTS, SLOTS), SLOTS) if 2 <= i < 10 else None
+        if i != 1:
+            early.append(Early(r, b, osems[0].at[i], part))
+        else:
+            early.append(b)
     message, tails = late[0], late[1]
     slide_weights = [late[i] for i in range(2, 8)]
     w_qkv, w_out, w_up, w_down = [late[i] for i in range(8, 12)]
     x_ref, res = late[12], [late[i] for i in range(13, 19)]
-    losses, spread, pairs, slide_grads = early[0], early[1], early[2:9], early[9:15]
-    packed_grad, slide_packed_grad, embeds = extra[:3]
+    losses, spread, pairs, slide_grads = early[0], early[1], early[2:10], early[10:16]
+    packed_grad, slide_packed_grad, embeds, placed = extra[:4]
     ids, slide_col = tails_of(tails[...])
     rows32 = lax.broadcasted_iota(jnp.int32, (32, 32), 0)
     columns32 = lax.broadcasted_iota(jnp.int32, (32, 32), 1)
     slide_row = jnp.sum(jnp.where(rows32 == columns32, slide_col, 0.0), axis=0, keepdims=True)
     arrived = message[...]
     at = lax.broadcasted_iota(jnp.int32, arrived.shape, 1)
-    for c in range(3):
-        part = jnp.sum(jnp.where(at == c, arrived, 0.0), axis=1)
-        embeds[:, c * LANES : (c + 1) * LANES] = part.astype(BF16)
+    for b in range(2):
+        for c in range(3):
+            part = jnp.sum(jnp.where(at == 3 * b + c, arrived, 0.0), axis=1)
+            for y in range(4):
+                placed[8 * y + 4 * b : 8 * y + 4 * b + 4, c * LANES : (c + 1) * LANES] = part[4 * y : 4 * y + 4]
+    embeds[...] = placed[...].astype(BF16)
     cots = slide_step(
-        embeds, slide_row, slide_col, label, censor, *slide_weights, losses, slide_grads, extra[3:9], slide_packed_grad, scaling
+        embeds, slide_row, slide_col, label, censor, *slide_weights, losses, slide_grads, extra[4:10], slide_packed_grad, scaling
     ).astype(F32)
     for g in [losses] + slide_grads:
         send(g)
-    mine = lax.broadcasted_iota(jnp.int32, (32, 1), 0) == where[0]
-    own = jnp.sum(jnp.where(mine, cots, 0.0), axis=0, keepdims=True)
-    member, slot, count = slots_of(ids, where[0])
-    usable = lax.broadcasted_iota(jnp.int32, (SLOTS, 1), 0).astype(F32) < count
-    grad = jnp.where(usable, own / count, 0.0)
+    first, slots = both_slots(ids, where[0])
+    grads = []
+    for b, usable in enumerate(usable_of(slots)):
+        mine = lax.broadcasted_iota(jnp.int32, (32, 1), 0) == first + 4 * b
+        own = jnp.sum(jnp.where(mine, cots, 0.0), axis=0, keepdims=True)
+        grads.append(jnp.where(usable, own / slots[b][2], 0.0))
+    grad = jnp.concatenate(grads, axis=0)
     normed, rstd = norm_parts(res[5][...])
     grad = norm_back(grad, normed, rstd)
 
     def put(i, a, b):
-        at = {3: 0, 2: 2, 1: 4, 0: 5}[i]
-        if i != 1:
-            pairs[at][...] = a
+        for at, value in ((6 - 2 * i, a), (7 - 2 * i, b)):
+            pairs[at][...] = value
             send(pairs[at])
-            at += 1
-        pairs[at][...] = b
-        send(pairs[at])
 
     grad = encode_back(grad, x_ref[...], w_qkv, w_out, w_up, w_down, HEADS, res, packed_grad, put).astype(BF16)
     for b in range(8):
-        spread[b * 128 : (b + 1) * 128, :] = mm_tn(choice(member, slot, b), grad).astype(BF16)
-    send(spread)
+        spread[b] = mm_tn(choice(slots, b), grad).astype(BF16)
+    leave([(spread.at[2 * y + h], outs[1].at[y]) for y in range(4)], sems[0])
     for e in early:
-        e.finish()
+        if e is not spread:
+            e.finish()
 
 
 def two_halves(flat, rows, core, halves, stage, sems, extra=None):
@@ -436,8 +459,9 @@
     columns32 = lax.broadcasted_iota(jnp.int32, (32, 32), 1)
     assign = jnp.sum(jnp.where(rows32 == columns32, ids[...].astype(F32), 0.0), axis=1, keepdims=True)
     cot = jnp.zeros((32, D), F32)
-    for r in range(32):
-        cot = cot + jnp.where(assign == float(r), arrived[r].astype(F32), 0.0)
+    for i in range(16):
+        region = float(i // 4 * 8 + i % 4)
+        cot = cot + jnp.where((assign == region) | (assign == region + 4.0), arrived[i].astype(F32), 0.0)
     cot = cot * 0.25
     grad = jnp.concatenate([cot] * PATCHES, axis=0)
     normed, rstd = norm_parts(res[5][...])
@@ -454,7 +478,7 @@
 
 def fold(rows, pad, tail, *refs):
     mine, got = refs[:2]
-    refs = refs[2:]
+    refs = refs[2 + tail :]
     if tail:
         out, extra = refs[:2]
         refs = refs[2:]
@@ -498,10 +522,6 @@
         copy.wait()
 
 
-def gate(source, unread, target):
-    pass
-
-
 def plane_sum(parts, out, buffer, total, sems):
     copies = [pltpu.make_async_copy(parts.at[:, i * 144 : (i + 1) * 144, :], buffer.at[:, i * 144 : (i + 1) * 144, :], sems.at[i]) for i in range(3)]
     for copy in copies:
@@ -592,7 +612,7 @@
     return lax.all_to_all(array, ALL, 0, 0, axis_index_groups=groups)
 
 
-def folded(mine, other, rows, pad, tail):
+def folded(mine, other, rows, pad, tail, after=()):
     got = lax.ppermute(other, "grp", OTHER_CORE)
     height = 128 * rows + 80 * tail
     chunk = 8 * rows + pad
@@ -604,7 +624,7 @@
         + [((128 * rows, LANES), F32), ((chunk, LANES), F32), ((16, chunk, LANES), BF16)]
         + [semaphores(2, 5), semaphores(17)]
         + [((80, LANES), BF16)] * tail,
-        (mine, got),
+        (mine, got) + after,
     )
 
 
@@ -648,12 +668,12 @@
     )
     both = jnp.concatenate([message, lax.ppermute(message, "dev", OTHER_PLANE)], axis=0)
     rows = exchange(jnp.broadcast_to(both[None], (16, 224, LANES)), PLANES)
-    region_res = [((SLOTS, D), F32)] + residuals(SLOTS, D, FF, HEADS)
+    region_res = [((2 * SLOTS, D), F32)] + residuals(2 * SLOTS, D, FF, HEADS)
     ins = (region_qkv, region_out, region_up, region_down)
     message, tails, *region_kept = call(
         region_forward,
         6 * US,
-        [((32, 8, LANES), F32), ((32, 16, LANES), BF16)] + region_res,
+        [((16, 8, LANES), F32), ((32, 16, LANES), BF16)] + region_res,
         like(ins)
         + [((32, 112, LANES), BF16)]
         + region_res
@@ -661,35 +681,29 @@
         (where, rows) + ins,
         scalars=1,
     )
-    all_regions = lax.all_to_all(message, "dev", 0, 0)
+    all_regions = exchange(message, PLANES)
     slide_weights = (slide_in, slide_qkv, slide_out, slide_up, slide_down, slide_head)
-    pairs = [
-        ((SLOTS, FF), BF16),
-        ((SLOTS, D), BF16),
-        ((SLOTS, D), BF16),
-        ((SLOTS, FF), BF16),
-        ((SLOTS, D), BF16),
-        ((SLOTS, D), BF16),
-        ((SLOTS, 3 * D), BF16),
-    ]
-    outs = [((SL_GRP, 1), F32), ((1024, D), BF16)] + pairs + like(slide_weights)
+    widths = (FF, D, D, FF, D, D, D, 3 * D)
+    pairs = [((SLOTS, n), BF16) for n in widths]
+    losses_out = [((SL_GRP, 1), F32)]
+    outs = losses_out + [((4, 128, D), BF16)] + pairs + like(slide_weights)
+    buffers = losses_out + [((8, 128, D), BF16)] + [((2 * SLOTS, n), BF16) for n in widths] + like(slide_weights)
     ins = (all_regions, tails) + slide_weights + (region_qkv, region_out, region_up, region_down) + tuple(region_kept)
     losses, spread, *rest = call(
         functools.partial(region_backward, scaling),
         12 * US,
         outs,
         like(ins)
-        + outs
-        + [((SLOTS, 3 * D), BF16), ((32, 3 * D_SL), BF16), ((32, D), BF16)]
+        + buffers
+        + [((2 * SLOTS, 3 * D), BF16), ((32, 3 * D_SL), BF16), ((32, D), BF16), ((32, D), F32)]
         + residuals(32, D_SL, D_SL, H_SL)
-        + [semaphores(19), semaphores(15)],
+        + [semaphores(19), semaphores(16)],
         (where, bin_label.reshape(SL_GRP, 1), censored.reshape(SL_GRP, 1)) + ins,
         scalars=1,
         whole=2,
     )
-    arrived = lax.all_to_all(spread.reshape(32, 32, D), "dev", 0, 0)
-    hidden, down_grad, second, up_grad, mid_grad, first, packed_grad = rest[:7]
-    ins = (hidden, down_grad, second, up_grad, region_kept[3], mid_grad, first, packed_grad)
+    arrived = exchange(spread.reshape(16, 32, D), PLANES)
+    ins = tuple(rest[:8])
     mine, other = call(
         region_weights,
         5 * US,
@@ -702,12 +716,12 @@
     region_parts = exchange(region_chunks, PLANES)
     (region_sums,) = call(
         plane_sum,
-        2 * US,
+        20 * US,
         [((432, LANES), F32)],
         like((region_parts,)) + [((432, LANES), F32), semaphores(3)],
         (region_parts,),
     )
-    slide_flat = jnp.concatenate([g.astype(F32).reshape(-1) for g in rest[7:]]).reshape(4, 2, 4, 2, 4, 1155)
+    slide_flat = jnp.concatenate([g.astype(F32).reshape(-1) for g in rest[8:]]).reshape(4, 2, 4, 2, 4, 1155)
     y, x = member_index // 8, lax.rem(member_index, 4)
     zero = jnp.zeros((), jnp.int32)
     slide_rows = lax.dynamic_slice(slide_flat, (zero, zero, y, zero, x, zero), (4, 2, 1, 2, 1, 1155))
@@ -724,14 +738,7 @@
         scalars=1,
         whole=1,
     )
-    other = pl.pallas_call(
-        gate,
-        out_shape=jax.ShapeDtypeStruct(other.shape, other.dtype),
-        in_specs=[pl.BlockSpec(memory_space=pl.ANY)] * 2,
-        out_specs=pl.BlockSpec(memory_space=pl.ANY),
-        input_output_aliases={0: 0},
-    )(other, region_parts)
-    tile_chunks, slide_sums = folded(mine, other, 63, 8, 1)
+    tile_chunks, slide_sums = folded(mine, other, 63, 8, 1, (region_sums,))
     tile_parts = exchange(tile_chunks, PLANES)
     ins = (tile_parts, region_sums, slide_sums)
     (last,) = call(

time: 209 us -> 190 us (0.909)
  waiting for transfers between devices: 78.7 us -> 31.1 us
  blocking collectives: 22 us -> 54.4 us
  starting transfers between devices: 32.1 us -> 28.8 us
  local copies, waits for them, and re-layouts: 15.3 us -> 12.6 us
    all_to_all x1 -> x2, blocking collectives: 22 us -> 54.4 us  [exchange(): return lax.all_to_all(array, ALL, 0, 0, axis_index_groups=groups)]
    all_to_all x3 -> x4, waiting for transfers between devices: 51.5 us -> 25.7 us  [exchange(): return lax.all_to_all(array, ALL, 0, 0, axis_index_groups=groups)]
    all_to_all x2 -> x0, waiting for transfers between devices: 17.5 us -> none  [the longest x1 9.66 us: body(): all_regions = lax.all_to_all(message, 'dev', 0, 0)]
    all_to_all x2 -> x0, starting transfers between devices: 12.5 us -> none  [the longest x1 8.24 us: body(): all_regions = lax.all_to_all(message, 'dev', 0, 0)]
    all_to_all x3 -> x4, starting transfers between devices: 13.2 us -> 22.3 us  [exchange(): return lax.all_to_all(array, ALL, 0, 0, axis_index_groups=groups)]
    ppermute x2, waiting for transfers between devices: 7.68 us -> 3.33 us  [folded(): got = lax.ppermute(other, 'grp', OTHER_CORE)]
    unnamed x37 -> x31, local copies, waits for them, and re-layouts: 7.12 us -> 3.51 us
  transfers between devices with their start and end apart: 8 -> 7, of which waited for: 8 -> 5; matrix products, arithmetic and copies ran while one was open for 4% -> 4% of each run, Pallas kernels for 11% -> 12%
where the time goes in v5:
time: 190 us; the launch traced here: 189 us
  Pallas kernels  58.3 us (31%)
  blocking collectives  54.4 us (29%)
  waiting for transfers between devices  31.1 us (16%)
  starting transfers between devices  28.8 us (15%)
  local copies, waits for them, and re-layouts  12.6 us (7%)
  other arithmetic  2.02 us (1%)
    pallas_call x9, Pallas kernels, call(): pl.pallas_call(kernel, out_shape=[jax.ShapeDtypeStruct(shape, kind) for s...  58.3 us
    all_to_all x2, blocking collectives, exchange(): return lax.all_to_all(array, ALL, 0, 0, axis_index_groups=groups)  54.4 us
    all_to_all x4, waiting for transfers between devices, exchange(): return lax.all_to_all(array, ALL, 0, 0, axis_index_groups=groups)  25.7 us
    all_to_all x4, starting transfers between devices, exchange(): return lax.all_to_all(array, ALL, 0, 0, axis_index_groups=groups)  22.3 us
    ppermute x1, starting transfers between devices, body(): lax.ppermute(message, 'dev', OTHER_PLANE)  6.37 us
  transfers between devices with their start and end apart: 7, of which 5 were waited for; matrix products, arithmetic and copies ran while one was open for 4% of the time, Pallas kernels for 12%

profile of v5, /device:TPU:32, one launch (start us, length us, event | category | flops | bytes accessed | tf_op | source)
XLA Modules:
  0.0 188.9 jit_solution(16843253282537678129)
XLA Ops:
  1.3 1.6 copy.35
  2.9 6.9 %shard_map.219 = (bf16[112,128]{1,0:T(8,128)(2,1)}, f32[128,384]{1,0:T(8,128)}, bf16[128,1152]{1,0:T(8,128)(2,1)}, f32[6,128,128]{2,1,0:T(8,128)}, bf16[128,384]...) custom-call(s32[1]{0:T(128)} %bitcast.where, s32[1,32]{1,0:T(1,128)} %ids.3, ...), custom_call_target="tpu_custom_call" | custom-call | flops 7699999744 | bytes 6516872 | tf_op jit(solution)/shard_map/pallas_call | solution.py:570
  9.8 6.4 %collective-permute-start = (bf16[112,128]{1,0:T(8,128)(2,1)}, bf16[112,128]{1,0:T(8,128)(2,1)S(1)}, u32[]{:S(2)}, u32[]{:S(2)}) collective-permute-start(bf16[112,128]{1,0:T(8,128)(2,1)} %get-tuple-element.43), channel_id=1, source_target_pairs={{0,4},{1,5},{2,6},{3,7},{4,0},{5,1},{6,2},{7,3},{8,12},{9,13},{10,... | collective-permute-start | bytes 86024 | tf_op jit(solution)/shard_map/ppermute | solution.py:669
  16.2 2.1 %collective-permute-done = bf16[112,128]{1,0:T(8,128)(2,1)S(1)} collective-permute-done((bf16[112,128]{1,0:T(8,128)(2,1)}, bf16[112,128]{1,0:T(8,128)(2,1)S(1)}, u32[]{:S(2)}, u32[]{:S(2)}) %collective-permute-start) | collective-permute-done | bytes 28704 | tf_op jit(solution)/shard_map/ppermute | solution.py:669
  18.2 0.8 pad_maximum_fusion
  19.0 0.1 broadcast_in_dim.2
  19.1 22.0 %all_to_all.30.refs_0_ = bf16[16,224,128]{2,1,0:T(8,128)(2,1)} all-to-all(bf16[16,224,128]{2,1,0:T(8,128)(2,1)S(1)} %broadcast_in_dim.2), channel_id=1, replica_groups={{0,1,2,3,8,9,10,11,16,17,18,19,24,25,26,27},{4,5,6,7,12,13,14,15,20,21,..., dimensions={0} | all-to-all | bytes 1835008 | tf_op jit(solution)/shard_map/all_to_all | solution.py:612
  41.1 0.0 copy-start.10
  41.1 0.0 copy-start.11
  41.1 0.0 copy-start.2
  41.1 8.1 %shard_map.220 = (f32[16,8,128]{2,1,0:T(8,128)}, bf16[32,16,128]{2,1,0:T(8,128)(2,1)}, f32[128,384]{1,0:T(8,128)}, bf16[128,1152]{1,0:T(8,128)(2,1)}, f32[6,128,...) custom-call(s32[1]{0:T(128)} %bitcast.where, ...), custom_call_target="tpu_custom_call" | custom-call | flops 6600000000 | bytes 6815748 | tf_op jit(solution)/shard_map/pallas_call | solution.py:570
  49.3 3.7 %all-to-all-start.1 = ((f32[16,8,128]{2,1,0:T(8,128)}), f32[16,8,128]{2,1,0:T(8,128)S(1)}, u32[]{:S(2)}, u32[]{:S(2)}) async-start(f32[16,8,128]{2,1,0:T(8,128)} %get-tuple-element.44), calls=%async_computation.1 | async-start | bytes 131072 | tf_op jit(solution)/shard_map/all_to_all | solution.py:612
  53.0 0.0 copy-done.10
  53.0 0.7 copy.36.label
  53.7 0.0 copy-done.11
  53.7 0.7 copy.37.censor
  54.3 0.0 copy-done.2
  54.3 0.8 copy.38.refs_2_
  55.2 0.0 copy-done.8
  55.2 0.7 copy.39.refs_7_
  55.9 4.5 %all-to-all-done.1.refs_0_ = f32[16,8,128]{2,1,0:T(8,128)S(1)} async-done(((f32[16,8,128]{2,1,0:T(8,128)}), f32[16,8,128]{2,1,0:T(8,128)S(1)}, u32[]{:S(2)}, u32[]{:S(2)}) %all-to-all-start.1) | async-done | bytes 65568 | tf_op jit(solution)/shard_map/all_to_all | solution.py:612
  60.4 0.6 copy-done.6
  61.0 13.2 %shard_map.221 = (f32[4,1]{1,0:T(4,128)}, bf16[4,128,384]{2,1,0:T(8,128)(2,1)}, bf16[64,1536]{1,0:T(8,128)(2,1)}, bf16[64,384]{1,0:T(8,128)(2,1)}, bf16[64,384]{...) custom-call(s32[1]{0:T(128)} %bitcast.where, ...), custom_call_target="tpu_custom_call" | custom-call | flops 13200000000 | bytes 8260660 | tf_op jit(solution)/shard_map/pallas_call | solution.py:570
  74.2 3.6 %all-to-all-start.2 = ((bf16[16,32,384]{2,1,0:T(8,128)(2,1)}), bf16[16,32,384]{2,1,0:T(8,128)(2,1)S(1)}, u32[]{:S(2)}, u32[]{:S(2)}) async-start(bf16[16,32,384]{2,1,0:T(8,128)(2,1)} %bitcast.20), calls=%async_computation.2 | async-start | bytes 786432 | tf_op jit(solution)/shard_map/all_to_all | solution.py:612
  77.8 1.2 reshape.83
  79.0 1.2 reshape.84
  80.2 0.0 copy-start.4
  80.3 0.0 copy-start.3
  80.3 0.0 copy-start.7
  80.3 4.9 %shard_map.222 = (bf16[6912,128]{1,0:T(8,128)(2,1)}, bf16[6912,128]{1,0:T(8,128)(2,1)}) custom-call(s32[1]{0:T(128)} %bitcast.5.core, bf16[64,1536]{1,0:T(8,128)(2,1)} %get-tuple-element.68.refs_0_, bf16[64,384]{1,0:T(8,128)(2,1)} %get-tuple-element.69.refs_1_, bf16[64,384]{1,0:T(8,128)(2,1)} %get-tuple-element.70.refs_2_, ...), custom_call_target="tpu_custom_call" | custom-call | flops 5500000256 | bytes 4325380 | tf_op jit(solution)/shard_map/pallas_call | solution.py:570
  85.2 0.1 collective-permute-start.1
  85.4 0.0 copy-done.5
  85.4 0.2 reshape.85
  85.5 0.0 copy-done.4
  85.5 0.2 reshape.86
  85.7 0.0 copy-done.3
  85.7 0.2 reshape.87
  85.8 0.0 copy-done.7
  85.9 0.1 reshape.88
  86.0 3.3 %collective-permute-done.1.refs_1_ = bf16[6912,128]{1,0:T(8,128)(2,1)} collective-permute-done((bf16[6912,128]{1,0:T(8,128)(2,1)}, bf16[6912,128]{1,0:T(8,128)(2,1)}, u32[]{:S(2)}, u32[]{:S(2)}) %collective-permute-start.1) | collective-permute-done | bytes 1769504 | tf_op jit(solution)/shard_map/ppermute | solution.py:616
  89.4 3.6 %shard_map.223.refs_14_ = bf16[16,432,128]{2,1,0:T(8,128)(2,1)} custom-call(bf16[6912,128]{1,0:T(8,128)(2,1)} %get-tuple-element.76.refs_0_, bf16[6912,128]{1,0:T(8,128)(2,1)} %collective-permute-done.1.refs_1_), custom_call_target="tpu_custom_call" | custom-call | flops 4400000000 | bytes 5308416 | tf_op jit(solution)/shard_map/pallas_call | solution.py:570
  93.0 0.0 all-to-all-done.2.refs_0_
  93.0 0.0 copy-start.1
  93.0 7.2 %all-to-all-start.3 = ((bf16[16,432,128]{2,1,0:T(8,128)(2,1)}), bf16[16,432,128]{2,1,0:T(8,128)(2,1)S(1)}, u32[]{:S(2)}, u32[]{:S(2)}) async-start(bf16[16,432,128]{2,1,0:T(8,128)(2,1)} %shard_map.223.refs_14_), calls=%async_computation.3 | async-start | bytes 3538944 | tf_op jit(solution)/shard_map/all_to_all | solution.py:612
  100.2 0.0 copy-done.1
  100.2 0.9 reshape.97
  101.2 0.1 dynamic-slice_convert_fusion
  101.4 0.6 reshape.92.refs_2_
  102.0 12.8 %shard_map.224 = (bf16[8144,128]{1,0:T(8,128)(2,1)}, bf16[8144,128]{1,0:T(8,128)(2,1)}) custom-call(s32[1]{0:T(128)} %bitcast.5.core, s32[1,32]{1,0:T(1,128)} %ids.3, bf16[16,32,384]{2,1,0:T(8,128)(2,1)} %copy-done.1, bf16[128,768]{1,0:T(8,128)(2,1)} %bitcast.23, bf16[2,80,128]{2,1,0:T(8,128)(2,1)} %reshape.92.refs_2_, bf16[384,1152]{1,0:T(8,128)(2,1)} %refs_3_.7, ...), custom_call_target="tpu_custom_call" | custom-call | flops 14300000256 | bytes 12271748 | tf_op jit(solution)/shard_map/pallas_call | solution.py:570
  114.8 0.1 collective-permute-start.2
  114.9 13.2 %all-to-all-done.3.parts = bf16[16,432,128]{2,1,0:T(8,128)(2,1)S(1)} async-done(((bf16[16,432,128]{2,1,0:T(8,128)(2,1)}), bf16[16,432,128]{2,1,0:T(8,128)(2,1)S(1)}, u32[]{:S(2)}, u32[]{:S(2)}) %all-to-all-start.3) | async-done | bytes 1769504 | tf_op jit(solution)/shard_map/all_to_all | solution.py:612
  128.1 1.2 copy-done
  129.3 2.2 %shard_map.225.refs_2_.region_in = f32[432,128]{1,0:T(8,128)} custom-call(bf16[16,432,128]{2,1,0:T(8,128)(2,1)} %copy-done), custom_call_target="tpu_custom_call" | custom-call | flops 22000001024 | bytes 1990656 | tf_op jit(solution)/shard_map/pallas_call | solution.py:570
  131.6 0.0 collective-permute-done.2.refs_1_
  131.6 3.8 %shard_map.226 = (bf16[16,512,128]{2,1,0:T(8,128)(2,1)}, bf16[80,128]{1,0:T(8,128)(2,1)}) custom-call(bf16[8144,128]{1,0:T(8,128)(2,1)} %get-tuple-element.78.refs_0_, bf16[8144,128]{1,0:T(8,128)(2,1)} %collective-permute-done.2.refs_1_, f32[432,128]{1,0:T(8,128)} %shard_map.225.refs_2_.region_in), custom_call_target="tpu_custom_call" | custom-call | flops 4400000000 | bytes 6508544 | tf_op jit(solution)/shard_map/pallas_call | solution.py:570
  135.4 32.4 %all_to_all.31.tile_in = bf16[16,512,128]{2,1,0:T(8,128)(2,1)} all-to-all(bf16[16,512,128]{2,1,0:T(8,128)(2,1)} %get-tuple-element.80), channel_id=1, replica_groups={{0,1,2,3,8,9,10,11,16,17,18,19,24,25,26,27},{4,5,6,7,12,13,14,15,20,21,..., dimensions={0} | all-to-all | bytes 4194304 | tf_op jit(solution)/shard_map/all_to_all | solution.py:612
  167.8 2.7 %shard_map.227 = bf16[8,128,128]{2,1,0:T(8,128)(2,1)} custom-call(bf16[16,512,128]{2,1,0:T(8,128)(2,1)} %all_to_all.31.tile_in, f32[432,128]{1,0:T(8,128)} %shard_map.225.refs_2_.region_in, bf16[80,128]{1,0:T(8,128)(2,1)} %get-tuple-element.81.slide_in), custom_call_target="tpu_custom_call" | custom-call | flops 3300000000 | bytes 2600960 | tf_op jit(solution)/shard_map/pallas_call | solution.py:570
  170.5 7.9 %all-to-all-start.5 = ((bf16[8,128,128]{2,1,0:T(8,128)(2,1)}), bf16[8,128,128]{2,1,0:T(8,128)(2,1)S(1)}, u32[]{:S(2)}, u32[]{:S(2)}) async-start(bf16[8,128,128]{2,1,0:T(8,128)(2,1)} %shard_map.227), calls=%async_computation.5 | async-start | bytes 524288 | tf_op jit(solution)/shard_map/all_to_all | solution.py:612
  178.3 0.0 copy-done.9
  178.3 0.6 reduce
  178.9 8.0 %all-to-all-done.5 = bf16[8,128,128]{2,1,0:T(8,128)(2,1)S(1)} async-done(((bf16[8,128,128]{2,1,0:T(8,128)(2,1)}), bf16[8,128,128]{2,1,0:T(8,128)(2,1)S(1)}, u32[]{:S(2)}, u32[]{:S(2)}) %all-to-all-start.5) | async-done | bytes 262176 | tf_op jit(solution)/shard_map/all_to_all | solution.py:612
  187.0 0.6 slice_bitcast_fusion
  187.6 0.6 slice_bitcast_fusion.1
  188.3 0.6 slice_multiply_fusion
  (15 shorter events, 0.2 us)
Async XLA Ops:
  9.8 8.4 %collective-permute-start = (bf16[112,128]{1,0:T(8,128)(2,1)}, bf16[112,128]{1,0:T(8,128)(2,1)S(1)}, u32[]{:S(2)}, u32[]{:S(2)}) collective-permute-start(bf16[112,128]{1,0:T(8,128)(2,1)} %get-tuple-element.43), channel_id=1, source_target_pairs={{0,4},{1,5},{2,6},{3,7},{4,0},{5,1},{6,2},{7,3},{8,12},{9,13},{10,... | collective-permute-start | bytes 86024 | tf_op jit(solution)/shard_map/ppermute | solution.py:669
  41.1 11.9 %copy-start.10 = (s32[1,4]{1,0:T(1,128)S(1)}, s32[1,4]{1,0:T(1,128)}, u32[]{:S(2)}) copy-start(s32[1,4]{1,0:T(1,128)} %param.23) | copy-start | bytes 52
  41.1 12.6 %copy-start.11 = (s32[1,4]{1,0:T(1,128)S(1)}, s32[1,4]{1,0:T(1,128)}, u32[]{:S(2)}) copy-start(s32[1,4]{1,0:T(1,128)} %param.24) | copy-start | bytes 52
  41.1 13.2 %copy-start.2 = (bf16[384,192]{0,1:T(8,128)(2,1)S(1)}, bf16[384,192]{0,1:T(8,128)(2,1)}, u32[]{:S(2)}) copy-start(bf16[384,192]{0,1:T(8,128)(2,1)} %param.34) | copy-start | bytes 442372
  41.1 14.1 %copy-start.8 = (bf16[192,4]{0,1:T(4,128)(2,1)S(1)}, bf16[192,4]{0,1:T(4,128)(2,1)}, u32[]{:S(2)}) copy-start(bf16[192,4]{0,1:T(4,128)(2,1)} %param.39) | copy-start | bytes 4612
  49.3 11.1 %all-to-all-start.1 = ((f32[16,8,128]{2,1,0:T(8,128)}), f32[16,8,128]{2,1,0:T(8,128)S(1)}, u32[]{:S(2)}, u32[]{:S(2)}) async-start(f32[16,8,128]{2,1,0:T(8,128)} %get-tuple-element.44), calls=%async_computation.1 | async-start | bytes 131072 | tf_op jit(solution)/shard_map/all_to_all | solution.py:612
  60.4 0.6 copy-start.6
  74.2 18.8 %all-to-all-start.2 = ((bf16[16,32,384]{2,1,0:T(8,128)(2,1)}), bf16[16,32,384]{2,1,0:T(8,128)(2,1)S(1)}, u32[]{:S(2)}, u32[]{:S(2)}) async-start(bf16[16,32,384]{2,1,0:T(8,128)(2,1)} %bitcast.20), calls=%async_computation.2 | async-start | bytes 786432 | tf_op jit(solution)/shard_map/all_to_all | solution.py:612
  80.2 5.1 %copy-start.5 = (bf16[192,192]{1,0:T(8,128)(2,1)S(1)}, bf16[192,192]{1,0:T(8,128)(2,1)}, u32[]{:S(2)}) copy-start(bf16[192,192]{1,0:T(8,128)(2,1)} %get-tuple-element.57) | copy-start | bytes 221188
  80.2 5.3 %copy-start.4 = (bf16[192,192]{1,0:T(8,128)(2,1)S(1)}, bf16[192,192]{1,0:T(8,128)(2,1)}, u32[]{:S(2)}) copy-start(bf16[192,192]{1,0:T(8,128)(2,1)} %get-tuple-element.58) | copy-start | bytes 221188
  80.3 5.4 %copy-start.3 = (bf16[192,192]{1,0:T(8,128)(2,1)S(1)}, bf16[192,192]{1,0:T(8,128)(2,1)}, u32[]{:S(2)}) copy-start(bf16[192,192]{1,0:T(8,128)(2,1)} %get-tuple-element.59) | copy-start | bytes 221188
  80.3 5.6 %copy-start.7 = (bf16[192,4]{1,0:T(8,128)(2,1)S(1)}, bf16[192,4]{1,0:T(8,128)(2,1)}, u32[]{:S(2)}) copy-start(bf16[192,4]{1,0:T(8,128)(2,1)} %get-tuple-element.60) | copy-start | bytes 4612
  85.2 4.1 %collective-permute-start.1 = (bf16[6912,128]{1,0:T(8,128)(2,1)}, bf16[6912,128]{1,0:T(8,128)(2,1)}, u32[]{:S(2)}, u32[]{:S(2)}) collective-permute-start(bf16[6912,128]{1,0:T(8,128)(2,1)} %get-tuple-element.77), channel_id=1, source_target_pairs={{0,32},{32,0},{64,96},{96,64},{128,160},{160,128},{192,224},{224,1... | collective-permute-start | bytes 5308424 | tf_op jit(solution)/shard_map/ppermute | solution.py:616
  93.0 7.2 %copy-start.1 = (bf16[16,32,384]{2,1,0:T(8,128)(2,1)}, bf16[16,32,384]{2,1,0:T(8,128)(2,1)S(1)}, u32[]{:S(2)}) copy-start(bf16[16,32,384]{2,1,0:T(8,128)(2,1)S(1)} %all-to-all-done.2.refs_0_) | copy-start | bytes 1179652
  93.0 35.1 %all-to-all-start.3 = ((bf16[16,432,128]{2,1,0:T(8,128)(2,1)}), bf16[16,432,128]{2,1,0:T(8,128)(2,1)S(1)}, u32[]{:S(2)}, u32[]{:S(2)}) async-start(bf16[16,432,128]{2,1,0:T(8,128)(2,1)} %shard_map.223.refs_14_), calls=%async_computation.3 | async-start | bytes 3538944 | tf_op jit(solution)/shard_map/all_to_all | solution.py:612
  114.8 16.8 %collective-permute-start.2 = (bf16[8144,128]{1,0:T(8,128)(2,1)}, bf16[8144,128]{1,0:T(8,128)(2,1)}, u32[]{:S(2)}, u32[]{:S(2)}) collective-permute-start(bf16[8144,128]{1,0:T(8,128)(2,1)} %get-tuple-element.79), channel_id=1, source_target_pairs={{0,32},{32,0},{64,96},{96,64},{128,160},{160,128},{192,224},{224,1... | collective-permute-start | bytes 6254600 | tf_op jit(solution)/shard_map/ppermute | solution.py:616
  128.1 1.2 copy-start
  167.8 10.6 %copy-start.9 = (f32[4,1]{1,0:T(4,128)S(1)}, f32[4,1]{1,0:T(4,128)}, u32[]{:S(2)}) copy-start(f32[4,1]{1,0:T(4,128)} %get-tuple-element.53) | copy-start | bytes 52
  170.5 16.5 %all-to-all-start.5 = ((bf16[8,128,128]{2,1,0:T(8,128)(2,1)}), bf16[8,128,128]{2,1,0:T(8,128)(2,1)S(1)}, u32[]{:S(2)}, u32[]{:S(2)}) async-start(bf16[8,128,128]{2,1,0:T(8,128)(2,1)} %shard_map.227), calls=%async_computation.5 | async-start | bytes 524288 | tf_op jit(solution)/shard_map/all_to_all | solution.py:612

commit v6 on v5

--- a/solution.py
+++ b/solution.py
@@ -155,8 +155,8 @@
 
 
 class Early:
-    def __init__(self, target, buffer, sem, part=None):
-        self.copy = pltpu.make_async_copy(buffer if part is None else buffer.at[part], target, sem)
+    def __init__(self, target, buffer, sem):
+        self.copy = pltpu.make_async_copy(buffer, target, sem)
         self.buffer = buffer
 
     def __getitem__(self, index):
@@ -365,11 +365,7 @@
         late[i] = Late(ins[i], bufs[i], sems[0].at[i])
     early = []
     for i, (r, b) in enumerate(zip(outs, obufs)):
-        part = pl.ds(pl.multiple_of(h * SLOTS, SLOTS), SLOTS) if 2 <= i < 10 else None
-        if i != 1:
-            early.append(Early(r, b, osems[0].at[i], part))
-        else:
-            early.append(b)
+        early.append(Early(r, b, osems[0].at[i]) if i != 1 else b)
     message, tails = late[0], late[1]
     slide_weights = [late[i] for i in range(2, 8)]
     w_qkv, w_out, w_up, w_down = [late[i] for i in range(8, 12)]
@@ -417,35 +413,42 @@
             e.finish()
 
 
-def two_halves(flat, rows, core, halves, stage, sems, extra=None):
-    run = 32 * rows
+def two_halves(flat, runs, core, halves, stage, sems):
+    run = 32 * 63
     copies = []
     for side in range(2):
         which = core if side == 0 else 1 - core
-        for z in range(4):
+        for z in runs:
             start = pl.multiple_of((2 * z + which) * run, 32)
             stage[side, z * run : (z + 1) * run, :] = flat[pl.ds(start, run), :].astype(BF16)
             part = pl.ds(z * run, run)
             copies.append(pltpu.make_async_copy(stage.at[side, part, :], halves[side].at[part, :], sems.at[side, z]))
             copies[-1].start()
-        if extra is not None:
-            stage[side, 4 * run : 4 * run + 80, :] = extra.ref()[which]
-            part = pl.ds(4 * run, 80)
-            copies.append(pltpu.make_async_copy(stage.at[side, part, :], halves[side].at[part, :], sems.at[side, 4]))
-            copies[-1].start()
-    for copy in copies:
-        copy.wait()
-
-
-def region_weights(core, *refs):
-    ins, halves, bufs, flat, stage, sems, osems = cut(refs, 8, 2, 8, 1, 1, 1, 1)
+    return copies
+
+
+def region_weights(core, where, *refs):
+    ins, halves, bufs, flat, run_buf, stage, sems, osems = cut(refs, 8, 2, 8, 1, 1, 1, 1, 1)
     late = [Late(r, b, sems[0].at[i]) for i, (r, b) in enumerate(zip(ins, bufs))]
     hidden, grad, second, up_grad, mixture, mid_grad, first, packed_grad = late
     put_rows(flat[0], 9216, hidden[...], grad[...])
     put_rows(flat[0], 4608, second[...], up_grad[...])
     put_rows(flat[0], 3456, mixture[...], mid_grad[...])
     put_rows(flat[0], 0, first[...], packed_grad[...])
-    two_halves(flat[0], 54, core[0], halves, stage[0], osems[0])
+    h = lax.rem(where[0] // 4, 2)
+    copies = []
+    for side in range(2):
+        which = core[0] if side == 0 else 1 - core[0]
+        for z in range(4):
+            for y in range(4):
+                start = pl.multiple_of((2 * z + which) * 1728 + y * 432 + h * 216, 8)
+                run_buf[0][y * 216 : (y + 1) * 216, :] = flat[0][pl.ds(start, 216), :]
+            part = pl.ds(z * 864, 864)
+            stage[0][side, z * 864 : (z + 1) * 864, :] = run_buf[0][...].astype(BF16)
+            copies.append(pltpu.make_async_copy(stage[0].at[side, part, :], halves[side].at[part, :], osems[0].at[side, z]))
+            copies[-1].start()
+    for copy in copies:
+        copy.wait()
 
 
 def tile_backward(core, ids, *refs):
@@ -468,12 +471,24 @@
     grad = norm_back(grad, normed, rstd)
     bases = (2304, 5760, 6912, 11520)
 
+    leaving = []
+
     def put(i, a, b):
         put_rows(flat[0], bases[i], a, b)
+        if i == 2:
+            leaving.extend(two_halves(flat[0], (2, 3), core[0], halves, stage[0], osems[0]))
 
     grad = encode_back(grad, x_ref[...], w_qkv, w_out, w_up, w_down, HEADS, res, packed_grad[0], put)
+    for side in range(2):
+        which = core[0] if side == 0 else 1 - core[0]
+        stage[0][side, 8064:8144, :] = slide_rows.ref()[which]
+        part = pl.ds(8064, 80)
+        leaving.append(pltpu.make_async_copy(stage[0].at[side, part, :], halves[side].at[part, :], osems[0].at[side, 4]))
+        leaving[-1].start()
     put_rows(flat[0], 0, patches[...], grad.astype(BF16))
-    two_halves(flat[0], 63, core[0], halves, stage[0], osems[0], slide_rows)
+    leaving.extend(two_halves(flat[0], (0, 1), core[0], halves, stage[0], osems[0]))
+    for copy in leaving:
+        copy.wait()
 
 
 def fold(rows, pad, tail, *refs):
@@ -486,7 +501,8 @@
         out = refs[0]
         refs = refs[1:]
     a, b, total, stage, chunks, sems, osems = refs[:7]
-    run = 32 * rows
+    planes = 2 if tail else 1
+    run = 16 * planes * rows
     arriving = []
     for z in range(4 + tail):
         part = pl.ds(z * run, run if z < 4 else 80)
@@ -507,13 +523,13 @@
         leaving.append(pltpu.make_async_copy(refs[7], extra, osems.at[16]))
         leaving[-1].start()
     if pad:
-        stage[8 * rows :, :] = jnp.zeros((pad, LANES), F32)
+        stage[4 * planes * rows :, :] = jnp.zeros((pad, LANES), F32)
     for y in range(4):
         for x in range(4):
             for z in range(4):
-                for h in range(2):
-                    source = (z * 32 + y * 8 + h * 4 + x) * rows
-                    target = (z * 2 + h) * rows
+                for h in range(planes):
+                    source = (z * 16 * planes + y * 4 * planes + h * 4 + x) * rows
+                    target = (z * planes + h) * rows
                     stage[target : target + rows, :] = total[source : source + rows, :]
             chunks[y * 4 + x] = stage[...].astype(BF16)
             leaving.append(pltpu.make_async_copy(chunks.at[y * 4 + x], out.at[y * 4 + x], osems.at[y * 4 + x]))
@@ -523,20 +539,22 @@
 
 
 def plane_sum(parts, out, buffer, total, sems):
-    copies = [pltpu.make_async_copy(parts.at[:, i * 144 : (i + 1) * 144, :], buffer.at[:, i * 144 : (i + 1) * 144, :], sems.at[i]) for i in range(3)]
-    for copy in copies:
-        copy.start()
-    for i in range(3):
+    copies = []
+    for i in range(2):
+        part = pl.ds(i * 112, 112)
+        copies.append(pltpu.make_async_copy(parts.at[:, part, :], buffer.at[:, part, :], sems.at[i]))
+        copies[-1].start()
+    for i in range(2):
         copies[i].wait()
-        for start in range(i * 144, (i + 1) * 144, 48):
-            value = buffer[0, start : start + 48, :].astype(F32)
-            for j in range(1, 16):
-                value = value + buffer[j, start : start + 48, :].astype(F32)
-            total[start : start + 48, :] = value
+        rows = slice(i * 112, (i + 1) * 112)
+        value = buffer[0, rows, :].astype(F32)
+        for j in range(1, 16):
+            value = value + buffer[j, rows, :].astype(F32)
+        total[rows, :] = value
     leave([(total, out)], sems)
 
 
-def merge(tile_in, region_in, slide_in, out, tile_buf, region_buf, slide_buf, total, slide_total, stage, chunks, sems, osems):
+def merge(where, tile_in, region_in, slide_in, out, tile_buf, region_buf, slide_buf, total, slide_total, stage, chunks, sems, osems):
     tile_late = Late(tile_in, tile_buf, sems.at[0])
     region_late = Late(region_in, region_buf, sems.at[1])
     slide_late = Late(slide_in, slide_buf, sems.at[2])
@@ -548,11 +566,13 @@
             value = value + tile_late[i, start : start + 64, :].astype(F32)
         total[start : start + 64, :] = value
     region_total = region_late.ref()
+    h = lax.rem(where[0] // 4, 2)
     leaving = []
     for i in range(8):
         stage[0:63, :] = total[i * 63 : (i + 1) * 63, :]
         stage[63:64, :] = jnp.zeros((1, LANES), F32)
-        stage[64:118, :] = region_total[i * 54 : (i + 1) * 54, :]
+        rows = region_total[i // 2 * 54 : (i // 2 + 1) * 54, :]
+        stage[64:118, :] = jnp.where(h == i % 2, rows, 0.0)
         stage[118:128, :] = slide_total[i * 10 : (i + 1) * 10, :]
         chunks[i] = stage[...].astype(BF16)
         leaving.append(pltpu.make_async_copy(chunks.at[i], out.at[i], osems.at[i]))
@@ -614,14 +634,15 @@
 
 def folded(mine, other, rows, pad, tail, after=()):
     got = lax.ppermute(other, "grp", OTHER_CORE)
-    height = 128 * rows + 80 * tail
-    chunk = 8 * rows + pad
+    planes = 1 + tail
+    height = 64 * planes * rows + 80 * tail
+    chunk = 4 * planes * rows + pad
     return call(
         functools.partial(fold, rows, pad, tail),
         4 * US,
         [((16, chunk, LANES), BF16)] + [((80, LANES), BF16)] * tail,
         [((height, LANES), BF16)] * 2
-        + [((128 * rows, LANES), F32), ((chunk, LANES), F32), ((16, chunk, LANES), BF16)]
+        + [((64 * planes * rows, LANES), F32), ((chunk, LANES), F32), ((16, chunk, LANES), BF16)]
         + [semaphores(2, 5), semaphores(17)]
         + [((80, LANES), BF16)] * tail,
         (mine, got) + after,
@@ -684,10 +705,10 @@
     all_regions = exchange(message, PLANES)
     slide_weights = (slide_in, slide_qkv, slide_out, slide_up, slide_down, slide_head)
     widths = (FF, D, D, FF, D, D, D, 3 * D)
-    pairs = [((SLOTS, n), BF16) for n in widths]
+    pairs = [((2 * SLOTS, n), BF16) for n in widths]
     losses_out = [((SL_GRP, 1), F32)]
     outs = losses_out + [((4, 128, D), BF16)] + pairs + like(slide_weights)
-    buffers = losses_out + [((8, 128, D), BF16)] + [((2 * SLOTS, n), BF16) for n in widths] + like(slide_weights)
+    buffers = losses_out + [((8, 128, D), BF16)] + pairs + like(slide_weights)
     ins = (all_regions, tails) + slide_weights + (region_qkv, region_out, region_up, region_down) + tuple(region_kept)
     losses, spread, *rest = call(
         functools.partial(region_backward, scaling),
@@ -707,18 +728,19 @@
     mine, other = call(
         region_weights,
         5 * US,
-        [((6912, LANES), BF16)] * 2,
-        like(ins) + [((13824, LANES), F32), ((2, 6912, LANES), BF16), semaphores(8), semaphores(2, 5)],
-        (core,) + ins,
-        scalars=1,
-    )
-    (region_chunks,) = folded(mine, other, 54, 0, 0)
+        [((3456, LANES), BF16)] * 2,
+        like(ins)
+        + [((13824, LANES), F32), ((864, LANES), F32), ((2, 3456, LANES), BF16), semaphores(8), semaphores(2, 4)],
+        (core, where) + ins,
+        scalars=2,
+    )
+    (region_chunks,) = folded(mine, other, 54, 8, 0)
     region_parts = exchange(region_chunks, PLANES)
     (region_sums,) = call(
         plane_sum,
         20 * US,
-        [((432, LANES), F32)],
-        like((region_parts,)) + [((432, LANES), F32), semaphores(3)],
+        [((224, LANES), F32)],
+        like((region_parts,)) + [((224, LANES), F32), semaphores(2)],
         (region_parts,),
     )
     slide_flat = jnp.concatenate([g.astype(F32).reshape(-1) for g in rest[8:]]).reshape(4, 2, 4, 2, 4, 1155)
@@ -748,7 +770,8 @@
         like(ins)
         + [((512, LANES), F32), ((80, LANES), F32), ((128, LANES), F32), ((8, 128, LANES), BF16)]
         + [semaphores(3), semaphores(8)],
-        ins,
+        (where,) + ins,
+        scalars=1,
     )
     total = jnp.sum(exchange(last, COLUMNS).astype(F32), axis=0)
     tile_result = total[0:63].reshape(8064)

time: 190 us -> 180 us (0.947)
  waiting for transfers between devices: 31.1 us -> 19.4 us
  local copies, waits for them, and re-layouts: 12.6 us -> 15.5 us
  Pallas kernels: 58.3 us -> 56.1 us
    all_to_all x4, waiting for transfers between devices: 25.7 us -> 16.6 us  [exchange(): return lax.all_to_all(array, ALL, 0, 0, axis_index_groups=groups)]
    ppermute x2, waiting for transfers between devices: 3.33 us -> 0.75 us  [folded(): got = lax.ppermute(other, 'grp', OTHER_CORE)]
    pallas_call x9, Pallas kernels: 58.3 us -> 56.1 us  [call(): pl.pallas_call(kernel, out_shape=[jax.ShapeDtypeStruct(shape, kind) for s...]
    unnamed x31 -> x33, local copies, waits for them, and re-layouts: 3.51 us -> 5.5 us
  transfers between devices with their start and end apart: 7 -> 7, of which waited for: 5 -> 5; matrix products, arithmetic and copies ran while one was open for 4% -> 5% of each run, Pallas kernels for 12% -> 12%
where the time goes in v6:
time: 180 us; the launch traced here: 179 us
  Pallas kernels  56.1 us (31%)
  blocking collectives  55.8 us (31%)
  starting transfers between devices  29 us (16%)
  waiting for transfers between devices  19.4 us (11%)
  local copies, waits for them, and re-layouts  15.5 us (9%)
  other arithmetic  2.02 us (1%)
    pallas_call x9, Pallas kernels, call(): pl.pallas_call(kernel, out_shape=[jax.ShapeDtypeStruct(shape, kind) for s...  56.1 us
    all_to_all x2, blocking collectives, exchange(): return lax.all_to_all(array, ALL, 0, 0, axis_index_groups=groups)  55.8 us
    all_to_all x4, starting transfers between devices, exchange(): return lax.all_to_all(array, ALL, 0, 0, axis_index_groups=groups)  22.4 us
    all_to_all x4, waiting for transfers between devices, exchange(): return lax.all_to_all(array, ALL, 0, 0, axis_index_groups=groups)  16.6 us
    ppermute x1, starting transfers between devices, body(): lax.ppermute(message, 'dev', OTHER_PLANE)  6.38 us
    unnamed x33, local copies, waits for them, and re-layouts  5.5 us
    reshape x6, local copies, waits for them, and re-layouts, body(): g.astype(F32).reshape(-1)  3.89 us
  transfers between devices with their start and end apart: 7, of which 5 were waited for; matrix products, arithmetic and copies ran while one was open for 5% of the time, Pallas kernels for 12%

profile of v6, /device:TPU:32, one launch (start us, length us, event | category | flops | bytes accessed | tf_op | source)
XLA Modules:
  0.0 179.3 jit_solution(15042540392603831079)
XLA Ops:
  1.3 1.6 copy.35
  2.9 6.9 %shard_map.219 = (bf16[112,128]{1,0:T(8,128)(2,1)}, f32[128,384]{1,0:T(8,128)}, bf16[128,1152]{1,0:T(8,128)(2,1)}, f32[6,128,128]{2,1,0:T(8,128)}, bf16[128,384]...) custom-call(s32[1]{0:T(128)} %bitcast.where, s32[1,32]{1,0:T(1,128)} %ids.3, ...), custom_call_target="tpu_custom_call" | custom-call | flops 7699999744 | bytes 6516872 | tf_op jit(solution)/shard_map/pallas_call | solution.py:590
  9.8 6.4 %collective-permute-start = (bf16[112,128]{1,0:T(8,128)(2,1)}, bf16[112,128]{1,0:T(8,128)(2,1)S(1)}, u32[]{:S(2)}, u32[]{:S(2)}) collective-permute-start(bf16[112,128]{1,0:T(8,128)(2,1)} %get-tuple-element.43), channel_id=1, source_target_pairs={{0,4},{1,5},{2,6},{3,7},{4,0},{5,1},{6,2},{7,3},{8,12},{9,13},{10,... | collective-permute-start | bytes 86024 | tf_op jit(solution)/shard_map/ppermute | solution.py:690
  16.2 2.1 %collective-permute-done = bf16[112,128]{1,0:T(8,128)(2,1)S(1)} collective-permute-done((bf16[112,128]{1,0:T(8,128)(2,1)}, bf16[112,128]{1,0:T(8,128)(2,1)S(1)}, u32[]{:S(2)}, u32[]{:S(2)}) %collective-permute-start) | collective-permute-done | bytes 28704 | tf_op jit(solution)/shard_map/ppermute | solution.py:690
  18.2 0.8 pad_maximum_fusion
  19.0 0.1 broadcast_in_dim.2
  19.1 22.0 %all_to_all.30.refs_0_ = bf16[16,224,128]{2,1,0:T(8,128)(2,1)} all-to-all(bf16[16,224,128]{2,1,0:T(8,128)(2,1)S(1)} %broadcast_in_dim.2), channel_id=1, replica_groups={{0,1,2,3,8,9,10,11,16,17,18,19,24,25,26,27},{4,5,6,7,12,13,14,15,20,21,..., dimensions={0} | all-to-all | bytes 1835008 | tf_op jit(solution)/shard_map/all_to_all | solution.py:632
  41.1 0.0 copy-start.9
  41.1 8.2 %shard_map.220 = (f32[16,8,128]{2,1,0:T(8,128)}, bf16[32,16,128]{2,1,0:T(8,128)(2,1)}, f32[128,384]{1,0:T(8,128)}, bf16[128,1152]{1,0:T(8,128)(2,1)}, f32[6,128,...) custom-call(s32[1]{0:T(128)} %bitcast.where, ...), custom_call_target="tpu_custom_call" | custom-call | flops 6600000000 | bytes 6815748 | tf_op jit(solution)/shard_map/pallas_call | solution.py:590
  49.3 3.7 %all-to-all-start.1 = ((f32[16,8,128]{2,1,0:T(8,128)}), f32[16,8,128]{2,1,0:T(8,128)S(1)}, u32[]{:S(2)}, u32[]{:S(2)}) async-start(f32[16,8,128]{2,1,0:T(8,128)} %get-tuple-element.44), calls=%async_computation.1 | async-start | bytes 131072 | tf_op jit(solution)/shard_map/all_to_all | solution.py:632
  53.0 0.0 copy-done.9
  53.0 0.7 copy.36.label
  53.7 0.0 copy-done.10
  53.7 0.7 copy.37.censor
  54.4 0.0 copy-done.2
  54.4 0.8 copy.38.refs_2_
  55.2 0.0 copy-done.7
  55.2 0.7 copy.39.refs_7_
  55.9 4.5 %all-to-all-done.1.refs_0_ = f32[16,8,128]{2,1,0:T(8,128)S(1)} async-done(((f32[16,8,128]{2,1,0:T(8,128)}), f32[16,8,128]{2,1,0:T(8,128)S(1)}, u32[]{:S(2)}, u32[]{:S(2)}) %all-to-all-start.1) | async-done | bytes 65568 | tf_op jit(solution)/shard_map/all_to_all | solution.py:632
  60.4 0.6 copy-done.5
  61.0 13.2 %shard_map.221 = (f32[4,1]{1,0:T(4,128)}, bf16[4,128,384]{2,1,0:T(8,128)(2,1)}, bf16[128,1536]{1,0:T(8,128)(2,1)}, bf16[128,384]{1,0:T(8,128)(2,1)}, bf16[128,38...) custom-call(s32[1]{0:T(128)} %bitcast.where, ...), custom_call_target="tpu_custom_call" | custom-call | flops 13200000000 | bytes 9047092 | tf_op jit(solution)/shard_map/pallas_call | solution.py:590
  74.2 0.0 copy-start.4
  74.2 0.0 copy-start.3
  74.2 0.0 copy-start.6
  74.3 3.7 %all-to-all-start.2 = ((bf16[16,32,384]{2,1,0:T(8,128)(2,1)}), bf16[16,32,384]{2,1,0:T(8,128)(2,1)S(1)}, u32[]{:S(2)}, u32[]{:S(2)}) async-start(bf16[16,32,384]{2,1,0:T(8,128)(2,1)} %bitcast.20), calls=%async_computation.2 | async-start | bytes 786432 | tf_op jit(solution)/shard_map/all_to_all | solution.py:632
  78.0 1.2 reshape.83
  79.2 1.2 reshape.84
  80.4 1.0 reshape.85
  81.4 0.0 copy-done.4
  81.5 0.2 reshape.86
  81.6 0.0 copy-done.3
  81.6 0.2 reshape.87
  81.8 0.0 copy-done.6
  81.8 0.1 reshape.88
  81.9 4.4 %shard_map.222 = (bf16[3456,128]{1,0:T(8,128)(2,1)}, bf16[3456,128]{1,0:T(8,128)(2,1)}) custom-call(s32[1]{0:T(128)} %bitcast.5.core, s32[1]{0:T(128)} %bitcast.where, bf16[128,1536]{1,0:T(8,128)(2,1)} %get-tuple-element.68.refs_0_, bf16[128,384]{1,0:T(8,128)(2,1)} %get-tuple-element.69.refs_1_, bf16[128,384]{1,0:T(8,128)(2,1)} %get-tuple-element.70.refs_2_, ...), custom_call_target="tpu_custom_call" | custom-call | flops 5500000256 | bytes 3342344 | tf_op jit(solution)/shard_map/pallas_call | solution.py:590
  86.3 0.1 collective-permute-start.1
  86.4 0.9 reshape.97
  87.4 0.1 dynamic-slice_convert_fusion
  87.6 0.6 reshape.92.refs_2_
  88.2 0.7 collective-permute-done.1.refs_1_
  89.0 0.9 copy-done.12
  89.9 2.8 %shard_map.223.refs_14_ = bf16[16,224,128]{2,1,0:T(8,128)(2,1)} custom-call(bf16[3456,128]{1,0:T(8,128)(2,1)} %get-tuple-element.76.refs_0_, bf16[3456,128]{1,0:T(8,128)(2,1)} %copy-done.12), custom_call_target="tpu_custom_call" | custom-call | flops 4400000000 | bytes 2686976 | tf_op jit(solution)/shard_map/pallas_call | solution.py:590
  92.8 0.0 all-to-all-done.2.refs_0_
  92.8 0.0 copy-start.1
  92.8 7.2 %all-to-all-start.3 = ((bf16[16,224,128]{2,1,0:T(8,128)(2,1)}), bf16[16,224,128]{2,1,0:T(8,128)(2,1)S(1)}, u32[]{:S(2)}, u32[]{:S(2)}) async-start(bf16[16,224,128]{2,1,0:T(8,128)(2,1)} %shard_map.223.refs_14_), calls=%async_computation.3 | async-start | bytes 1835008 | tf_op jit(solution)/shard_map/all_to_all | solution.py:632
  100.0 0.0 copy-done.1
  100.0 12.3 %shard_map.224 = (bf16[8144,128]{1,0:T(8,128)(2,1)}, bf16[8144,128]{1,0:T(8,128)(2,1)}) custom-call(s32[1]{0:T(128)} %bitcast.5.core, s32[1,32]{1,0:T(1,128)} %ids.3, bf16[16,32,384]{2,1,0:T(8,128)(2,1)} %copy-done.1, bf16[128,768]{1,0:T(8,128)(2,1)} %bitcast.23, bf16[2,80,128]{2,1,0:T(8,128)(2,1)} %reshape.92.refs_2_, bf16[384,1152]{1,0:T(8,128)(2,1)} %refs_3_.7, ...), custom_call_target="tpu_custom_call" | custom-call | flops 14300000256 | bytes 11419780 | tf_op jit(solution)/shard_map/pallas_call | solution.py:590
  112.3 0.1 collective-permute-start.2
  112.4 3.8 %all-to-all-done.3.parts = bf16[16,224,128]{2,1,0:T(8,128)(2,1)S(1)} async-done(((bf16[16,224,128]{2,1,0:T(8,128)(2,1)}), bf16[16,224,128]{2,1,0:T(8,128)(2,1)S(1)}, u32[]{:S(2)}, u32[]{:S(2)}) %all-to-all-start.3) | async-done | bytes 917536 | tf_op jit(solution)/shard_map/all_to_all | solution.py:632
  116.2 0.9 copy-done
  117.1 1.9 %shard_map.225.refs_2_.region_in = f32[224,128]{1,0:T(8,128)} custom-call(bf16[16,224,128]{2,1,0:T(8,128)(2,1)} %copy-done), custom_call_target="tpu_custom_call" | custom-call | flops 22000001024 | bytes 1032192 | tf_op jit(solution)/shard_map/pallas_call | solution.py:590
  119.0 0.0 collective-permute-done.2.refs_1_
  119.0 0.0 copy-start.11
  119.0 1.3 copy-done.11
  120.4 3.8 %shard_map.226 = (bf16[16,512,128]{2,1,0:T(8,128)(2,1)}, bf16[80,128]{1,0:T(8,128)(2,1)}) custom-call(bf16[8144,128]{1,0:T(8,128)(2,1)} %get-tuple-element.78.refs_0_, bf16[8144,128]{1,0:T(8,128)(2,1)} %copy-done.11, f32[224,128]{1,0:T(8,128)} %shard_map.225.refs_2_.region_in), custom_call_target="tpu_custom_call" | custom-call | flops 4400000000 | bytes 6402048 | tf_op jit(solution)/shard_map/pallas_call | solution.py:590
  124.1 33.7 %all_to_all.31.tile_in = bf16[16,512,128]{2,1,0:T(8,128)(2,1)} all-to-all(bf16[16,512,128]{2,1,0:T(8,128)(2,1)} %get-tuple-element.80), channel_id=1, replica_groups={{0,1,2,3,8,9,10,11,16,17,18,19,24,25,26,27},{4,5,6,7,12,13,14,15,20,21,..., dimensions={0} | all-to-all | bytes 4194304 | tf_op jit(solution)/shard_map/all_to_all | solution.py:632
  157.9 2.7 %shard_map.227 = bf16[8,128,128]{2,1,0:T(8,128)(2,1)} custom-call(s32[1]{0:T(128)} %bitcast.where, bf16[16,512,128]{2,1,0:T(8,128)(2,1)} %all_to_all.31.tile_in, f32[224,128]{1,0:T(8,128)} %shard_map.225.refs_2_.region_in, bf16[80,128]{1,0:T(8,128)(2,1)} %get-tuple-element.81.slide_in), custom_call_target="tpu_custom_call" | custom-call | flops 3300000000 | bytes 2494468 | tf_op jit(solution)/shard_map/pallas_call | solution.py:590
  160.6 7.8 %all-to-all-start.5 = ((bf16[8,128,128]{2,1,0:T(8,128)(2,1)}), bf16[8,128,128]{2,1,0:T(8,128)(2,1)S(1)}, u32[]{:S(2)}, u32[]{:S(2)}) async-start(bf16[8,128,128]{2,1,0:T(8,128)(2,1)} %shard_map.227), calls=%async_computation.5 | async-start | bytes 524288 | tf_op jit(solution)/shard_map/all_to_all | solution.py:632
  168.4 0.0 copy-done.8
  168.5 0.6 reduce
  169.1 8.3 %all-to-all-done.5 = bf16[8,128,128]{2,1,0:T(8,128)(2,1)S(1)} async-done(((bf16[8,128,128]{2,1,0:T(8,128)(2,1)}), bf16[8,128,128]{2,1,0:T(8,128)(2,1)S(1)}, u32[]{:S(2)}, u32[]{:S(2)}) %all-to-all-start.5) | async-done | bytes 262176 | tf_op jit(solution)/shard_map/all_to_all | solution.py:632
  177.5 0.6 slice_bitcast_fusion
  178.1 0.6 slice_bitcast_fusion.1
  178.7 0.6 slice_multiply_fusion
  (17 shorter events, 0.2 us)
Async XLA Ops:
  9.8 8.4 %collective-permute-start = (bf16[112,128]{1,0:T(8,128)(2,1)}, bf16[112,128]{1,0:T(8,128)(2,1)S(1)}, u32[]{:S(2)}, u32[]{:S(2)}) collective-permute-start(bf16[112,128]{1,0:T(8,128)(2,1)} %get-tuple-element.43), channel_id=1, source_target_pairs={{0,4},{1,5},{2,6},{3,7},{4,0},{5,1},{6,2},{7,3},{8,12},{9,13},{10,... | collective-permute-start | bytes 86024 | tf_op jit(solution)/shard_map/ppermute | solution.py:690
  41.1 11.9 %copy-start.9 = (s32[1,4]{1,0:T(1,128)S(1)}, s32[1,4]{1,0:T(1,128)}, u32[]{:S(2)}) copy-start(s32[1,4]{1,0:T(1,128)} %param.23) | copy-start | bytes 52
  41.1 12.6 %copy-start.10 = (s32[1,4]{1,0:T(1,128)S(1)}, s32[1,4]{1,0:T(1,128)}, u32[]{:S(2)}) copy-start(s32[1,4]{1,0:T(1,128)} %param.24) | copy-start | bytes 52
  41.1 13.2 %copy-start.2 = (bf16[384,192]{0,1:T(8,128)(2,1)S(1)}, bf16[384,192]{0,1:T(8,128)(2,1)}, u32[]{:S(2)}) copy-start(bf16[384,192]{0,1:T(8,128)(2,1)} %param.34) | copy-start | bytes 442372
  41.1 14.0 %copy-start.7 = (bf16[192,4]{0,1:T(4,128)(2,1)S(1)}, bf16[192,4]{0,1:T(4,128)(2,1)}, u32[]{:S(2)}) copy-start(bf16[192,4]{0,1:T(4,128)(2,1)} %param.39) | copy-start | bytes 4612
  49.3 11.1 %all-to-all-start.1 = ((f32[16,8,128]{2,1,0:T(8,128)}), f32[16,8,128]{2,1,0:T(8,128)S(1)}, u32[]{:S(2)}, u32[]{:S(2)}) async-start(f32[16,8,128]{2,1,0:T(8,128)} %get-tuple-element.44), calls=%async_computation.1 | async-start | bytes 131072 | tf_op jit(solution)/shard_map/all_to_all | solution.py:632
  60.4 0.6 copy-start.5
  74.2 7.2 %copy-start.4 = (bf16[192,192]{1,0:T(8,128)(2,1)S(1)}, bf16[192,192]{1,0:T(8,128)(2,1)}, u32[]{:S(2)}) copy-start(bf16[192,192]{1,0:T(8,128)(2,1)} %get-tuple-element.58) | copy-start | bytes 221188
  74.2 7.4 %copy-start.3 = (bf16[192,192]{1,0:T(8,128)(2,1)S(1)}, bf16[192,192]{1,0:T(8,128)(2,1)}, u32[]{:S(2)}) copy-start(bf16[192,192]{1,0:T(8,128)(2,1)} %get-tuple-element.59) | copy-start | bytes 221188
  74.2 7.5 %copy-start.6 = (bf16[192,4]{1,0:T(8,128)(2,1)S(1)}, bf16[192,4]{1,0:T(8,128)(2,1)}, u32[]{:S(2)}) copy-start(bf16[192,4]{1,0:T(8,128)(2,1)} %get-tuple-element.60) | copy-start | bytes 4612
  74.3 18.5 %all-to-all-start.2 = ((bf16[16,32,384]{2,1,0:T(8,128)(2,1)}), bf16[16,32,384]{2,1,0:T(8,128)(2,1)S(1)}, u32[]{:S(2)}, u32[]{:S(2)}) async-start(bf16[16,32,384]{2,1,0:T(8,128)(2,1)} %bitcast.20), calls=%async_computation.2 | async-start | bytes 786432 | tf_op jit(solution)/shard_map/all_to_all | solution.py:632
  86.3 2.7 %collective-permute-start.1 = (bf16[3456,128]{1,0:T(8,128)(2,1)}, bf16[3456,128]{1,0:T(8,128)(2,1)S(1)}, u32[]{:S(2)}, u32[]{:S(2)}) collective-permute-start(bf16[3456,128]{1,0:T(8,128)(2,1)} %get-tuple-element.77), channel_id=1, source_target_pairs={{0,32},{32,0},{64,96},{96,64},{128,160},{160,128},{192,224},{224,1... | collective-permute-start | bytes 2654216 | tf_op jit(solution)/shard_map/ppermute | solution.py:636
  89.0 0.9 copy-start.12
  92.8 7.2 %copy-start.1 = (bf16[16,32,384]{2,1,0:T(8,128)(2,1)}, bf16[16,32,384]{2,1,0:T(8,128)(2,1)S(1)}, u32[]{:S(2)}) copy-start(bf16[16,32,384]{2,1,0:T(8,128)(2,1)S(1)} %all-to-all-done.2.refs_0_) | copy-start | bytes 1179652
  92.8 23.4 %all-to-all-start.3 = ((bf16[16,224,128]{2,1,0:T(8,128)(2,1)}), bf16[16,224,128]{2,1,0:T(8,128)(2,1)S(1)}, u32[]{:S(2)}, u32[]{:S(2)}) async-start(bf16[16,224,128]{2,1,0:T(8,128)(2,1)} %shard_map.223.refs_14_), calls=%async_computation.3 | async-start | bytes 1835008 | tf_op jit(solution)/shard_map/all_to_all | solution.py:632
  112.3 6.7 %collective-permute-start.2 = (bf16[8144,128]{1,0:T(8,128)(2,1)}, bf16[8144,128]{1,0:T(8,128)(2,1)S(1)}, u32[]{:S(2)}, u32[]{:S(2)}) collective-permute-start(bf16[8144,128]{1,0:T(8,128)(2,1)} %get-tuple-element.79), channel_id=1, source_target_pairs={{0,32},{32,0},{64,96},{96,64},{128,160},{160,128},{192,224},{224,1... | collective-permute-start | bytes 6254600 | tf_op jit(solution)/shard_map/ppermute | solution.py:636
  116.2 0.9 copy-start
  119.0 1.3 copy-start.11
  157.9 10.6 %copy-start.8 = (f32[4,1]{1,0:T(4,128)S(1)}, f32[4,1]{1,0:T(4,128)}, u32[]{:S(2)}) copy-start(f32[4,1]{1,0:T(4,128)} %get-tuple-element.53) | copy-start | bytes 52
  160.6 16.8 %all-to-all-start.5 = ((bf16[8,128,128]{2,1,0:T(8,128)(2,1)}), bf16[8,128,128]{2,1,0:T(8,128)(2,1)S(1)}, u32[]{:S(2)}, u32[]{:S(2)}) async-start(bf16[8,128,128]{2,1,0:T(8,128)(2,1)} %shard_map.227), calls=%async_computation.5 | async-start | bytes 524288 | tf_op jit(solution)/shard_map/all_to_all | solution.py:632

commit v7 on v6

--- a/solution.py
+++ b/solution.py
@@ -89,19 +89,22 @@
     return out
 
 
-def encode_back(grad, x, w_qkv, w_out, w_up, w_down, heads, res, packed_grad, put):
+def encode_back(grad, x, w_qkv, w_out, w_up, w_down, heads, res, packed_grad, put, slope=None):
     packed_ref, attend_ref, mixture_ref, mid_ref, up_ref, _ = res
     width = x.shape[1]
     grad_b = grad.astype(BF16)
-    hidden, slope = gelu_parts(up_ref[...])
-    up_grad = (mm_nt(grad_b, w_down[...]).astype(BF16).astype(F32) * slope).astype(BF16)
-    put(3, hidden.astype(BF16), grad_b)
+    hidden = mixture = None
+    if slope is None:
+        hidden, slope = gelu_parts(up_ref[...])
+        hidden, mixture = hidden.astype(BF16), mixture_ref[...]
+    up_grad = (mm_nt(grad_b, w_down[...]).astype(BF16).astype(F32) * slope[...]).astype(BF16)
+    put(3, hidden, grad_b)
     normed, rstd = norm_parts(mid_ref[...])
     put(2, normed.astype(BF16), up_grad)
     normed_grad = mm_nt(up_grad, w_up[...]).astype(BF16).astype(F32)
     mid_grad = grad + norm_back(normed_grad, normed, rstd)
     mid_b = mid_grad.astype(BF16)
-    put(1, mixture_ref[...], mid_b)
+    put(1, mixture, mid_b)
     mix_grad = mm_nt(mid_b, w_out[...]).astype(BF16)
     for h in range(heads):
         q = packed_ref[:, h * HEAD : (h + 1) * HEAD]
@@ -122,10 +125,9 @@
     return mid_grad + norm_back(normed_grad, normed, rstd)
 
 
-def put_rows(flat, base, a, b):
-    rows, columns = a.shape[1], b.shape[1]
+def put_rows(flat, base, left, b):
+    rows, columns = left.shape[0], b.shape[1]
     chunks = columns // 128
-    left = a.T
     for c in range(0, chunks, 3):
         part = mm(left, b[:, c * 128 : (c + 3) * 128]).astype(BF16).astype(F32)
         for j in range(3):
@@ -267,8 +269,26 @@
     return [k < count for _, _, count in slots]
 
 
+def prepare(more, *refs):
+    ins, outs, bufs, obufs, sems, osems = cut(refs, 4 + more, 5 + more, 4 + more, 5 + more, 1, 1)
+    up, mid, x, mixture, *others = [Late(r, b, sems[0].at[i]) for i, (r, b) in enumerate(zip(ins, bufs))]
+    early = [Early(r, b, osems[0].at[i]) for i, (r, b) in enumerate(zip(outs, obufs))]
+    hidden, slope = gelu_parts(up[...])
+    early[0][...] = slope
+    early[1][...] = hidden.astype(BF16).T
+    early[2][...] = norm_parts(mid[...])[0].astype(BF16).T
+    early[3][...] = mixture[...].T
+    early[4][...] = norm_parts(x[...])[0].astype(BF16).T
+    for e, other in zip(early[5:], others):
+        e[...] = other[...].T
+    for e in early:
+        send(e)
+    for e in early:
+        e.finish()
+
+
 def region_forward(where, *refs):
-    ins, outs, bufs, rows, obufs, block, sems, osems, bsems, rsems = cut(refs, 5, 9, 4, 1, 7, 1, 1, 1, 1, 1)
+    ins, _, outs, bufs, rows, obufs, block, sems, osems, bsems, rsems = cut(refs, 5, 1, 9, 4, 1, 7, 1, 1, 1, 1, 1)
     rows = rows[0]
     h = lax.rem(where[0] // 4, 2)
     arriving = []
@@ -357,9 +377,9 @@
 
 
 def region_backward(scaling, where, label, censor, *refs):
-    ins, outs, bufs, obufs, extra, sems, osems = cut(refs, 19, 16, 19, 16, 10, 1, 1)
+    ins, outs, bufs, obufs, extra, sems, osems = cut(refs, 18, 12, 18, 12, 10, 1, 1)
     h = lax.rem(where[0] // 4, 2)
-    order = list(range(8)) + [18, 13, 17, 16, 14, 15, 9, 8, 10, 11, 12]
+    order = list(range(8)) + [17, 11, 16, 15, 10, 9, 14, 13, 8, 12]
     late = dict()
     for i in list(dict.fromkeys(order)):
         late[i] = Late(ins[i], bufs[i], sems[0].at[i])
@@ -369,8 +389,8 @@
     message, tails = late[0], late[1]
     slide_weights = [late[i] for i in range(2, 8)]
     w_qkv, w_out, w_up, w_down = [late[i] for i in range(8, 12)]
-    x_ref, res = late[12], [late[i] for i in range(13, 19)]
-    losses, spread, pairs, slide_grads = early[0], early[1], early[2:10], early[10:16]
+    x_ref, res = late[12], [late[13], late[14], None, late[15], None, late[17]]
+    losses, spread, pairs, slide_grads = early[0], early[1], early[2:6], early[6:12]
     packed_grad, slide_packed_grad, embeds, placed = extra[:4]
     ids, slide_col = tails_of(tails[...])
     rows32 = lax.broadcasted_iota(jnp.int32, (32, 32), 0)
@@ -400,11 +420,10 @@
     grad = norm_back(grad, normed, rstd)
 
     def put(i, a, b):
-        for at, value in ((6 - 2 * i, a), (7 - 2 * i, b)):
-            pairs[at][...] = value
-            send(pairs[at])
-
-    grad = encode_back(grad, x_ref[...], w_qkv, w_out, w_up, w_down, HEADS, res, packed_grad, put).astype(BF16)
+        pairs[i][...] = b
+        send(pairs[i])
+
+    grad = encode_back(grad, x_ref[...], w_qkv, w_out, w_up, w_down, HEADS, res, packed_grad, put, late[16]).astype(BF16)
     for b in range(8):
         spread[b] = mm_tn(choice(slots, b), grad).astype(BF16)
     leave([(spread.at[2 * y + h], outs[1].at[y]) for y in range(4)], sems[0])
@@ -430,7 +449,7 @@
 def region_weights(core, where, *refs):
     ins, halves, bufs, flat, run_buf, stage, sems, osems = cut(refs, 8, 2, 8, 1, 1, 1, 1, 1)
     late = [Late(r, b, sems[0].at[i]) for i, (r, b) in enumerate(zip(ins, bufs))]
-    hidden, grad, second, up_grad, mixture, mid_grad, first, packed_grad = late
+    hidden, second, mixture, first, packed_grad, mid_grad, up_grad, grad = late
     put_rows(flat[0], 9216, hidden[...], grad[...])
     put_rows(flat[0], 4608, second[...], up_grad[...])
     put_rows(flat[0], 3456, mixture[...], mid_grad[...])
@@ -452,12 +471,11 @@
 
 
 def tile_backward(core, ids, *refs):
-    ins, _, halves, bufs, packed_grad, flat, stage, sems, osems = cut(refs, 14, 1, 2, 14, 1, 1, 1, 1, 1)
-    late = [Late(ins[i], bufs[i], sems[0].at[i]) for i in (0, 13, 6, 12, 11, 5, 10, 4, 9, 8, 3, 7, 1, 2)]
-    late = dict(zip((0, 13, 6, 12, 11, 5, 10, 4, 9, 8, 3, 7, 1, 2), late))
-    arrived, patches, slide_rows = late[0], late[1], late[2]
-    w_qkv, w_out, w_up, w_down = [late[i] for i in range(3, 7)]
-    x_ref, res = late[7], [late[i] for i in range(8, 14)]
+    ins, _, halves, bufs, packed_grad, flat, stage, sems, osems = cut(refs, 16, 1, 2, 16, 1, 1, 1, 1, 1)
+    late = {i: Late(ins[i], bufs[i], sems[0].at[i]) for i in (0, 9, 4, 10, 11, 8, 3, 12, 2, 13, 6, 7, 1, 5, 14, 15)}
+    arrived, x_ref = late[0], late[5]
+    w_qkv, w_out, w_up, w_down = [late[i] for i in range(1, 5)]
+    res = [late[6], late[7], None, late[8], None, late[9]]
     rows32 = lax.broadcasted_iota(jnp.int32, (32, 32), 0)
     columns32 = lax.broadcasted_iota(jnp.int32, (32, 32), 1)
     assign = jnp.sum(jnp.where(rows32 == columns32, ids[...].astype(F32), 0.0), axis=1, keepdims=True)
@@ -474,56 +492,35 @@
     leaving = []
 
     def put(i, a, b):
-        put_rows(flat[0], bases[i], a, b)
+        put_rows(flat[0], bases[i], late[14 - i][...], b)
         if i == 2:
             leaving.extend(two_halves(flat[0], (2, 3), core[0], halves, stage[0], osems[0]))
 
-    grad = encode_back(grad, x_ref[...], w_qkv, w_out, w_up, w_down, HEADS, res, packed_grad[0], put)
-    for side in range(2):
-        which = core[0] if side == 0 else 1 - core[0]
-        stage[0][side, 8064:8144, :] = slide_rows.ref()[which]
-        part = pl.ds(8064, 80)
-        leaving.append(pltpu.make_async_copy(stage[0].at[side, part, :], halves[side].at[part, :], osems[0].at[side, 4]))
-        leaving[-1].start()
-    put_rows(flat[0], 0, patches[...], grad.astype(BF16))
+    grad = encode_back(grad, x_ref[...], w_qkv, w_out, w_up, w_down, HEADS, res, packed_grad[0], put, late[10])
+    put_rows(flat[0], 0, late[15][...], grad.astype(BF16))
     leaving.extend(two_halves(flat[0], (0, 1), core[0], halves, stage[0], osems[0]))
     for copy in leaving:
         copy.wait()
 
 
-def fold(rows, pad, tail, *refs):
-    mine, got = refs[:2]
-    refs = refs[2 + tail :]
-    if tail:
-        out, extra = refs[:2]
-        refs = refs[2:]
-    else:
-        out = refs[0]
-        refs = refs[1:]
-    a, b, total, stage, chunks, sems, osems = refs[:7]
-    planes = 2 if tail else 1
+def fold(planes, rows, pad, *refs):
+    unread = planes - 1
+    ins, _, outs, bufs, total, stage, chunks, sems, osems = cut(refs, 2, unread, 1, 2, 1, 1, 1, 1, 1)
+    stage, total = stage[0], total[0]
     run = 16 * planes * rows
     arriving = []
-    for z in range(4 + tail):
-        part = pl.ds(z * run, run if z < 4 else 80)
-        for side, (source, buffer) in enumerate(((mine, a), (got, b))):
-            arriving.append(pltpu.make_async_copy(source.at[part, :], buffer.at[part, :], sems.at[side, z]))
+    for z in range(4):
+        part = pl.ds(z * run, run)
+        for side in range(2):
+            arriving.append(pltpu.make_async_copy(ins[side].at[part, :], bufs[side].at[part, :], sems[0].at[side, z]))
             arriving[-1].start()
     for z in range(4):
         arriving[2 * z].wait()
         arriving[2 * z + 1].wait()
         part = pl.ds(z * run, run)
-        total[part, :] = a[part, :].astype(F32) + b[part, :].astype(F32)
+        total[part, :] = bufs[0][part, :].astype(F32) + bufs[1][part, :].astype(F32)
     leaving = []
-    if tail:
-        arriving[8].wait()
-        arriving[9].wait()
-        part = pl.ds(4 * run, 80)
-        refs[7][...] = (a[part, :].astype(F32) + b[part, :].astype(F32)).astype(BF16)
-        leaving.append(pltpu.make_async_copy(refs[7], extra, osems.at[16]))
-        leaving[-1].start()
-    if pad:
-        stage[4 * planes * rows :, :] = jnp.zeros((pad, LANES), F32)
+    stage[4 * planes * rows :, :] = jnp.zeros((pad, LANES), F32)
     for y in range(4):
         for x in range(4):
             for z in range(4):
@@ -531,8 +528,9 @@
                     source = (z * 16 * planes + y * 4 * planes + h * 4 + x) * rows
                     target = (z * planes + h) * rows
                     stage[target : target + rows, :] = total[source : source + rows, :]
-            chunks[y * 4 + x] = stage[...].astype(BF16)
-            leaving.append(pltpu.make_async_copy(chunks.at[y * 4 + x], out.at[y * 4 + x], osems.at[y * 4 + x]))
+            to = y * 4 + x
+            chunks[0][to] = stage[...].astype(BF16)
+            leaving.append(pltpu.make_async_copy(chunks[0].at[to], outs[0].at[to], osems[0].at[to]))
             leaving[-1].start()
     for copy in leaving:
         copy.wait()
@@ -632,20 +630,32 @@
     return lax.all_to_all(array, ALL, 0, 0, axis_index_groups=groups)
 
 
-def folded(mine, other, rows, pad, tail, after=()):
+def folded(mine, other, planes, rows, pad, after=()):
     got = lax.ppermute(other, "grp", OTHER_CORE)
-    planes = 1 + tail
-    height = 64 * planes * rows + 80 * tail
+    height = 64 * planes * rows
     chunk = 4 * planes * rows + pad
+    (out,) = call(
+        functools.partial(fold, planes, rows, pad),
+        4 * US,
+        [((16, chunk, LANES), BF16)],
+        [((height, LANES), BF16)] * 2
+        + [((height, LANES), F32), ((chunk, LANES), F32), ((16, chunk, LANES), BF16)]
+        + [semaphores(2, 4), semaphores(16)],
+        (mine, got) + after,
+    )
+    return out
+
+
+def prepared(kept, more):
+    x, packed, attend, mixture, mid, up, out = kept
+    ins = (up, mid, x, mixture) + more
+    outs = [(up.shape, F32)] + [((a.shape[1], a.shape[0]), BF16) for a in ins[:1] + ins[1:2] + ins[3:4] + ins[2:3] + more]
     return call(
-        functools.partial(fold, rows, pad, tail),
-        4 * US,
-        [((16, chunk, LANES), BF16)] + [((80, LANES), BF16)] * tail,
-        [((height, LANES), BF16)] * 2
-        + [((64 * planes * rows, LANES), F32), ((chunk, LANES), F32), ((16, chunk, LANES), BF16)]
-        + [semaphores(2, 5), semaphores(17)]
-        + [((80, LANES), BF16)] * tail,
-        (mine, got) + after,
+        functools.partial(prepare, len(more)),
+        3 * US,
+        outs,
+        like(ins) + outs + [semaphores(len(ins)), semaphores(len(outs))],
+        ins,
     )
 
 
@@ -689,6 +699,7 @@
     )
     both = jnp.concatenate([message, lax.ppermute(message, "dev", OTHER_PLANE)], axis=0)
     rows = exchange(jnp.broadcast_to(both[None], (16, 224, LANES)), PLANES)
+    tile_slope, *tile_left = prepared(tile_kept, (tokens,))
     region_res = [((2 * SLOTS, D), F32)] + residuals(2 * SLOTS, D, FF, HEADS)
     ins = (region_qkv, region_out, region_up, region_down)
     message, tails, *region_kept = call(
@@ -699,17 +710,20 @@
         + [((32, 112, LANES), BF16)]
         + region_res
         + [((8, LANES), F32), semaphores(4), semaphores(7), semaphores(33), semaphores(32)],
-        (where, rows) + ins,
+        (where, rows) + ins + (tile_slope,),
         scalars=1,
     )
     all_regions = exchange(message, PLANES)
     slide_weights = (slide_in, slide_qkv, slide_out, slide_up, slide_down, slide_head)
-    widths = (FF, D, D, FF, D, D, D, 3 * D)
+    widths = (3 * D, D, FF, D)
+    region_slope, *region_left = prepared(region_kept, ())
+    x, packed, attend, _, mid, _, out = region_kept
     pairs = [((2 * SLOTS, n), BF16) for n in widths]
     losses_out = [((SL_GRP, 1), F32)]
     outs = losses_out + [((4, 128, D), BF16)] + pairs + like(slide_weights)
     buffers = losses_out + [((8, 128, D), BF16)] + pairs + like(slide_weights)
-    ins = (all_regions, tails) + slide_weights + (region_qkv, region_out, region_up, region_down) + tuple(region_kept)
+    ins = (all_regions, tails) + slide_weights + (region_qkv, region_out, region_up, region_down)
+    ins = ins + (x, packed, attend, mid, region_slope, out)
     losses, spread, *rest = call(
         functools.partial(region_backward, scaling),
         12 * US,
@@ -718,13 +732,13 @@
         + buffers
         + [((2 * SLOTS, 3 * D), BF16), ((32, 3 * D_SL), BF16), ((32, D), BF16), ((32, D), F32)]
         + residuals(32, D_SL, D_SL, H_SL)
-        + [semaphores(19), semaphores(16)],
+        + [semaphores(18), semaphores(12)],
         (where, bin_label.reshape(SL_GRP, 1), censored.reshape(SL_GRP, 1)) + ins,
         scalars=1,
         whole=2,
     )
     arrived = exchange(spread.reshape(16, 32, D), PLANES)
-    ins = tuple(rest[:8])
+    ins = tuple(region_left) + tuple(rest[:4])
     mine, other = call(
         region_weights,
         5 * US,
@@ -734,7 +748,7 @@
         (core, where) + ins,
         scalars=2,
     )
-    (region_chunks,) = folded(mine, other, 54, 8, 0)
+    region_chunks = folded(mine, other, 1, 54, 8)
     region_parts = exchange(region_chunks, PLANES)
     (region_sums,) = call(
         plane_sum,
@@ -743,24 +757,29 @@
         like((region_parts,)) + [((224, LANES), F32), semaphores(2)],
         (region_parts,),
     )
-    slide_flat = jnp.concatenate([g.astype(F32).reshape(-1) for g in rest[8:]]).reshape(4, 2, 4, 2, 4, 1155)
+    slide_flat = jnp.concatenate([g.astype(F32).reshape(-1) for g in rest[4:]]).reshape(4, 2, 4, 2, 4, 1155)
     y, x = member_index // 8, lax.rem(member_index, 4)
     zero = jnp.zeros((), jnp.int32)
-    slide_rows = lax.dynamic_slice(slide_flat, (zero, zero, y, zero, x, zero), (4, 2, 1, 2, 1, 1155))
-    slide_rows = slide_rows.reshape(4, 2, 2, 1155).transpose(1, 0, 2, 3)
-    slide_rows = jnp.pad(slide_rows, ((0, 0), (0, 0), (0, 0), (0, 125))).astype(BF16).reshape(2, 80, LANES)
-    ins = (arrived, tokens, slide_rows, tile_qkv, tile_out, tile_up, tile_down) + tuple(tile_kept)
+
+    def slide_part(c):
+        part = lax.dynamic_slice(slide_flat, (zero, c, y, zero, x, zero), (4, 1, 1, 2, 1, 1155))
+        return jnp.pad(part.reshape(8, 1155), ((0, 0), (0, 125))).astype(BF16).reshape(80, LANES)
+
+    slide_got = lax.ppermute(slide_part(1 - core[0]), "grp", OTHER_CORE)
+    slide_sums = (slide_part(core[0]).astype(F32) + slide_got.astype(F32)).astype(BF16)
+    x, packed, attend, _, mid, _, out = tile_kept
+    ins = (arrived, tile_qkv, tile_out, tile_up, tile_down, x, packed, attend, mid, out, tile_slope) + tuple(tile_left)
     mine, other = call(
         tile_backward,
         13 * US,
-        [((8144, LANES), BF16)] * 2,
+        [((8064, LANES), BF16)] * 2,
         like(ins)
-        + [((128, 3 * D), BF16), ((16128, LANES), F32), ((2, 8144, LANES), BF16), semaphores(14), semaphores(2, 5)],
+        + [((128, 3 * D), BF16), ((16128, LANES), F32), ((2, 8064, LANES), BF16), semaphores(16), semaphores(2, 4)],
         (core, tile_region) + ins + (region_chunks,),
         scalars=1,
         whole=1,
     )
-    tile_chunks, slide_sums = folded(mine, other, 63, 8, 1, (region_sums,))
+    tile_chunks = folded(mine, other, 2, 63, 8, (region_sums,))
     tile_parts = exchange(tile_chunks, PLANES)
     ins = (tile_parts, region_sums, slide_sums)
     (last,) = call(

time: 180 us -> 185 us (1.028)
  blocking collectives: 55.8 us -> 0 us
  waiting for transfers between devices: 19.4 us -> 64.5 us
  starting transfers between devices: 29 us -> 37.7 us
  Pallas kernels: 56.1 us -> 61.5 us
    all_to_all x2 -> x0, blocking collectives: 55.8 us -> none  [exchange(): return lax.all_to_all(array, ALL, 0, 0, axis_index_groups=groups)]
    all_to_all x4 -> x6, waiting for transfers between devices: 16.6 us -> 61.3 us  [exchange(): return lax.all_to_all(array, ALL, 0, 0, axis_index_groups=groups)]
    all_to_all x4 -> x6, starting transfers between devices: 22.4 us -> 31 us  [exchange(): return lax.all_to_all(array, ALL, 0, 0, axis_index_groups=groups)]
    pallas_call x9 -> x11, Pallas kernels: 56.1 us -> 61.5 us  [call(): pl.pallas_call(kernel, out_shape=[jax.ShapeDtypeStruct(shape, kind) for s...]
    unnamed x33 -> x37, local copies, waits for them, and re-layouts: 5.5 us -> 6.47 us
  transfers between devices with their start and end apart: 7 -> 10, of which waited for: 5 -> 8; matrix products, arithmetic and copies ran while one was open for 5% -> 3% of each run, Pallas kernels for 12% -> 13%
where the time goes in v7:
time: 185 us; the launch traced here: 184 us
  waiting for transfers between devices  64.5 us (35%)
  Pallas kernels  61.5 us (33%)
  starting transfers between devices  37.7 us (20%)
  local copies, waits for them, and re-layouts  16 us (9%)
  other arithmetic  2.64 us (1%)
    pallas_call x11, Pallas kernels, call(): pl.pallas_call(kernel, out_shape=[jax.ShapeDtypeStruct(shape, kind) for s...  61.5 us
    all_to_all x6, waiting for transfers between devices, exchange(): return lax.all_to_all(array, ALL, 0, 0, axis_index_groups=groups)  61.3 us
    all_to_all x6, starting transfers between devices, exchange(): return lax.all_to_all(array, ALL, 0, 0, axis_index_groups=groups)  31 us
    unnamed x37, local copies, waits for them, and re-layouts  6.47 us
    ppermute x1, starting transfers between devices, body(): lax.ppermute(message, 'dev', OTHER_PLANE)  6.38 us
  transfers between devices with their start and end apart: 10, of which 8 were waited for; matrix products, arithmetic and copies ran while one was open for 3% of the time, Pallas kernels for 13%

profile of v7, /device:TPU:32, one launch (start us, length us, event | category | flops | bytes accessed | tf_op | source)
XLA Modules:
  0.0 184.1 jit_solution(5363092608427937268)
XLA Ops:
  0.6 1.6 copy.34
  2.9 6.9 %shard_map.219 = (bf16[112,128]{1,0:T(8,128)(2,1)}, f32[128,384]{1,0:T(8,128)}, bf16[128,1152]{1,0:T(8,128)(2,1)}, f32[6,128,128]{2,1,0:T(8,128)}, bf16[128,384]...) custom-call(s32[1]{0:T(128)} %bitcast.where, s32[1,32]{1,0:T(1,128)} %ids.3, ...), custom_call_target="tpu_custom_call" | custom-call | flops 7699999744 | bytes 6516872 | tf_op jit(solution)/shard_map/pallas_call | solution.py:588
  9.8 0.0 copy-start.4
  9.8 0.0 copy-start.10
  9.8 0.0 copy-start.12
  9.8 0.0 copy-start.13
  9.8 6.4 %collective-permute-start = (bf16[112,128]{1,0:T(8,128)(2,1)}, bf16[112,128]{1,0:T(8,128)(2,1)S(1)}, u32[]{:S(2)}, u32[]{:S(2)}) collective-permute-start(bf16[112,128]{1,0:T(8,128)(2,1)} %get-tuple-element.48), channel_id=1, source_target_pairs={{0,4},{1,5},{2,6},{3,7},{4,0},{5,1},{6,2},{7,3},{8,12},{9,13},{10,... | collective-permute-start | bytes 86024 | tf_op jit(solution)/shard_map/ppermute | solution.py:700
  16.2 2.1 %collective-permute-done = bf16[112,128]{1,0:T(8,128)(2,1)S(1)} collective-permute-done((bf16[112,128]{1,0:T(8,128)(2,1)}, bf16[112,128]{1,0:T(8,128)(2,1)S(1)}, u32[]{:S(2)}, u32[]{:S(2)}) %collective-permute-start) | collective-permute-done | bytes 28704 | tf_op jit(solution)/shard_map/ppermute | solution.py:700
  18.3 0.8 pad_maximum_fusion
  19.0 1.1 broadcast_in_dim.2
  20.1 7.0 %all-to-all-start = ((bf16[16,224,128]{2,1,0:T(8,128)(2,1)}), bf16[16,224,128]{2,1,0:T(8,128)(2,1)S(1)}, u32[]{:S(2)}, u32[]{:S(2)}) async-start(bf16[16,224,128]{2,1,0:T(8,128)(2,1)} %broadcast_in_dim.2), calls=%async_computation | async-start | bytes 1835008 | tf_op jit(solution)/shard_map/all_to_all | solution.py:630
  27.2 0.0 copy-done.4
  27.2 0.8 copy.37.refs_2_
  28.0 0.7 copy.38.refs_7_
  28.8 0.7 copy.35.label
  29.4 0.7 copy.36.censor
  30.1 3.6 %shard_map.220 = (f32[128,1536]{1,0:T(8,128)}, bf16[1536,128]{1,0:T(8,128)(2,1)}, bf16[384,128]{1,0:T(8,128)(2,1)}, bf16[384,128]{1,0:T(8,128)(2,1)}, bf16[384,1...) custom-call(f32[128,1536]{1,0:T(8,128)} %get-tuple-element.49.refs_0_, f32[128,384]{1,0:T(8,128)} %get-tuple-element.50.refs_1_.refs_8_, ...), custom_call_target="tpu_custom_call" | custom-call | flops 3300000000 | bytes 3145728 | tf_op jit(solution)/shard_map/pallas_call | solution.py:588
  33.7 8.5 %all-to-all-done.refs_0_ = bf16[16,224,128]{2,1,0:T(8,128)(2,1)S(1)} async-done(((bf16[16,224,128]{2,1,0:T(8,128)(2,1)}), bf16[16,224,128]{2,1,0:T(8,128)(2,1)S(1)}, u32[]{:S(2)}, u32[]{:S(2)}) %all-to-all-start) | async-done | bytes 917536 | tf_op jit(solution)/shard_map/all_to_all | solution.py:630
  42.1 0.9 copy-done.1
  43.1 8.1 %shard_map.221 = (f32[16,8,128]{2,1,0:T(8,128)}, bf16[32,16,128]{2,1,0:T(8,128)(2,1)}, f32[128,384]{1,0:T(8,128)}, bf16[128,1152]{1,0:T(8,128)(2,1)}, f32[6,128,...) custom-call(s32[1]{0:T(128)} %bitcast.where, ...), custom_call_target="tpu_custom_call" | custom-call | flops 6600000000 | bytes 7602180 | tf_op jit(solution)/shard_map/pallas_call | solution.py:588
  51.2 3.7 %all-to-all-start.1 = ((f32[16,8,128]{2,1,0:T(8,128)}), f32[16,8,128]{2,1,0:T(8,128)S(1)}, u32[]{:S(2)}, u32[]{:S(2)}) async-start(f32[16,8,128]{2,1,0:T(8,128)} %get-tuple-element.54), calls=%async_computation.1 | async-start | bytes 131072 | tf_op jit(solution)/shard_map/all_to_all | solution.py:630
  54.9 3.2 %shard_map.222 = (f32[128,1536]{1,0:T(8,128)}, bf16[1536,128]{1,0:T(8,128)(2,1)}, bf16[384,128]{1,0:T(8,128)(2,1)}, bf16[384,128]{1,0:T(8,128)(2,1)}, bf16[384,128]{1,0:T(8,128)(2,1)}) custom-call(f32[128,1536]{1,0:T(8,128)} %get-tuple-element.60.refs_0_, f32[128,384]{1,0:T(8,128)} %get-tuple-element.59.refs_1_.refs_15_, ...), custom_call_target="tpu_custom_call" | custom-call | flops 3300000000 | bytes 2752512 | tf_op jit(solution)/shard_map/pallas_call | solution.py:588
  58.1 4.2 %all-to-all-done.1.refs_0_ = f32[16,8,128]{2,1,0:T(8,128)S(1)} async-done(((f32[16,8,128]{2,1,0:T(8,128)}), f32[16,8,128]{2,1,0:T(8,128)S(1)}, u32[]{:S(2)}, u32[]{:S(2)}) %all-to-all-start.1) | async-done | bytes 65568 | tf_op jit(solution)/shard_map/all_to_all | solution.py:630
  62.3 0.6 copy-done.8
  62.9 12.2 %shard_map.223 = (f32[4,1]{1,0:T(4,128)}, bf16[4,128,384]{2,1,0:T(8,128)(2,1)}, bf16[128,1152]{1,0:T(8,128)(2,1)}, bf16[128,384]{1,0:T(8,128)(2,1)}, bf16[128,15...) custom-call(s32[1]{0:T(128)} %bitcast.where, ...), custom_call_target="tpu_custom_call" | custom-call | flops 13200000000 | bytes 8260660 | tf_op jit(solution)/shard_map/pallas_call | solution.py:588
  75.1 1.2 reshape.90
  76.3 1.2 reshape.91
  77.5 4.6 %shard_map.224 = (bf16[3456,128]{1,0:T(8,128)(2,1)}, bf16[3456,128]{1,0:T(8,128)(2,1)}) custom-call(s32[1]{0:T(128)} %bitcast.5.core, s32[1]{0:T(128)} %bitcast.where, bf16[1536,128]{1,0:T(8,128)(2,1)} %get-tuple-element.74.refs_0_, bf16[384,128]{1,0:T(8,128)(2,1)} %get-tuple-element.75.refs_1_, bf16[384,128]{1,0:T(8,128)(2,1)} %get-tuple-element.76.refs_2_, ...), custom_call_target="tpu_custom_call" | custom-call | flops 5500000256 | bytes 3342344 | tf_op jit(solution)/shard_map/pallas_call | solution.py:588
  82.1 0.1 collective-permute-start.1
  82.2 3.6 %all-to-all-start.2 = ((bf16[16,32,384]{2,1,0:T(8,128)(2,1)}), bf16[16,32,384]{2,1,0:T(8,128)(2,1)S(1)}, u32[]{:S(2)}, u32[]{:S(2)}) async-start(bf16[16,32,384]{2,1,0:T(8,128)(2,1)} %bitcast.6), calls=%async_computation.2 | async-start | bytes 786432 | tf_op jit(solution)/shard_map/all_to_all | solution.py:630
  85.8 0.0 collective-permute-done.1.refs_1_
  85.8 1.0 copy-done.14
  86.8 2.8 %shard_map.225.refs_16_ = bf16[16,224,128]{2,1,0:T(8,128)(2,1)} custom-call(bf16[3456,128]{1,0:T(8,128)(2,1)} %get-tuple-element.82.refs_0_, bf16[3456,128]{1,0:T(8,128)(2,1)} %copy-done.14), custom_call_target="tpu_custom_call" | custom-call | flops 4400000000 | bytes 2686976 | tf_op jit(solution)/shard_map/pallas_call | solution.py:588
  89.6 7.2 %all-to-all-done.2.refs_0_ = bf16[16,32,384]{2,1,0:T(8,128)(2,1)S(1)} async-done(((bf16[16,32,384]{2,1,0:T(8,128)(2,1)}), bf16[16,32,384]{2,1,0:T(8,128)(2,1)S(1)}, u32[]{:S(2)}, u32[]{:S(2)}) %all-to-all-start.2) | async-done | bytes 393248 | tf_op jit(solution)/shard_map/all_to_all | solution.py:630
  96.8 3.9 %all-to-all-start.3 = ((bf16[16,224,128]{2,1,0:T(8,128)(2,1)}), bf16[16,224,128]{2,1,0:T(8,128)(2,1)S(1)}, u32[]{:S(2)}, u32[]{:S(2)}) async-start(bf16[16,224,128]{2,1,0:T(8,128)(2,1)} %shard_map.225.refs_16_), calls=%async_computation.3 | async-start | bytes 1835008 | tf_op jit(solution)/shard_map/all_to_all | solution.py:630
  100.7 11.7 %shard_map.226 = (bf16[8064,128]{1,0:T(8,128)(2,1)}, bf16[8064,128]{1,0:T(8,128)(2,1)}) custom-call(s32[1]{0:T(128)} %bitcast.5.core, s32[1,32]{1,0:T(1,128)} %ids.3, bf16[16,32,384]{2,1,0:T(8,128)(2,1)} %copy-done.3, bf16[384,1152]{1,0:T(8,128)(2,1)} %refs_1_.5, bf16[384,384]{1,0:T(8,128)(2,1)} %refs_2_.6, bf16[384,1536]{1,0:T(8,128)(2,1)} %refs_3_.7, ...), custom_call_target="tpu_custom_call" | custom-call | flops 14300000256 | bytes 11927684 | tf_op jit(solution)/shard_map/pallas_call | solution.py:588
  112.4 0.1 collective-permute-start.2
  112.6 0.2 reshape.92
  112.7 3.6 %all-to-all-done.3.parts = bf16[16,224,128]{2,1,0:T(8,128)(2,1)S(1)} async-done(((bf16[16,224,128]{2,1,0:T(8,128)(2,1)}), bf16[16,224,128]{2,1,0:T(8,128)(2,1)S(1)}, u32[]{:S(2)}, u32[]{:S(2)}) %all-to-all-start.3) | async-done | bytes 917536 | tf_op jit(solution)/shard_map/all_to_all | solution.py:630
  116.3 0.9 copy-done.2
  117.3 1.9 %shard_map.227.refs_2_.region_in = f32[224,128]{1,0:T(8,128)} custom-call(bf16[16,224,128]{2,1,0:T(8,128)(2,1)} %copy-done.2), custom_call_target="tpu_custom_call" | custom-call | flops 22000001024 | bytes 1032192 | tf_op jit(solution)/shard_map/pallas_call | solution.py:588
  119.1 0.0 collective-permute-done.2.refs_1_
  119.2 4.0 %shard_map.228 = bf16[16,512,128]{2,1,0:T(8,128)(2,1)} custom-call(bf16[8064,128]{1,0:T(8,128)(2,1)} %get-tuple-element.84.refs_0_, bf16[8064,128]{1,0:T(8,128)(2,1)} %collective-permute-done.2.refs_1_, f32[224,128]{1,0:T(8,128)} %shard_map.227.refs_2_.region_in), custom_call_target="tpu_custom_call" | custom-call | flops 4400000000 | bytes 6340608 | tf_op jit(solution)/shard_map/pallas_call | solution.py:588
  123.2 4.9 %all-to-all-start.4 = ((bf16[16,512,128]{2,1,0:T(8,128)(2,1)}), bf16[16,512,128]{2,1,0:T(8,128)(2,1)S(1)}, u32[]{:S(2)}, u32[]{:S(2)}) async-start(bf16[16,512,128]{2,1,0:T(8,128)(2,1)} %shard_map.228), calls=%async_computation.4 | async-start | bytes 4194304 | tf_op jit(solution)/shard_map/all_to_all | solution.py:630
  128.1 0.0 copy-done.6
  128.1 0.2 reshape.93
  128.2 0.2 reshape.94
  128.4 0.0 copy-done.9
  128.4 0.1 reshape.95
  128.6 0.9 reshape.105
  129.5 0.3 convert_reduce_fusion.1
  129.9 0.1 reshape.100
  129.9 0.1 collective-permute-start.3
  130.0 1.1 collective-permute-done.3
  131.2 0.6 add_convert_fusion.slide_in
  131.8 29.1 %all-to-all-done.4.tile_in = bf16[16,512,128]{2,1,0:T(8,128)(2,1)S(1)} async-done(((bf16[16,512,128]{2,1,0:T(8,128)(2,1)}), bf16[16,512,128]{2,1,0:T(8,128)(2,1)S(1)}, u32[]{:S(2)}, u32[]{:S(2)}) %all-to-all-start.4) | async-done | bytes 2097184 | tf_op jit(solution)/shard_map/all_to_all | solution.py:630
  160.9 1.3 copy-done
  162.2 2.7 %shard_map.229 = bf16[8,128,128]{2,1,0:T(8,128)(2,1)} custom-call(s32[1]{0:T(128)} %bitcast.where, bf16[16,512,128]{2,1,0:T(8,128)(2,1)} %copy-done, f32[224,128]{1,0:T(8,128)} %shard_map.227.refs_2_.region_in, bf16[80,128]{1,0:T(8,128)(2,1)} %add_convert_fusion.slide_in), custom_call_target="tpu_custom_call" | custom-call | flops 3300000000 | bytes 2494468 | tf_op jit(solution)/shard_map/pallas_call | solution.py:588
  164.9 8.0 %all-to-all-start.5 = ((bf16[8,128,128]{2,1,0:T(8,128)(2,1)}), bf16[8,128,128]{2,1,0:T(8,128)(2,1)S(1)}, u32[]{:S(2)}, u32[]{:S(2)}) async-start(bf16[8,128,128]{2,1,0:T(8,128)(2,1)} %shard_map.229), calls=%async_computation.5 | async-start | bytes 524288 | tf_op jit(solution)/shard_map/all_to_all | solution.py:630
  173.0 0.6 reduce
  173.6 8.7 %all-to-all-done.5 = bf16[8,128,128]{2,1,0:T(8,128)(2,1)S(1)} async-done(((bf16[8,128,128]{2,1,0:T(8,128)(2,1)}), bf16[8,128,128]{2,1,0:T(8,128)(2,1)S(1)}, u32[]{:S(2)}, u32[]{:S(2)}) %all-to-all-start.5) | async-done | bytes 262176 | tf_op jit(solution)/shard_map/all_to_all | solution.py:630
  182.3 0.6 slice_bitcast_fusion
  182.9 0.6 slice_bitcast_fusion.1
  183.5 0.6 slice_multiply_fusion
  (31 shorter events, 0.2 us)
Async XLA Ops:
  9.8 17.4 %copy-start.4 = (bf16[384,192]{0,1:T(8,128)(2,1)S(1)}, bf16[384,192]{0,1:T(8,128)(2,1)}, u32[]{:S(2)}) copy-start(bf16[384,192]{0,1:T(8,128)(2,1)} %param.34) | copy-start | bytes 442372
  9.8 18.2 %copy-start.10 = (bf16[192,4]{0,1:T(4,128)(2,1)S(1)}, bf16[192,4]{0,1:T(4,128)(2,1)}, u32[]{:S(2)}) copy-start(bf16[192,4]{0,1:T(4,128)(2,1)} %param.39) | copy-start | bytes 4612
  9.8 18.9 %copy-start.12 = (s32[1,4]{1,0:T(1,128)S(1)}, s32[1,4]{1,0:T(1,128)}, u32[]{:S(2)}) copy-start(s32[1,4]{1,0:T(1,128)} %param.23) | copy-start | bytes 52
  9.8 19.6 %copy-start.13 = (s32[1,4]{1,0:T(1,128)S(1)}, s32[1,4]{1,0:T(1,128)}, u32[]{:S(2)}) copy-start(s32[1,4]{1,0:T(1,128)} %param.24) | copy-start | bytes 52
  9.8 8.4 %collective-permute-start = (bf16[112,128]{1,0:T(8,128)(2,1)}, bf16[112,128]{1,0:T(8,128)(2,1)S(1)}, u32[]{:S(2)}, u32[]{:S(2)}) collective-permute-start(bf16[112,128]{1,0:T(8,128)(2,1)} %get-tuple-element.48), channel_id=1, source_target_pairs={{0,4},{1,5},{2,6},{3,7},{4,0},{5,1},{6,2},{7,3},{8,12},{9,13},{10,... | collective-permute-start | bytes 86024 | tf_op jit(solution)/shard_map/ppermute | solution.py:700
  20.1 22.1 %all-to-all-start = ((bf16[16,224,128]{2,1,0:T(8,128)(2,1)}), bf16[16,224,128]{2,1,0:T(8,128)(2,1)S(1)}, u32[]{:S(2)}, u32[]{:S(2)}) async-start(bf16[16,224,128]{2,1,0:T(8,128)(2,1)} %broadcast_in_dim.2), calls=%async_computation | async-start | bytes 1835008 | tf_op jit(solution)/shard_map/all_to_all | solution.py:630
  42.1 0.9 copy-start.1
  51.2 11.1 %all-to-all-start.1 = ((f32[16,8,128]{2,1,0:T(8,128)}), f32[16,8,128]{2,1,0:T(8,128)S(1)}, u32[]{:S(2)}, u32[]{:S(2)}) async-start(f32[16,8,128]{2,1,0:T(8,128)} %get-tuple-element.54), calls=%async_computation.1 | async-start | bytes 131072 | tf_op jit(solution)/shard_map/all_to_all | solution.py:630
  62.3 0.6 copy-start.8
  82.1 3.7 %collective-permute-start.1 = (bf16[3456,128]{1,0:T(8,128)(2,1)}, bf16[3456,128]{1,0:T(8,128)(2,1)S(1)}, u32[]{:S(2)}, u32[]{:S(2)}) collective-permute-start(bf16[3456,128]{1,0:T(8,128)(2,1)} %get-tuple-element.83), channel_id=1, source_target_pairs={{0,32},{32,0},{64,96},{96,64},{128,160},{160,128},{192,224},{224,1... | collective-permute-start | bytes 2654216 | tf_op jit(solution)/shard_map/ppermute | solution.py:634
  82.2 14.6 %all-to-all-start.2 = ((bf16[16,32,384]{2,1,0:T(8,128)(2,1)}), bf16[16,32,384]{2,1,0:T(8,128)(2,1)S(1)}, u32[]{:S(2)}, u32[]{:S(2)}) async-start(bf16[16,32,384]{2,1,0:T(8,128)(2,1)} %bitcast.6), calls=%async_computation.2 | async-start | bytes 786432 | tf_op jit(solution)/shard_map/all_to_all | solution.py:630
  85.8 1.0 copy-start.14
  96.8 3.9 %copy-start.3 = (bf16[16,32,384]{2,1,0:T(8,128)(2,1)}, bf16[16,32,384]{2,1,0:T(8,128)(2,1)S(1)}, u32[]{:S(2)}) copy-start(bf16[16,32,384]{2,1,0:T(8,128)(2,1)S(1)} %all-to-all-done.2.refs_0_) | copy-start | bytes 1179652
  96.8 19.5 %all-to-all-start.3 = ((bf16[16,224,128]{2,1,0:T(8,128)(2,1)}), bf16[16,224,128]{2,1,0:T(8,128)(2,1)S(1)}, u32[]{:S(2)}, u32[]{:S(2)}) async-start(bf16[16,224,128]{2,1,0:T(8,128)(2,1)} %shard_map.225.refs_16_), calls=%async_computation.3 | async-start | bytes 1835008 | tf_op jit(solution)/shard_map/all_to_all | solution.py:630
  100.7 11.9 %copy-start.7 = (bf16[192,192]{1,0:T(8,128)(2,1)S(1)}, bf16[192,192]{1,0:T(8,128)(2,1)}, u32[]{:S(2)}) copy-start(bf16[192,192]{1,0:T(8,128)(2,1)} %get-tuple-element.88) | copy-start | bytes 221188
  112.4 6.7 %collective-permute-start.2 = (bf16[8064,128]{1,0:T(8,128)(2,1)}, bf16[8064,128]{1,0:T(8,128)(2,1)}, u32[]{:S(2)}, u32[]{:S(2)}) collective-permute-start(bf16[8064,128]{1,0:T(8,128)(2,1)} %get-tuple-element.85), channel_id=1, source_target_pairs={{0,32},{32,0},{64,96},{96,64},{128,160},{160,128},{192,224},{224,1... | collective-permute-start | bytes 6193160 | tf_op jit(solution)/shard_map/ppermute | solution.py:634
  116.3 0.9 copy-start.2
  123.1 4.9 %copy-start.6 = (bf16[192,192]{1,0:T(8,128)(2,1)S(1)}, bf16[192,192]{1,0:T(8,128)(2,1)}, u32[]{:S(2)}) copy-start(bf16[192,192]{1,0:T(8,128)(2,1)} %get-tuple-element.89) | copy-start | bytes 221188
  123.1 5.1 %copy-start.5 = (bf16[192,192]{1,0:T(8,128)(2,1)S(1)}, bf16[192,192]{1,0:T(8,128)(2,1)}, u32[]{:S(2)}) copy-start(bf16[192,192]{1,0:T(8,128)(2,1)} %get-tuple-element.90) | copy-start | bytes 221188
  123.1 5.2 %copy-start.9 = (bf16[192,4]{1,0:T(8,128)(2,1)S(1)}, bf16[192,4]{1,0:T(8,128)(2,1)}, u32[]{:S(2)}) copy-start(bf16[192,4]{1,0:T(8,128)(2,1)} %get-tuple-element.91) | copy-start | bytes 4612
  123.2 37.8 %all-to-all-start.4 = ((bf16[16,512,128]{2,1,0:T(8,128)(2,1)}), bf16[16,512,128]{2,1,0:T(8,128)(2,1)S(1)}, u32[]{:S(2)}, u32[]{:S(2)}) async-start(bf16[16,512,128]{2,1,0:T(8,128)(2,1)} %shard_map.228), calls=%async_computation.4 | async-start | bytes 4194304 | tf_op jit(solution)/shard_map/all_to_all | solution.py:630
  129.9 1.3 collective-permute-start.3
  131.8 41.1 %copy-start.11 = (f32[4,1]{1,0:T(4,128)S(1)}, f32[4,1]{1,0:T(4,128)}, u32[]{:S(2)}) copy-start(f32[4,1]{1,0:T(4,128)} %get-tuple-element.64) | copy-start | bytes 52
  160.9 1.3 copy-start
  164.9 17.3 %all-to-all-start.5 = ((bf16[8,128,128]{2,1,0:T(8,128)(2,1)}), bf16[8,128,128]{2,1,0:T(8,128)(2,1)S(1)}, u32[]{:S(2)}, u32[]{:S(2)}) async-start(bf16[8,128,128]{2,1,0:T(8,128)(2,1)} %shard_map.229), calls=%async_computation.5 | async-start | bytes 524288 | tf_op jit(solution)/shard_map/all_to_all | solution.py:630

commit v8 on v6

--- a/solution.py
+++ b/solution.py
@@ -316,7 +316,7 @@
 
 def slide_step(embeds, slide_row, slide_col, label, censor, slide_in, w_qkv, w_out, w_up, w_down, head, losses, grads, res, packed_grad, scaling):
     emb = embeds[...]
-    x = mm(emb, slide_in[...])
+    x = mm_nt(emb, slide_in[...])
     out = encode(x, slide_col == slide_row, w_qkv, w_out, w_up, w_down, H_SL, res)
     normed, rstd = norm_parts(out)
     sums, sizes, masks = [], [], []
@@ -327,22 +327,24 @@
         sizes.append(size)
         sums.append(jnp.sum(mask * normed, axis=0, keepdims=True) / size)
     pooled = jnp.concatenate(sums, axis=0).astype(BF16)
-    logits = mm(pooled, head[...])
+    logits = mm_nt(pooled, head[...])
     soft = jnp.log1p(jnp.exp(-jnp.abs(logits)))
     log_hazard = -(jnp.maximum(-logits, 0.0) + soft)
     log_stay = -(jnp.maximum(logits, 0.0) + soft)
-    bin_at = lax.broadcasted_iota(jnp.int32, (SL_GRP, NBINS), 1)
-    at = (bin_at == label[...]).astype(F32)
-    before = (bin_at < label[...]).astype(F32)
-    held = censor[...].astype(F32)
+    bin_at = lax.broadcasted_iota(jnp.int32, (SL_GRP, NBINS), 1).astype(F32)
+    same = lax.broadcasted_iota(jnp.int32, (SL_GRP, SL_GRP), 0) == lax.broadcasted_iota(jnp.int32, (SL_GRP, SL_GRP), 1)
+    bins = jnp.sum(jnp.where(same, label[...].astype(F32), 0.0), axis=1, keepdims=True)
+    held = jnp.sum(jnp.where(same, censor[...].astype(F32), 0.0), axis=1, keepdims=True)
+    at = jnp.where(bin_at == bins, 1.0, 0.0)
+    before = jnp.where(bin_at < bins, 1.0, 0.0)
     past = jnp.sum(before * log_stay, axis=1, keepdims=True)
     seen = past + jnp.sum(at * log_hazard, axis=1, keepdims=True)
     lived = past + jnp.sum(at * log_stay, axis=1, keepdims=True)
-    losses[...] = -(1.0 - held) * seen - held * lived
+    losses[...] = jnp.sum(jnp.where(same, -(1.0 - held) * seen - held * lived, 0.0), axis=0, keepdims=True)
     chance = 1.0 / (1.0 + jnp.exp(-logits))
     logit_grad = (scaling * (before * chance + at * (chance - (1.0 - held)))).astype(BF16)
     grads[5][...] = mm_tn(pooled, logit_grad).astype(BF16)
-    pooled_grad = mm_nt(logit_grad, head[...]).astype(BF16).astype(F32)
+    pooled_grad = mm(logit_grad, head[...]).astype(BF16).astype(F32)
     grad = jnp.zeros_like(normed)
     for s in range(SL_GRP):
         grad = grad + masks[s] * (pooled_grad[s : s + 1] / sizes[s])
@@ -353,7 +355,7 @@
 
     grad = encode_back(grad, x, w_qkv, w_out, w_up, w_down, H_SL, res, packed_grad, put).astype(BF16)
     grads[0][...] = mm_tn(emb, grad).astype(BF16)
-    return mm_nt(grad, slide_in[...]).astype(BF16)
+    return mm(grad, slide_in[...]).astype(BF16)
 
 
 def region_backward(scaling, where, label, censor, *refs):
@@ -581,7 +583,7 @@
         copy.wait()
 
 
-def call(kernel, macs, outs, scratch, inputs, scalars=0, whole=0):
+def call(kernel, macs, outs, scratch, inputs, scalars=0, whole=0, mebibytes=60):
     specs = [pl.BlockSpec(memory_space=pltpu.SMEM)] * scalars
     specs += [pl.BlockSpec(memory_space=pltpu.VMEM)] * whole
     specs += [pl.BlockSpec(memory_space=pl.ANY)] * (len(inputs) - scalars - whole)
@@ -593,7 +595,7 @@
         in_specs=specs,
         out_specs=[pl.BlockSpec(memory_space=pl.ANY)] * len(outs),
         scratch_shapes=[pltpu.VMEM(*item) if isinstance(item, tuple) else item for item in scratch],
-        compiler_params=pltpu.CompilerParams(vmem_limit_bytes=60 * 1024 * 1024),
+        compiler_params=pltpu.CompilerParams(vmem_limit_bytes=mebibytes * 1024 * 1024),
         cost_estimate=cost,
     )(*inputs)
 
@@ -646,6 +648,7 @@
         + [semaphores(2, 5), semaphores(17)]
         + [((80, LANES), BF16)] * tail,
         (mine, got) + after,
+        mebibytes=24 if tail else 60,
     )
 
 
@@ -706,10 +709,10 @@
     slide_weights = (slide_in, slide_qkv, slide_out, slide_up, slide_down, slide_head)
     widths = (FF, D, D, FF, D, D, D, 3 * D)
     pairs = [((2 * SLOTS, n), BF16) for n in widths]
-    losses_out = [((SL_GRP, 1), F32)]
+    losses_out = [((1, SL_GRP), F32)]
     outs = losses_out + [((4, 128, D), BF16)] + pairs + like(slide_weights)
     buffers = losses_out + [((8, 128, D), BF16)] + pairs + like(slide_weights)
-    ins = (all_regions, tails) + slide_weights + (region_qkv, region_out, region_up, region_down) + tuple(region_kept)
+    ins = (all_regions, tails, slide_in.T) + slide_weights[1:5] + (slide_head.T,) + (region_qkv, region_out, region_up, region_down) + tuple(region_kept)
     losses, spread, *rest = call(
         functools.partial(region_backward, scaling),
         12 * US,
@@ -719,7 +722,7 @@
         + [((2 * SLOTS, 3 * D), BF16), ((32, 3 * D_SL), BF16), ((32, D), BF16), ((32, D), F32)]
         + residuals(32, D_SL, D_SL, H_SL)
         + [semaphores(19), semaphores(16)],
-        (where, bin_label.reshape(SL_GRP, 1), censored.reshape(SL_GRP, 1)) + ins,
+        (where, bin_label, censored) + ins,
         scalars=1,
         whole=2,
     )
@@ -742,6 +745,7 @@
         [((224, LANES), F32)],
         like((region_parts,)) + [((224, LANES), F32), semaphores(2)],
         (region_parts,),
+        mebibytes=24,
     )
     slide_flat = jnp.concatenate([g.astype(F32).reshape(-1) for g in rest[8:]]).reshape(4, 2, 4, 2, 4, 1155)
     y, x = member_index // 8, lax.rem(member_index, 4)
@@ -772,12 +776,13 @@
         + [semaphores(3), semaphores(8)],
         (where,) + ins,
         scalars=1,
+        mebibytes=24,
     )
     total = jnp.sum(exchange(last, COLUMNS).astype(F32), axis=0)
     tile_result = total[0:63].reshape(8064)
     region_result = total[64:118].reshape(6912)
     slide_result = total[118:128].reshape(1280)[:1155] * 0.5
-    return (losses.reshape(1, SL_GRP), tile_result, region_result, slide_result)
+    return (losses, tile_result, region_result, slide_result)
 
 
 def solution(mesh):

time: 180 us -> 179 us (level)
  blocking collectives: 55.8 us -> 73.3 us
  starting transfers between devices: 29 us -> 21.1 us
  waiting for transfers between devices: 19.4 us -> 14.2 us
  local copies, waits for them, and re-layouts: 15.5 us -> 11.3 us
    all_to_all x2 -> x3, blocking collectives: 55.8 us -> 73.3 us  [exchange(): return lax.all_to_all(array, ALL, 0, 0, axis_index_groups=groups)]
    all_to_all x4 -> x3, starting transfers between devices: 22.4 us -> 14.5 us  [exchange(): return lax.all_to_all(array, ALL, 0, 0, axis_index_groups=groups)]
    all_to_all x4 -> x3, waiting for transfers between devices: 16.6 us -> 11.2 us  [exchange(): return lax.all_to_all(array, ALL, 0, 0, axis_index_groups=groups)]
    unnamed x33 -> x19, local copies, waits for them, and re-layouts: 5.5 us -> 2.64 us
  transfers between devices with their start and end apart: 7 -> 6, of which waited for: 5 -> 5; matrix products, arithmetic and copies ran while one was open for 5% -> 3% of each run, Pallas kernels for 12% -> 11%
where the time goes in v8:
time: 179 us
  blocking collectives  73.3 us (41%)
  Pallas kernels  55.7 us (31%)
  starting transfers between devices  21.1 us (12%)
  waiting for transfers between devices  14.2 us (8%)
  local copies, waits for them, and re-layouts  11.3 us (6%)
    all_to_all x3, blocking collectives, exchange(): return lax.all_to_all(array, ALL, 0, 0, axis_index_groups=groups)  73.3 us
    pallas_call x9, Pallas kernels, call(): pl.pallas_call(kernel, out_shape=[jax.ShapeDtypeStruct(shape, kind) for s...  55.7 us
    all_to_all x3, starting transfers between devices, exchange(): return lax.all_to_all(array, ALL, 0, 0, axis_index_groups=groups)  14.5 us
    all_to_all x3, waiting for transfers between devices, exchange(): return lax.all_to_all(array, ALL, 0, 0, axis_index_groups=groups)  11.2 us
    ppermute x1, starting transfers between devices, body(): lax.ppermute(message, 'dev', OTHER_PLANE)  6.37 us
    reshape x6, local copies, waits for them, and re-layouts, body(): g.astype(F32).reshape(-1)  3.89 us
  transfers between devices with their start and end apart: 6, of which 5 were waited for; matrix products, arithmetic and copies ran while one was open for 3% of the time, Pallas kernels for 11%

profile of v8, /device:TPU:32, one launch (start us, length us, event | category | flops | bytes accessed | tf_op | source)
XLA Modules:
  0.0 178.6 jit_solution(13776557777040866795)
XLA Ops:
  1.3 1.6 copy.27
  2.9 6.9 %shard_map.219 = (bf16[112,128]{1,0:T(8,128)(2,1)}, f32[128,384]{1,0:T(8,128)}, bf16[128,1152]{1,0:T(8,128)(2,1)}, f32[6,128,128]{2,1,0:T(8,128)}, bf16[128,384]...) custom-call(s32[1]{0:T(128)} %bitcast.where, s32[1,32]{1,0:T(1,128)} %ids.3, ...), custom_call_target="tpu_custom_call" | custom-call | flops 7699999744 | bytes 6516872 | tf_op jit(solution)/shard_map/pallas_call | solution.py:592
  9.8 6.4 %collective-permute-start = (bf16[112,128]{1,0:T(8,128)(2,1)}, bf16[112,128]{1,0:T(8,128)(2,1)S(1)}, u32[]{:S(2)}, u32[]{:S(2)}) collective-permute-start(bf16[112,128]{1,0:T(8,128)(2,1)} %get-tuple-element.43), channel_id=1, source_target_pairs={{0,4},{1,5},{2,6},{3,7},{4,0},{5,1},{6,2},{7,3},{8,12},{9,13},{10,... | collective-permute-start | bytes 86024 | tf_op jit(solution)/shard_map/ppermute | solution.py:693
  16.1 2.1 %collective-permute-done = bf16[112,128]{1,0:T(8,128)(2,1)S(1)} collective-permute-done((bf16[112,128]{1,0:T(8,128)(2,1)}, bf16[112,128]{1,0:T(8,128)(2,1)S(1)}, u32[]{:S(2)}, u32[]{:S(2)}) %collective-permute-start) | collective-permute-done | bytes 28704 | tf_op jit(solution)/shard_map/ppermute | solution.py:693
  18.2 0.8 pad_maximum_fusion
  19.0 0.1 broadcast_in_dim.2
  19.1 22.0 %all_to_all.30.refs_0_ = bf16[16,224,128]{2,1,0:T(8,128)(2,1)} all-to-all(bf16[16,224,128]{2,1,0:T(8,128)(2,1)S(1)} %broadcast_in_dim.2), channel_id=1, replica_groups={{0,1,2,3,8,9,10,11,16,17,18,19,24,25,26,27},{4,5,6,7,12,13,14,15,20,21,..., dimensions={0} | all-to-all | bytes 1835008 | tf_op jit(solution)/shard_map/all_to_all | solution.py:634
  41.1 8.1 %shard_map.220 = (f32[16,8,128]{2,1,0:T(8,128)}, bf16[32,16,128]{2,1,0:T(8,128)(2,1)}, f32[128,384]{1,0:T(8,128)}, bf16[128,1152]{1,0:T(8,128)(2,1)}, f32[6,128,...) custom-call(s32[1]{0:T(128)} %bitcast.where, ...), custom_call_target="tpu_custom_call" | custom-call | flops 6600000000 | bytes 6815748 | tf_op jit(solution)/shard_map/pallas_call | solution.py:592
  49.2 3.7 %all-to-all-start.1 = ((f32[16,8,128]{2,1,0:T(8,128)}), f32[16,8,128]{2,1,0:T(8,128)S(1)}, u32[]{:S(2)}, u32[]{:S(2)}) async-start(f32[16,8,128]{2,1,0:T(8,128)} %get-tuple-element.44), calls=%async_computation.1 | async-start | bytes 131072 | tf_op jit(solution)/shard_map/all_to_all | solution.py:634
  52.9 7.4 %all-to-all-done.1.refs_0_ = f32[16,8,128]{2,1,0:T(8,128)S(1)} async-done(((f32[16,8,128]{2,1,0:T(8,128)}), f32[16,8,128]{2,1,0:T(8,128)S(1)}, u32[]{:S(2)}, u32[]{:S(2)}) %all-to-all-start.1) | async-done | bytes 65568 | tf_op jit(solution)/shard_map/all_to_all | solution.py:634
  60.3 0.0 copy-start.4
  60.3 0.6 copy-done.4
  60.9 13.3 %shard_map.221 = (f32[1,4]{1,0:T(1,128)}, bf16[4,128,384]{2,1,0:T(8,128)(2,1)}, bf16[128,1536]{1,0:T(8,128)(2,1)}, bf16[128,384]{1,0:T(8,128)(2,1)}, bf16[128,38...) custom-call(s32[1]{0:T(128)} %bitcast.where, ...), custom_call_target="tpu_custom_call" | custom-call | flops 13200000000 | bytes 9047092 | tf_op jit(solution)/shard_map/pallas_call | solution.py:592
  74.2 0.0 copy-start.3
  74.2 0.0 copy-start.2
  74.2 0.0 copy-start.5
  74.2 3.7 %all-to-all-start.2 = ((bf16[16,32,384]{2,1,0:T(8,128)(2,1)}), bf16[16,32,384]{2,1,0:T(8,128)(2,1)S(1)}, u32[]{:S(2)}, u32[]{:S(2)}) async-start(bf16[16,32,384]{2,1,0:T(8,128)(2,1)} %bitcast.19), calls=%async_computation.2 | async-start | bytes 786432 | tf_op jit(solution)/shard_map/all_to_all | solution.py:634
  77.9 1.2 reshape.71
  79.1 1.2 reshape.72
  80.4 1.0 reshape.73
  81.4 0.0 copy-done.3
  81.4 0.2 reshape.74
  81.6 0.0 copy-done.2
  81.6 0.2 reshape.75
  81.8 0.0 copy-done.5
  81.8 0.1 reshape.76
  81.9 4.3 %shard_map.222 = (bf16[3456,128]{1,0:T(8,128)(2,1)}, bf16[3456,128]{1,0:T(8,128)(2,1)}) custom-call(s32[1]{0:T(128)} %bitcast.5.core, s32[1]{0:T(128)} %bitcast.where, bf16[128,1536]{1,0:T(8,128)(2,1)} %get-tuple-element.68.refs_0_, bf16[128,384]{1,0:T(8,128)(2,1)} %get-tuple-element.69.refs_1_, bf16[128,384]{1,0:T(8,128)(2,1)} %get-tuple-element.70.refs_2_, ...), custom_call_target="tpu_custom_call" | custom-call | flops 5500000256 | bytes 3342344 | tf_op jit(solution)/shard_map/pallas_call | solution.py:592
  86.2 0.1 collective-permute-start.1
  86.4 0.9 reshape.85
  87.3 0.1 dynamic-slice_convert_fusion
  87.5 0.6 reshape.80.refs_2_
  88.2 0.7 collective-permute-done.1.refs_1_
  88.9 0.0 copy-start.6
  88.9 0.9 copy-done.6
  89.8 2.8 %shard_map.223.refs_14_ = bf16[16,224,128]{2,1,0:T(8,128)(2,1)} custom-call(bf16[3456,128]{1,0:T(8,128)(2,1)} %get-tuple-element.76.refs_0_, bf16[3456,128]{1,0:T(8,128)(2,1)} %copy-done.6), custom_call_target="tpu_custom_call" | custom-call | flops 4400000000 | bytes 2686976 | tf_op jit(solution)/shard_map/pallas_call | solution.py:592
  92.7 0.0 all-to-all-done.2.refs_0_
  92.7 0.0 copy-start.1
  92.7 7.2 %all-to-all-start.3 = ((bf16[16,224,128]{2,1,0:T(8,128)(2,1)}), bf16[16,224,128]{2,1,0:T(8,128)(2,1)S(1)}, u32[]{:S(2)}, u32[]{:S(2)}) async-start(bf16[16,224,128]{2,1,0:T(8,128)(2,1)} %shard_map.223.refs_14_), calls=%async_computation.3 | async-start | bytes 1835008 | tf_op jit(solution)/shard_map/all_to_all | solution.py:634
  99.9 0.0 copy-done.1
  99.9 12.3 %shard_map.224 = (bf16[8144,128]{1,0:T(8,128)(2,1)}, bf16[8144,128]{1,0:T(8,128)(2,1)}) custom-call(s32[1]{0:T(128)} %bitcast.5.core, s32[1,32]{1,0:T(1,128)} %ids.3, bf16[16,32,384]{2,1,0:T(8,128)(2,1)} %copy-done.1, bf16[128,768]{1,0:T(8,128)(2,1)} %bitcast.22, bf16[2,80,128]{2,1,0:T(8,128)(2,1)} %reshape.80.refs_2_, bf16[384,1152]{1,0:T(8,128)(2,1)} %refs_3_.7, ...), custom_call_target="tpu_custom_call" | custom-call | flops 14300000256 | bytes 11419780 | tf_op jit(solution)/shard_map/pallas_call | solution.py:592
  112.2 0.1 collective-permute-start.2
  112.3 3.8 %all-to-all-done.3.parts = bf16[16,224,128]{2,1,0:T(8,128)(2,1)S(1)} async-done(((bf16[16,224,128]{2,1,0:T(8,128)(2,1)}), bf16[16,224,128]{2,1,0:T(8,128)(2,1)S(1)}, u32[]{:S(2)}, u32[]{:S(2)}) %all-to-all-start.3) | async-done | bytes 917536 | tf_op jit(solution)/shard_map/all_to_all | solution.py:634
  116.1 0.0 copy-start
  116.1 0.4 shard_map.225.refs_2_.region_in
  116.4 0.2 collective-permute-done.2.refs_1_
  116.6 1.0 copy-done
  117.6 6.7 %shard_map.226 = (bf16[16,512,128]{2,1,0:T(8,128)(2,1)S(1)}, bf16[80,128]{1,0:T(8,128)(2,1)S(1)}) custom-call(bf16[8144,128]{1,0:T(8,128)(2,1)S(1)} %copy-done, bf16[8144,128]{1,0:T(8,128)(2,1)S(1)} %collective-permute-done.2.refs_1_, f32[224,128]{1,0:T(8,128)S(1)} %shard_map.225.refs_2_.region_in), custom_call_target="tpu_custom_call" | custom-call | flops 4400000000 | bytes 6402048 | tf_op jit(solution)/shard_map/pallas_call | solution.py:592
  124.3 34.7 %all_to_all.31.tile_in = bf16[16,512,128]{2,1,0:T(8,128)(2,1)S(1)} all-to-all(bf16[16,512,128]{2,1,0:T(8,128)(2,1)S(1)} %get-tuple-element.80), channel_id=1, replica_groups={{0,1,2,3,8,9,10,11,16,17,18,19,24,25,26,27},{4,5,6,7,12,13,14,15,20,21,..., dimensions={0} | all-to-all | bytes 4194304 | tf_op jit(solution)/shard_map/all_to_all | solution.py:634
  159.0 1.1 shard_map.227
  160.1 16.6 %all_to_all.32 = bf16[8,128,128]{2,1,0:T(8,128)(2,1)S(1)} all-to-all(bf16[8,128,128]{2,1,0:T(8,128)(2,1)S(1)} %shard_map.227), channel_id=1, replica_groups={{0,4,64,68,128,132,192,196},{1,5,65,69,129,133,193,197},{2,6,66,70,130,..., dimensions={0} | all-to-all | bytes 524288 | tf_op jit(solution)/shard_map/all_to_all | solution.py:634
  176.7 0.6 slice_bitcast_fusion
  177.3 0.6 slice_bitcast_fusion.1
  178.0 0.6 slice_multiply_fusion
  (10 shorter events, 0.2 us)
Async XLA Ops:
  9.8 8.4 %collective-permute-start = (bf16[112,128]{1,0:T(8,128)(2,1)}, bf16[112,128]{1,0:T(8,128)(2,1)S(1)}, u32[]{:S(2)}, u32[]{:S(2)}) collective-permute-start(bf16[112,128]{1,0:T(8,128)(2,1)} %get-tuple-element.43), channel_id=1, source_target_pairs={{0,4},{1,5},{2,6},{3,7},{4,0},{5,1},{6,2},{7,3},{8,12},{9,13},{10,... | collective-permute-start | bytes 86024 | tf_op jit(solution)/shard_map/ppermute | solution.py:693
  49.2 11.1 %all-to-all-start.1 = ((f32[16,8,128]{2,1,0:T(8,128)}), f32[16,8,128]{2,1,0:T(8,128)S(1)}, u32[]{:S(2)}, u32[]{:S(2)}) async-start(f32[16,8,128]{2,1,0:T(8,128)} %get-tuple-element.44), calls=%async_computation.1 | async-start | bytes 131072 | tf_op jit(solution)/shard_map/all_to_all | solution.py:634
  60.3 0.6 copy-start.4
  74.2 7.2 %copy-start.3 = (bf16[192,192]{1,0:T(8,128)(2,1)S(1)}, bf16[192,192]{1,0:T(8,128)(2,1)}, u32[]{:S(2)}) copy-start(bf16[192,192]{1,0:T(8,128)(2,1)} %get-tuple-element.58) | copy-start | bytes 221188
  74.2 7.4 %copy-start.2 = (bf16[192,192]{1,0:T(8,128)(2,1)S(1)}, bf16[192,192]{1,0:T(8,128)(2,1)}, u32[]{:S(2)}) copy-start(bf16[192,192]{1,0:T(8,128)(2,1)} %get-tuple-element.59) | copy-start | bytes 221188
  74.2 7.5 %copy-start.5 = (bf16[192,4]{1,0:T(8,128)(2,1)S(1)}, bf16[192,4]{1,0:T(8,128)(2,1)}, u32[]{:S(2)}) copy-start(bf16[192,4]{1,0:T(8,128)(2,1)} %get-tuple-element.60) | copy-start | bytes 4612
  74.2 18.4 %all-to-all-start.2 = ((bf16[16,32,384]{2,1,0:T(8,128)(2,1)}), bf16[16,32,384]{2,1,0:T(8,128)(2,1)S(1)}, u32[]{:S(2)}, u32[]{:S(2)}) async-start(bf16[16,32,384]{2,1,0:T(8,128)(2,1)} %bitcast.19), calls=%async_computation.2 | async-start | bytes 786432 | tf_op jit(solution)/shard_map/all_to_all | solution.py:634
  86.2 2.7 %collective-permute-start.1 = (bf16[3456,128]{1,0:T(8,128)(2,1)}, bf16[3456,128]{1,0:T(8,128)(2,1)S(1)}, u32[]{:S(2)}, u32[]{:S(2)}) collective-permute-start(bf16[3456,128]{1,0:T(8,128)(2,1)} %get-tuple-element.77), channel_id=1, source_target_pairs={{0,32},{32,0},{64,96},{96,64},{128,160},{160,128},{192,224},{224,1... | collective-permute-start | bytes 2654216 | tf_op jit(solution)/shard_map/ppermute | solution.py:638
  88.9 0.9 copy-start.6
  92.7 7.2 %copy-start.1 = (bf16[16,32,384]{2,1,0:T(8,128)(2,1)}, bf16[16,32,384]{2,1,0:T(8,128)(2,1)S(1)}, u32[]{:S(2)}) copy-start(bf16[16,32,384]{2,1,0:T(8,128)(2,1)S(1)} %all-to-all-done.2.refs_0_) | copy-start | bytes 1179652
  92.7 23.4 %all-to-all-start.3 = ((bf16[16,224,128]{2,1,0:T(8,128)(2,1)}), bf16[16,224,128]{2,1,0:T(8,128)(2,1)S(1)}, u32[]{:S(2)}, u32[]{:S(2)}) async-start(bf16[16,224,128]{2,1,0:T(8,128)(2,1)} %shard_map.223.refs_14_), calls=%async_computation.3 | async-start | bytes 1835008 | tf_op jit(solution)/shard_map/all_to_all | solution.py:634
  112.2 4.4 %collective-permute-start.2 = (bf16[8144,128]{1,0:T(8,128)(2,1)}, bf16[8144,128]{1,0:T(8,128)(2,1)S(1)}, u32[]{:S(2)}, u32[]{:S(2)}) collective-permute-start(bf16[8144,128]{1,0:T(8,128)(2,1)} %get-tuple-element.79), channel_id=1, source_target_pairs={{0,32},{32,0},{64,96},{96,64},{128,160},{160,128},{192,224},{224,1... | collective-permute-start | bytes 6254600 | tf_op jit(solution)/shard_map/ppermute | solution.py:638
  116.1 1.6 copy-start

commit v9 on v8

--- a/solution.py
+++ b/solution.py
@@ -493,39 +493,17 @@
         copy.wait()
 
 
-def fold(rows, pad, tail, *refs):
-    mine, got = refs[:2]
-    refs = refs[2 + tail :]
+def fold(rows, pad, tail, mine, got, *refs):
+    _, (out,), extra, (total, stage) = cut(refs, tail, 1, tail, 2)
+    planes = 1 + tail
+    run = 16 * planes * rows
+    for z in range(4):
+        part = pl.ds(z * run, run)
+        total[part, :] = mine[part, :].astype(F32) + got[part, :].astype(F32)
     if tail:
-        out, extra = refs[:2]
-        refs = refs[2:]
-    else:
-        out = refs[0]
-        refs = refs[1:]
-    a, b, total, stage, chunks, sems, osems = refs[:7]
-    planes = 2 if tail else 1
-    run = 16 * planes * rows
-    arriving = []
-    for z in range(4 + tail):
-        part = pl.ds(z * run, run if z < 4 else 80)
-        for side, (source, buffer) in enumerate(((mine, a), (got, b))):
-            arriving.append(pltpu.make_async_copy(source.at[part, :], buffer.at[part, :], sems.at[side, z]))
-            arriving[-1].start()
-    for z in range(4):
-        arriving[2 * z].wait()
-        arriving[2 * z + 1].wait()
-        part = pl.ds(z * run, run)
-        total[part, :] = a[part, :].astype(F32) + b[part, :].astype(F32)
-    leaving = []
-    if tail:
-        arriving[8].wait()
-        arriving[9].wait()
         part = pl.ds(4 * run, 80)
-        refs[7][...] = (a[part, :].astype(F32) + b[part, :].astype(F32)).astype(BF16)
-        leaving.append(pltpu.make_async_copy(refs[7], extra, osems.at[16]))
-        leaving[-1].start()
-    if pad:
-        stage[4 * planes * rows :, :] = jnp.zeros((pad, LANES), F32)
+        extra[0][...] = (mine[part, :].astype(F32) + got[part, :].astype(F32)).astype(BF16)
+    stage[4 * planes * rows :, :] = jnp.zeros((pad, LANES), F32)
     for y in range(4):
         for x in range(4):
             for z in range(4):
@@ -533,11 +511,7 @@
                     source = (z * 16 * planes + y * 4 * planes + h * 4 + x) * rows
                     target = (z * planes + h) * rows
                     stage[target : target + rows, :] = total[source : source + rows, :]
-            chunks[y * 4 + x] = stage[...].astype(BF16)
-            leaving.append(pltpu.make_async_copy(chunks.at[y * 4 + x], out.at[y * 4 + x], osems.at[y * 4 + x]))
-            leaving[-1].start()
-    for copy in leaving:
-        copy.wait()
+            out[y * 4 + x] = stage[...].astype(BF16)
 
 
 def plane_sum(parts, out, buffer, total, sems):
@@ -637,19 +611,17 @@
 def folded(mine, other, rows, pad, tail, after=()):
     got = lax.ppermute(other, "grp", OTHER_CORE)
     planes = 1 + tail
-    height = 64 * planes * rows + 80 * tail
     chunk = 4 * planes * rows + pad
-    return call(
+    outs = [(16, chunk, LANES)] + [(80, LANES)] * tail
+    return pl.pallas_call(
         functools.partial(fold, rows, pad, tail),
-        4 * US,
-        [((16, chunk, LANES), BF16)] + [((80, LANES), BF16)] * tail,
-        [((height, LANES), BF16)] * 2
-        + [((64 * planes * rows, LANES), F32), ((chunk, LANES), F32), ((16, chunk, LANES), BF16)]
-        + [semaphores(2, 5), semaphores(17)]
-        + [((80, LANES), BF16)] * tail,
-        (mine, got) + after,
-        mebibytes=24 if tail else 60,
-    )
+        out_shape=[jax.ShapeDtypeStruct(shape, BF16) for shape in outs],
+        in_specs=[pl.BlockSpec(memory_space=pltpu.VMEM)] * 2 + [pl.BlockSpec(memory_space=pl.ANY)] * tail,
+        out_specs=[pl.BlockSpec(memory_space=pltpu.VMEM)] * len(outs),
+        scratch_shapes=[pltpu.VMEM((64 * planes * rows, LANES), F32), pltpu.VMEM((chunk, LANES), F32)],
+        compiler_params=pltpu.CompilerParams(vmem_limit_bytes=24 * 1024 * 1024),
+        cost_estimate=pl.CostEstimate(flops=8 * US, bytes_accessed=1 << 20, transcendentals=0),
+    )(mine, got, *after)
 
 
 def body(

time: 179 us -> 171 us (0.955)
  Pallas kernels: 55.7 us -> 48.8 us
    pallas_call x9 -> x7, Pallas kernels: 55.7 us -> 46.3 us  [call(): pl.pallas_call(kernel, out_shape=[jax.ShapeDtypeStruct(shape, kind) for s...]
    pallas_call x0 -> x2, Pallas kernels: none -> 2.48 us  [folded(): pl.pallas_call(functools.partial(fold, rows, pad, tail), out_shape=[jax.S...]
where the time goes in v9:
time: 171 us
  blocking collectives  73.3 us (43%)
  Pallas kernels  48.8 us (29%)
  starting transfers between devices  21.1 us (12%)
  waiting for transfers between devices  14.2 us (8%)
  local copies, waits for them, and re-layouts  10.4 us (6%)
    all_to_all x3, blocking collectives, exchange(): return lax.all_to_all(array, ALL, 0, 0, axis_index_groups=groups)  73.3 us
    pallas_call x7, Pallas kernels, call(): pl.pallas_call(kernel, out_shape=[jax.ShapeDtypeStruct(shape, kind) for s...  46.3 us
    all_to_all x3, starting transfers between devices, exchange(): return lax.all_to_all(array, ALL, 0, 0, axis_index_groups=groups)  14.5 us
    all_to_all x3, waiting for transfers between devices, exchange(): return lax.all_to_all(array, ALL, 0, 0, axis_index_groups=groups)  11.2 us
    ppermute x1, starting transfers between devices, body(): lax.ppermute(message, 'dev', OTHER_PLANE)  6.37 us
    reshape x6, local copies, waits for them, and re-layouts, body(): g.astype(F32).reshape(-1)  3.89 us
  transfers between devices with their start and end apart: 6, of which 5 were waited for; matrix products, arithmetic and copies ran while one was open for 3% of the time, Pallas kernels for 11%

profile of v9, /device:TPU:32, one launch (start us, length us, event | category | flops | bytes accessed | tf_op | source)
XLA Modules:
  0.0 170.6 jit_solution(9404240026458032632)
XLA Ops:
  1.3 1.6 copy.27
  2.9 6.9 %shard_map.219 = (bf16[112,128]{1,0:T(8,128)(2,1)}, f32[128,384]{1,0:T(8,128)}, bf16[128,1152]{1,0:T(8,128)(2,1)}, f32[6,128,128]{2,1,0:T(8,128)}, bf16[128,384]...) custom-call(s32[1]{0:T(128)} %bitcast.where, s32[1,32]{1,0:T(1,128)} %ids.3, ...), custom_call_target="tpu_custom_call" | custom-call | flops 7699999744 | bytes 6516872 | tf_op jit(solution)/shard_map/pallas_call | solution.py:566
  9.8 6.4 %collective-permute-start = (bf16[112,128]{1,0:T(8,128)(2,1)}, bf16[112,128]{1,0:T(8,128)(2,1)S(1)}, u32[]{:S(2)}, u32[]{:S(2)}) collective-permute-start(bf16[112,128]{1,0:T(8,128)(2,1)} %get-tuple-element.43), channel_id=1, source_target_pairs={{0,4},{1,5},{2,6},{3,7},{4,0},{5,1},{6,2},{7,3},{8,12},{9,13},{10,... | collective-permute-start | bytes 86024 | tf_op jit(solution)/shard_map/ppermute | solution.py:665
  16.1 2.1 %collective-permute-done = bf16[112,128]{1,0:T(8,128)(2,1)S(1)} collective-permute-done((bf16[112,128]{1,0:T(8,128)(2,1)}, bf16[112,128]{1,0:T(8,128)(2,1)S(1)}, u32[]{:S(2)}, u32[]{:S(2)}) %collective-permute-start) | collective-permute-done | bytes 28704 | tf_op jit(solution)/shard_map/ppermute | solution.py:665
  18.2 0.8 pad_maximum_fusion
  19.0 0.1 broadcast_in_dim.2
  19.1 22.0 %all_to_all.30.refs_0_ = bf16[16,224,128]{2,1,0:T(8,128)(2,1)} all-to-all(bf16[16,224,128]{2,1,0:T(8,128)(2,1)S(1)} %broadcast_in_dim.2), channel_id=1, replica_groups={{0,1,2,3,8,9,10,11,16,17,18,19,24,25,26,27},{4,5,6,7,12,13,14,15,20,21,..., dimensions={0} | all-to-all | bytes 1835008 | tf_op jit(solution)/shard_map/all_to_all | solution.py:608
  41.1 8.1 %shard_map.220 = (f32[16,8,128]{2,1,0:T(8,128)}, bf16[32,16,128]{2,1,0:T(8,128)(2,1)}, f32[128,384]{1,0:T(8,128)}, bf16[128,1152]{1,0:T(8,128)(2,1)}, f32[6,128,...) custom-call(s32[1]{0:T(128)} %bitcast.where, ...), custom_call_target="tpu_custom_call" | custom-call | flops 6600000000 | bytes 6815748 | tf_op jit(solution)/shard_map/pallas_call | solution.py:566
  49.2 3.7 %all-to-all-start.1 = ((f32[16,8,128]{2,1,0:T(8,128)}), f32[16,8,128]{2,1,0:T(8,128)S(1)}, u32[]{:S(2)}, u32[]{:S(2)}) async-start(f32[16,8,128]{2,1,0:T(8,128)} %get-tuple-element.44), calls=%async_computation.1 | async-start | bytes 131072 | tf_op jit(solution)/shard_map/all_to_all | solution.py:608
  52.9 7.4 %all-to-all-done.1.refs_0_ = f32[16,8,128]{2,1,0:T(8,128)S(1)} async-done(((f32[16,8,128]{2,1,0:T(8,128)}), f32[16,8,128]{2,1,0:T(8,128)S(1)}, u32[]{:S(2)}, u32[]{:S(2)}) %all-to-all-start.1) | async-done | bytes 65568 | tf_op jit(solution)/shard_map/all_to_all | solution.py:608
  60.3 0.0 copy-start.5
  60.3 0.6 copy-done.5
  60.9 13.3 %shard_map.221 = (f32[1,4]{1,0:T(1,128)}, bf16[4,128,384]{2,1,0:T(8,128)(2,1)}, bf16[128,1536]{1,0:T(8,128)(2,1)}, bf16[128,384]{1,0:T(8,128)(2,1)}, bf16[128,38...) custom-call(s32[1]{0:T(128)} %bitcast.where, ...), custom_call_target="tpu_custom_call" | custom-call | flops 13200000000 | bytes 9047092 | tf_op jit(solution)/shard_map/pallas_call | solution.py:566
  74.2 0.0 copy-start.4
  74.2 0.0 copy-start.3
  74.2 0.0 copy-start.6
  74.2 3.7 %all-to-all-start.2 = ((bf16[16,32,384]{2,1,0:T(8,128)(2,1)}), bf16[16,32,384]{2,1,0:T(8,128)(2,1)S(1)}, u32[]{:S(2)}, u32[]{:S(2)}) async-start(bf16[16,32,384]{2,1,0:T(8,128)(2,1)} %bitcast.19), calls=%async_computation.2 | async-start | bytes 786432 | tf_op jit(solution)/shard_map/all_to_all | solution.py:608
  77.9 1.2 reshape.71
  79.1 1.2 reshape.72
  80.4 1.0 reshape.73
  81.4 0.0 copy-done.4
  81.4 0.2 reshape.74
  81.6 0.0 copy-done.3
  81.6 0.2 reshape.75
  81.8 0.0 copy-done.6
  81.8 0.1 reshape.76
  81.9 4.3 %shard_map.222 = (bf16[3456,128]{1,0:T(8,128)(2,1)}, bf16[3456,128]{1,0:T(8,128)(2,1)}) custom-call(s32[1]{0:T(128)} %bitcast.5.core, s32[1]{0:T(128)} %bitcast.where, bf16[128,1536]{1,0:T(8,128)(2,1)} %get-tuple-element.68.refs_0_, bf16[128,384]{1,0:T(8,128)(2,1)} %get-tuple-element.69.refs_1_, bf16[128,384]{1,0:T(8,128)(2,1)} %get-tuple-element.70.refs_2_, ...), custom_call_target="tpu_custom_call" | custom-call | flops 5500000256 | bytes 3342344 | tf_op jit(solution)/shard_map/pallas_call | solution.py:566
  86.2 0.0 copy-start.1
  86.2 0.1 collective-permute-start.1
  86.4 0.9 reshape.85
  87.4 0.1 dynamic-slice_convert_fusion
  87.6 0.6 reshape.80.refs_2_
  88.2 0.7 collective-permute-done.1.got
  88.9 0.0 copy-done.1
  89.0 1.4 shard_map.223.refs_14_
  90.3 0.0 all-to-all-done.2.refs_0_
  90.3 0.0 copy-start.2
  90.3 7.2 %all-to-all-start.3 = ((bf16[16,224,128]{2,1,0:T(8,128)(2,1)}), bf16[16,224,128]{2,1,0:T(8,128)(2,1)S(1)}, u32[]{:S(2)}, u32[]{:S(2)}) async-start(bf16[16,224,128]{2,1,0:T(8,128)(2,1)} %shard_map.223.refs_14_), calls=%async_computation.3 | async-start | bytes 1835008 | tf_op jit(solution)/shard_map/all_to_all | solution.py:608
  97.5 0.0 copy-done.2
  97.5 12.3 %shard_map.224 = (bf16[8144,128]{1,0:T(8,128)(2,1)}, bf16[8144,128]{1,0:T(8,128)(2,1)}) custom-call(s32[1]{0:T(128)} %bitcast.5.core, s32[1,32]{1,0:T(1,128)} %ids.3, bf16[16,32,384]{2,1,0:T(8,128)(2,1)} %copy-done.2, bf16[128,768]{1,0:T(8,128)(2,1)} %bitcast.22, bf16[2,80,128]{2,1,0:T(8,128)(2,1)} %reshape.80.refs_2_, bf16[384,1152]{1,0:T(8,128)(2,1)} %refs_3_.7, ...), custom_call_target="tpu_custom_call" | custom-call | flops 14300000256 | bytes 11419780 | tf_op jit(solution)/shard_map/pallas_call | solution.py:566
  109.8 0.1 collective-permute-start.2
  109.9 3.8 %all-to-all-done.3.parts = bf16[16,224,128]{2,1,0:T(8,128)(2,1)S(1)} async-done(((bf16[16,224,128]{2,1,0:T(8,128)(2,1)}), bf16[16,224,128]{2,1,0:T(8,128)(2,1)S(1)}, u32[]{:S(2)}, u32[]{:S(2)}) %all-to-all-start.3) | async-done | bytes 917536 | tf_op jit(solution)/shard_map/all_to_all | solution.py:608
  113.7 0.0 copy-start
  113.7 0.4 shard_map.225.refs_0_.region_in
  114.1 0.2 collective-permute-done.2.got
  114.3 1.0 copy-done
  115.3 1.1 shard_map.226
  116.4 34.7 %all_to_all.31.tile_in = bf16[16,512,128]{2,1,0:T(8,128)(2,1)S(1)} all-to-all(bf16[16,512,128]{2,1,0:T(8,128)(2,1)S(1)} %get-tuple-element.80), channel_id=1, replica_groups={{0,1,2,3,8,9,10,11,16,17,18,19,24,25,26,27},{4,5,6,7,12,13,14,15,20,21,..., dimensions={0} | all-to-all | bytes 4194304 | tf_op jit(solution)/shard_map/all_to_all | solution.py:608
  151.1 1.1 shard_map.227
  152.2 16.6 %all_to_all.32 = bf16[8,128,128]{2,1,0:T(8,128)(2,1)S(1)} all-to-all(bf16[8,128,128]{2,1,0:T(8,128)(2,1)S(1)} %shard_map.227), channel_id=1, replica_groups={{0,4,64,68,128,132,192,196},{1,5,65,69,129,133,193,197},{2,6,66,70,130,..., dimensions={0} | all-to-all | bytes 524288 | tf_op jit(solution)/shard_map/all_to_all | solution.py:608
  168.8 0.6 slice_bitcast_fusion
  169.4 0.6 slice_bitcast_fusion.1
  170.0 0.6 slice_multiply_fusion
  (10 shorter events, 0.2 us)
Async XLA Ops:
  9.8 8.4 %collective-permute-start = (bf16[112,128]{1,0:T(8,128)(2,1)}, bf16[112,128]{1,0:T(8,128)(2,1)S(1)}, u32[]{:S(2)}, u32[]{:S(2)}) collective-permute-start(bf16[112,128]{1,0:T(8,128)(2,1)} %get-tuple-element.43), channel_id=1, source_target_pairs={{0,4},{1,5},{2,6},{3,7},{4,0},{5,1},{6,2},{7,3},{8,12},{9,13},{10,... | collective-permute-start | bytes 86024 | tf_op jit(solution)/shard_map/ppermute | solution.py:665
  49.2 11.1 %all-to-all-start.1 = ((f32[16,8,128]{2,1,0:T(8,128)}), f32[16,8,128]{2,1,0:T(8,128)S(1)}, u32[]{:S(2)}, u32[]{:S(2)}) async-start(f32[16,8,128]{2,1,0:T(8,128)} %get-tuple-element.44), calls=%async_computation.1 | async-start | bytes 131072 | tf_op jit(solution)/shard_map/all_to_all | solution.py:608
  60.3 0.6 copy-start.5
  74.2 7.2 %copy-start.4 = (bf16[192,192]{1,0:T(8,128)(2,1)S(1)}, bf16[192,192]{1,0:T(8,128)(2,1)}, u32[]{:S(2)}) copy-start(bf16[192,192]{1,0:T(8,128)(2,1)} %get-tuple-element.58) | copy-start | bytes 221188
  74.2 7.4 %copy-start.3 = (bf16[192,192]{1,0:T(8,128)(2,1)S(1)}, bf16[192,192]{1,0:T(8,128)(2,1)}, u32[]{:S(2)}) copy-start(bf16[192,192]{1,0:T(8,128)(2,1)} %get-tuple-element.59) | copy-start | bytes 221188
  74.2 7.5 %copy-start.6 = (bf16[192,4]{1,0:T(8,128)(2,1)S(1)}, bf16[192,4]{1,0:T(8,128)(2,1)}, u32[]{:S(2)}) copy-start(bf16[192,4]{1,0:T(8,128)(2,1)} %get-tuple-element.60) | copy-start | bytes 4612
  74.2 16.1 %all-to-all-start.2 = ((bf16[16,32,384]{2,1,0:T(8,128)(2,1)}), bf16[16,32,384]{2,1,0:T(8,128)(2,1)S(1)}, u32[]{:S(2)}, u32[]{:S(2)}) async-start(bf16[16,32,384]{2,1,0:T(8,128)(2,1)} %bitcast.19), calls=%async_computation.2 | async-start | bytes 786432 | tf_op jit(solution)/shard_map/all_to_all | solution.py:608
  86.2 2.7 %copy-start.1 = (bf16[3456,128]{1,0:T(8,128)(2,1)S(1)}, bf16[3456,128]{1,0:T(8,128)(2,1)}, u32[]{:S(2)}) copy-start(bf16[3456,128]{1,0:T(8,128)(2,1)} %get-tuple-element.76.mine) | copy-start | bytes 2654212
  86.2 2.7 %collective-permute-start.1 = (bf16[3456,128]{1,0:T(8,128)(2,1)}, bf16[3456,128]{1,0:T(8,128)(2,1)S(1)}, u32[]{:S(2)}, u32[]{:S(2)}) collective-permute-start(bf16[3456,128]{1,0:T(8,128)(2,1)} %get-tuple-element.77), channel_id=1, source_target_pairs={{0,32},{32,0},{64,96},{96,64},{128,160},{160,128},{192,224},{224,1... | collective-permute-start | bytes 2654216 | tf_op jit(solution)/shard_map/ppermute | solution.py:612
  90.3 7.2 %copy-start.2 = (bf16[16,32,384]{2,1,0:T(8,128)(2,1)}, bf16[16,32,384]{2,1,0:T(8,128)(2,1)S(1)}, u32[]{:S(2)}) copy-start(bf16[16,32,384]{2,1,0:T(8,128)(2,1)S(1)} %all-to-all-done.2.refs_0_) | copy-start | bytes 1179652
  90.3 23.4 %all-to-all-start.3 = ((bf16[16,224,128]{2,1,0:T(8,128)(2,1)}), bf16[16,224,128]{2,1,0:T(8,128)(2,1)S(1)}, u32[]{:S(2)}, u32[]{:S(2)}) async-start(bf16[16,224,128]{2,1,0:T(8,128)(2,1)} %shard_map.223.refs_14_), calls=%async_computation.3 | async-start | bytes 1835008 | tf_op jit(solution)/shard_map/all_to_all | solution.py:608
  109.8 4.4 %collective-permute-start.2 = (bf16[8144,128]{1,0:T(8,128)(2,1)}, bf16[8144,128]{1,0:T(8,128)(2,1)S(1)}, u32[]{:S(2)}, u32[]{:S(2)}) collective-permute-start(bf16[8144,128]{1,0:T(8,128)(2,1)} %get-tuple-element.79), channel_id=1, source_target_pairs={{0,32},{32,0},{64,96},{96,64},{128,160},{160,128},{192,224},{224,1... | collective-permute-start | bytes 6254600 | tf_op jit(solution)/shard_map/ppermute | solution.py:612
  113.7 1.6 copy-start

commit v10 on v9

--- a/solution.py
+++ b/solution.py
@@ -366,8 +366,8 @@
     for i in list(dict.fromkeys(order)):
         late[i] = Late(ins[i], bufs[i], sems[0].at[i])
     early = []
-    for i, (r, b) in enumerate(zip(outs, obufs)):
-        early.append(Early(r, b, osems[0].at[i]) if i != 1 else b)
+    for i, r in enumerate(outs):
+        early.append(Early(r, obufs[i], osems[0].at[i]) if i != 1 else obufs[1])
     message, tails = late[0], late[1]
     slide_weights = [late[i] for i in range(2, 8)]
     w_qkv, w_out, w_up, w_down = [late[i] for i in range(8, 12)]
@@ -411,52 +411,40 @@
         spread[b] = mm_tn(choice(slots, b), grad).astype(BF16)
     leave([(spread.at[2 * y + h], outs[1].at[y]) for y in range(4)], sems[0])
     for e in early:
-        if e is not spread:
+        if isinstance(e, Early):
             e.finish()
 
 
-def two_halves(flat, runs, core, halves, stage, sems):
+def two_halves(flat, runs, core, halves):
     run = 32 * 63
-    copies = []
     for side in range(2):
         which = core if side == 0 else 1 - core
         for z in runs:
             start = pl.multiple_of((2 * z + which) * run, 32)
-            stage[side, z * run : (z + 1) * run, :] = flat[pl.ds(start, run), :].astype(BF16)
-            part = pl.ds(z * run, run)
-            copies.append(pltpu.make_async_copy(stage.at[side, part, :], halves[side].at[part, :], sems.at[side, z]))
-            copies[-1].start()
-    return copies
+            halves[side][z * run : (z + 1) * run, :] = flat[pl.ds(start, run), :].astype(BF16)
 
 
 def region_weights(core, where, *refs):
-    ins, halves, bufs, flat, run_buf, stage, sems, osems = cut(refs, 8, 2, 8, 1, 1, 1, 1, 1)
-    late = [Late(r, b, sems[0].at[i]) for i, (r, b) in enumerate(zip(ins, bufs))]
+    ins, halves, bufs, (flat, run_buf), (sems,) = cut(refs, 8, 2, 8, 2, 1)
+    late = [Late(r, b, sems.at[i]) for i, (r, b) in enumerate(zip(ins, bufs))]
     hidden, grad, second, up_grad, mixture, mid_grad, first, packed_grad = late
-    put_rows(flat[0], 9216, hidden[...], grad[...])
-    put_rows(flat[0], 4608, second[...], up_grad[...])
-    put_rows(flat[0], 3456, mixture[...], mid_grad[...])
-    put_rows(flat[0], 0, first[...], packed_grad[...])
+    put_rows(flat, 9216, hidden[...], grad[...])
+    put_rows(flat, 4608, second[...], up_grad[...])
+    put_rows(flat, 3456, mixture[...], mid_grad[...])
+    put_rows(flat, 0, first[...], packed_grad[...])
     h = lax.rem(where[0] // 4, 2)
-    copies = []
     for side in range(2):
         which = core[0] if side == 0 else 1 - core[0]
         for z in range(4):
             for y in range(4):
                 start = pl.multiple_of((2 * z + which) * 1728 + y * 432 + h * 216, 8)
-                run_buf[0][y * 216 : (y + 1) * 216, :] = flat[0][pl.ds(start, 216), :]
-            part = pl.ds(z * 864, 864)
-            stage[0][side, z * 864 : (z + 1) * 864, :] = run_buf[0][...].astype(BF16)
-            copies.append(pltpu.make_async_copy(stage[0].at[side, part, :], halves[side].at[part, :], osems[0].at[side, z]))
-            copies[-1].start()
-    for copy in copies:
-        copy.wait()
+                run_buf[y * 216 : (y + 1) * 216, :] = flat[pl.ds(start, 216), :]
+            halves[side][z * 864 : (z + 1) * 864, :] = run_buf[...].astype(BF16)
 
 
 def tile_backward(core, ids, *refs):
-    ins, _, halves, bufs, packed_grad, flat, stage, sems, osems = cut(refs, 14, 1, 2, 14, 1, 1, 1, 1, 1)
-    late = [Late(ins[i], bufs[i], sems[0].at[i]) for i in (0, 13, 6, 12, 11, 5, 10, 4, 9, 8, 3, 7, 1, 2)]
-    late = dict(zip((0, 13, 6, 12, 11, 5, 10, 4, 9, 8, 3, 7, 1, 2), late))
+    ins, _, halves, packed_grad, flat = cut(refs, 14, 1, 2, 1, 1)
+    late = ins
     arrived, patches, slide_rows = late[0], late[1], late[2]
     w_qkv, w_out, w_up, w_down = [late[i] for i in range(3, 7)]
     x_ref, res = late[7], [late[i] for i in range(8, 14)]
@@ -473,24 +461,18 @@
     grad = norm_back(grad, normed, rstd)
     bases = (2304, 5760, 6912, 11520)
 
-    leaving = []
 
     def put(i, a, b):
         put_rows(flat[0], bases[i], a, b)
         if i == 2:
-            leaving.extend(two_halves(flat[0], (2, 3), core[0], halves, stage[0], osems[0]))
+            two_halves(flat[0], (2, 3), core[0], halves)
 
     grad = encode_back(grad, x_ref[...], w_qkv, w_out, w_up, w_down, HEADS, res, packed_grad[0], put)
     for side in range(2):
         which = core[0] if side == 0 else 1 - core[0]
-        stage[0][side, 8064:8144, :] = slide_rows.ref()[which]
-        part = pl.ds(8064, 80)
-        leaving.append(pltpu.make_async_copy(stage[0].at[side, part, :], halves[side].at[part, :], osems[0].at[side, 4]))
-        leaving[-1].start()
+        halves[side][8064:8144, :] = slide_rows[which]
     put_rows(flat[0], 0, patches[...], grad.astype(BF16))
-    leaving.extend(two_halves(flat[0], (0, 1), core[0], halves, stage[0], osems[0]))
-    for copy in leaving:
-        copy.wait()
+    two_halves(flat[0], (0, 1), core[0], halves)
 
 
 def fold(rows, pad, tail, mine, got, *refs):
@@ -557,7 +539,7 @@
         copy.wait()
 
 
-def call(kernel, macs, outs, scratch, inputs, scalars=0, whole=0, mebibytes=60):
+def call(kernel, macs, outs, scratch, inputs, scalars=0, whole=0, mebibytes=60, direct=()):
     specs = [pl.BlockSpec(memory_space=pltpu.SMEM)] * scalars
     specs += [pl.BlockSpec(memory_space=pltpu.VMEM)] * whole
     specs += [pl.BlockSpec(memory_space=pl.ANY)] * (len(inputs) - scalars - whole)
@@ -567,7 +549,7 @@
         kernel,
         out_shape=[jax.ShapeDtypeStruct(shape, kind) for shape, kind in outs],
         in_specs=specs,
-        out_specs=[pl.BlockSpec(memory_space=pl.ANY)] * len(outs),
+        out_specs=[pl.BlockSpec(memory_space=pltpu.VMEM if i in direct else pl.ANY) for i in range(len(outs))],
         scratch_shapes=[pltpu.VMEM(*item) if isinstance(item, tuple) else item for item in scratch],
         compiler_params=pltpu.CompilerParams(vmem_limit_bytes=mebibytes * 1024 * 1024),
         cost_estimate=cost,
@@ -704,10 +686,11 @@
         region_weights,
         5 * US,
         [((3456, LANES), BF16)] * 2,
-        like(ins)
-        + [((13824, LANES), F32), ((864, LANES), F32), ((2, 3456, LANES), BF16), semaphores(8), semaphores(2, 4)],
+        like(ins) + [((13824, LANES), F32), ((864, LANES), F32), semaphores(8)],
         (core, where) + ins,
         scalars=2,
+        mebibytes=56,
+        direct=(0, 1),
     )
     (region_chunks,) = folded(mine, other, 54, 8, 0)
     region_parts = exchange(region_chunks, PLANES)
@@ -730,11 +713,12 @@
         tile_backward,
         13 * US,
         [((8144, LANES), BF16)] * 2,
-        like(ins)
-        + [((128, 3 * D), BF16), ((16128, LANES), F32), ((2, 8144, LANES), BF16), semaphores(14), semaphores(2, 5)],
+        [((128, 3 * D), BF16), ((16128, LANES), F32)],
         (core, tile_region) + ins + (region_chunks,),
         scalars=1,
-        whole=1,
+        whole=15,
+        mebibytes=30,
+        direct=(0, 1),
     )
     tile_chunks, slide_sums = folded(mine, other, 63, 8, 1, (region_sums,))
     tile_parts = exchange(tile_chunks, PLANES)

time: 171 us -> 176 us (1.029)
  local copies, waits for them, and re-layouts: 10.4 us -> 18.5 us
  Pallas kernels: 48.8 us -> 43.4 us
    unnamed x19 -> x45, local copies, waits for them, and re-layouts: 1.73 us -> 10.5 us
    pallas_call x7, Pallas kernels: 46.3 us -> 40.9 us  [call(): pl.pallas_call(kernel, out_shape=[jax.ShapeDtypeStruct(shape, kind) for s...]
    ppermute x2, waiting for transfers between devices: 0.94 us -> 4.7 us  [folded(): got = lax.ppermute(other, 'grp', OTHER_CORE)]
    all_to_all x3, waiting for transfers between devices: 11.2 us -> 8.04 us  [exchange(): return lax.all_to_all(array, ALL, 0, 0, axis_index_groups=groups)]
  transfers between devices with their start and end apart: 6 -> 6, of which waited for: 5 -> 5; matrix products, arithmetic and copies ran while one was open for 3% -> 3% of each run, Pallas kernels for 11% -> 7%
where the time goes in v10:
time: 176 us; the launch traced here: 175 us
  blocking collectives  74.3 us (42%)
  Pallas kernels  43.4 us (25%)
  starting transfers between devices  21 us (12%)
  local copies, waits for them, and re-layouts  18.5 us (11%)
  waiting for transfers between devices  14.8 us (8%)
    all_to_all x3, blocking collectives, exchange(): return lax.all_to_all(array, ALL, 0, 0, axis_index_groups=groups)  74.3 us
    pallas_call x7, Pallas kernels, call(): pl.pallas_call(kernel, out_shape=[jax.ShapeDtypeStruct(shape, kind) for s...  40.9 us
    all_to_all x3, starting transfers between devices, exchange(): return lax.all_to_all(array, ALL, 0, 0, axis_index_groups=groups)  14.5 us
    unnamed x45, local copies, waits for them, and re-layouts  10.5 us
    all_to_all x3, waiting for transfers between devices, exchange(): return lax.all_to_all(array, ALL, 0, 0, axis_index_groups=groups)  8.04 us
    ppermute x1, starting transfers between devices, body(): lax.ppermute(message, 'dev', OTHER_PLANE)  6.38 us
    ppermute x2, waiting for transfers between devices, folded(): got = lax.ppermute(other, 'grp', OTHER_CORE)  4.7 us
    reshape x6, local copies, waits for them, and re-layouts, body(): g.astype(F32).reshape(-1)  3.89 us
  transfers between devices with their start and end apart: 6, of which 5 were waited for; matrix products, arithmetic and copies ran while one was open for 3% of the time, Pallas kernels for 7%

profile of v10, /device:TPU:32, one launch (start us, length us, event | category | flops | bytes accessed | tf_op | source)
XLA Modules:
  0.0 175.0 jit_solution(11792672907578877581)
XLA Ops:
  1.3 1.6 copy.27
  2.9 6.9 %shard_map.219 = (bf16[112,128]{1,0:T(8,128)(2,1)}, f32[128,384]{1,0:T(8,128)}, bf16[128,1152]{1,0:T(8,128)(2,1)}, f32[6,128,128]{2,1,0:T(8,128)}, bf16[128,384]...) custom-call(s32[1]{0:T(128)} %bitcast.where, s32[1,32]{1,0:T(1,128)} %ids.3, ...), custom_call_target="tpu_custom_call" | custom-call | flops 7699999744 | bytes 6516872 | tf_op jit(solution)/shard_map/pallas_call | solution.py:548
  9.8 6.4 %collective-permute-start = (bf16[112,128]{1,0:T(8,128)(2,1)}, bf16[112,128]{1,0:T(8,128)(2,1)S(1)}, u32[]{:S(2)}, u32[]{:S(2)}) collective-permute-start(bf16[112,128]{1,0:T(8,128)(2,1)} %get-tuple-element.43), channel_id=1, source_target_pairs={{0,4},{1,5},{2,6},{3,7},{4,0},{5,1},{6,2},{7,3},{8,12},{9,13},{10,... | collective-permute-start | bytes 86024 | tf_op jit(solution)/shard_map/ppermute | solution.py:647
  16.2 2.1 %collective-permute-done = bf16[112,128]{1,0:T(8,128)(2,1)S(1)} collective-permute-done((bf16[112,128]{1,0:T(8,128)(2,1)}, bf16[112,128]{1,0:T(8,128)(2,1)S(1)}, u32[]{:S(2)}, u32[]{:S(2)}) %collective-permute-start) | collective-permute-done | bytes 28704 | tf_op jit(solution)/shard_map/ppermute | solution.py:647
  18.2 0.8 pad_maximum_fusion
  19.0 0.1 broadcast_in_dim.2
  19.1 22.0 %all_to_all.30.refs_0_ = bf16[16,224,128]{2,1,0:T(8,128)(2,1)} all-to-all(bf16[16,224,128]{2,1,0:T(8,128)(2,1)S(1)} %broadcast_in_dim.2), channel_id=1, replica_groups={{0,1,2,3,8,9,10,11,16,17,18,19,24,25,26,27},{4,5,6,7,12,13,14,15,20,21,..., dimensions={0} | all-to-all | bytes 1835008 | tf_op jit(solution)/shard_map/all_to_all | solution.py:590
  41.1 8.1 %shard_map.220 = (f32[16,8,128]{2,1,0:T(8,128)}, bf16[32,16,128]{2,1,0:T(8,128)(2,1)}, f32[128,384]{1,0:T(8,128)}, bf16[128,1152]{1,0:T(8,128)(2,1)}, f32[6,128,...) custom-call(s32[1]{0:T(128)} %bitcast.where, ...), custom_call_target="tpu_custom_call" | custom-call | flops 6600000000 | bytes 6815748 | tf_op jit(solution)/shard_map/pallas_call | solution.py:548
  49.2 3.7 %all-to-all-start.1 = ((f32[16,8,128]{2,1,0:T(8,128)}), f32[16,8,128]{2,1,0:T(8,128)S(1)}, u32[]{:S(2)}, u32[]{:S(2)}) async-start(f32[16,8,128]{2,1,0:T(8,128)} %get-tuple-element.44), calls=%async_computation.1 | async-start | bytes 131072 | tf_op jit(solution)/shard_map/all_to_all | solution.py:590
  52.9 7.4 %all-to-all-done.1.refs_0_ = f32[16,8,128]{2,1,0:T(8,128)S(1)} async-done(((f32[16,8,128]{2,1,0:T(8,128)}), f32[16,8,128]{2,1,0:T(8,128)S(1)}, u32[]{:S(2)}, u32[]{:S(2)}) %all-to-all-start.1) | async-done | bytes 65568 | tf_op jit(solution)/shard_map/all_to_all | solution.py:590
  60.3 0.6 copy-done.18
  60.9 13.3 %shard_map.221 = (f32[1,4]{1,0:T(1,128)}, bf16[4,128,384]{2,1,0:T(8,128)(2,1)}, bf16[128,1536]{1,0:T(8,128)(2,1)}, bf16[128,384]{1,0:T(8,128)(2,1)}, bf16[128,38...) custom-call(s32[1]{0:T(128)} %bitcast.where, ...), custom_call_target="tpu_custom_call" | custom-call | flops 13200000000 | bytes 9047092 | tf_op jit(solution)/shard_map/pallas_call | solution.py:548
  74.2 0.0 copy-start.17
  74.2 0.0 copy-start.16
  74.2 0.0 copy-start.19
  74.2 3.7 %all-to-all-start.2 = ((bf16[16,32,384]{2,1,0:T(8,128)(2,1)}), bf16[16,32,384]{2,1,0:T(8,128)(2,1)S(1)}, u32[]{:S(2)}, u32[]{:S(2)}) async-start(bf16[16,32,384]{2,1,0:T(8,128)(2,1)} %bitcast.21), calls=%async_computation.2 | async-start | bytes 786432 | tf_op jit(solution)/shard_map/all_to_all | solution.py:590
  77.9 1.2 reshape.71
  79.1 1.2 reshape.72
  80.4 1.0 reshape.73
  81.4 0.0 copy-done.17
  81.4 0.2 reshape.74
  81.6 0.0 copy-done.16
  81.6 0.2 reshape.75
  81.8 0.0 copy-done.19
  81.8 0.1 reshape.76
  81.9 4.3 %shard_map.222 = (bf16[3456,128]{1,0:T(8,128)(2,1)}, bf16[3456,128]{1,0:T(8,128)(2,1)}) custom-call(s32[1]{0:T(128)} %bitcast.5.core, s32[1]{0:T(128)} %bitcast.where, bf16[128,1536]{1,0:T(8,128)(2,1)} %get-tuple-element.68.refs_0_, bf16[128,384]{1,0:T(8,128)(2,1)} %get-tuple-element.69.refs_1_, bf16[128,384]{1,0:T(8,128)(2,1)} %get-tuple-element.70.refs_2_, ...), custom_call_target="tpu_custom_call" | custom-call | flops 5500000256 | bytes 3342344 | tf_op jit(solution)/shard_map/pallas_call | solution.py:548
  86.2 0.1 collective-permute-start.1
  86.4 0.9 reshape.85
  87.4 0.1 dynamic-slice_convert_fusion
  87.6 1.4 collective-permute-done.1.got
  89.0 1.2 copy-done.8
  90.1 0.0 copy-start.10
  90.2 0.0 copy-start.15
  90.2 1.4 shard_map.223.refs_14_
  91.6 0.0 all-to-all-done.2.refs_0_
  91.6 7.2 %all-to-all-start.3 = ((bf16[16,224,128]{2,1,0:T(8,128)(2,1)}), bf16[16,224,128]{2,1,0:T(8,128)(2,1)S(1)}, u32[]{:S(2)}, u32[]{:S(2)}) async-start(bf16[16,224,128]{2,1,0:T(8,128)(2,1)} %shard_map.223.refs_14_), calls=%async_computation.3 | async-start | bytes 1835008 | tf_op jit(solution)/shard_map/all_to_all | solution.py:590
  98.7 0.0 copy-done
  98.7 0.0 copy-done.1
  98.8 0.0 copy-done.4
  98.8 0.0 copy-done.5
  98.8 0.0 copy-done.10
  98.8 0.0 copy-done.15
  98.8 0.0 copy-start.2
  98.8 1.3 copy-done.2
  100.1 1.2 copy-done.3
  101.2 1.1 copy-done.9
  102.4 1.0 copy-done.11
  103.3 0.9 copy-done.12
  104.3 0.9 copy-done.13
  105.2 0.9 copy-done.14
  106.1 6.8 %shard_map.224 = (bf16[8144,128]{1,0:T(8,128)(2,1)S(1)}, bf16[8144,128]{1,0:T(8,128)(2,1)}) custom-call(s32[1]{0:T(128)} %bitcast.5.core, s32[1,32]{1,0:T(1,128)S(1)} %copy-done.5, bf16[16,32,384]{2,1,0:T(8,128)(2,1)S(1)} %all-to-all-done.2.refs_0_, bf16[128,768]{1,0:T(8,128)(2,1)S(1)} %bitcast.20, bf16[2,80,128]{2,1,0:T(8,128)(2,1)S(1)} %reshape.80.refs_2_, ...), custom_call_target="tpu_custom_call" | custom-call | flops 14300000256 | bytes 11419780 | tf_op jit(solution)/shard_map/pallas_call | solution.py:548
  113.0 1.3 copy-done.6
  114.3 0.0 collective-permute-start.2
  114.3 0.6 all-to-all-done.3.parts
  114.9 0.4 shard_map.225.refs_0_.region_in
  115.3 3.3 %collective-permute-done.2.got = bf16[8144,128]{1,0:T(8,128)(2,1)S(1)} collective-permute-done((bf16[8144,128]{1,0:T(8,128)(2,1)}, bf16[8144,128]{1,0:T(8,128)(2,1)S(1)}, u32[]{:S(2)}, u32[]{:S(2)}) %collective-permute-start.2) | collective-permute-done | bytes 2084896 | tf_op jit(solution)/shard_map/ppermute | solution.py:594
  118.6 0.0 copy-done.7
  118.6 1.1 shard_map.226
  119.8 35.7 %all_to_all.31.tile_in = bf16[16,512,128]{2,1,0:T(8,128)(2,1)S(1)} all-to-all(bf16[16,512,128]{2,1,0:T(8,128)(2,1)S(1)} %get-tuple-element.80), channel_id=1, replica_groups={{0,1,2,3,8,9,10,11,16,17,18,19,24,25,26,27},{4,5,6,7,12,13,14,15,20,21,..., dimensions={0} | all-to-all | bytes 4194304 | tf_op jit(solution)/shard_map/all_to_all | solution.py:590
  155.4 1.1 shard_map.227
  156.6 16.6 %all_to_all.32 = bf16[8,128,128]{2,1,0:T(8,128)(2,1)S(1)} all-to-all(bf16[8,128,128]{2,1,0:T(8,128)(2,1)S(1)} %shard_map.227), channel_id=1, replica_groups={{0,4,64,68,128,132,192,196},{1,5,65,69,129,133,193,197},{2,6,66,70,130,..., dimensions={0} | all-to-all | bytes 524288 | tf_op jit(solution)/shard_map/all_to_all | solution.py:590
  173.2 0.6 slice_bitcast_fusion
  173.8 0.6 slice_bitcast_fusion.1
  174.4 0.6 slice_multiply_fusion
  (25 shorter events, 0.2 us)
Async XLA Ops:
  9.8 8.4 %collective-permute-start = (bf16[112,128]{1,0:T(8,128)(2,1)}, bf16[112,128]{1,0:T(8,128)(2,1)S(1)}, u32[]{:S(2)}, u32[]{:S(2)}) collective-permute-start(bf16[112,128]{1,0:T(8,128)(2,1)} %get-tuple-element.43), channel_id=1, source_target_pairs={{0,4},{1,5},{2,6},{3,7},{4,0},{5,1},{6,2},{7,3},{8,12},{9,13},{10,... | collective-permute-start | bytes 86024 | tf_op jit(solution)/shard_map/ppermute | solution.py:647
  49.2 11.1 %all-to-all-start.1 = ((f32[16,8,128]{2,1,0:T(8,128)}), f32[16,8,128]{2,1,0:T(8,128)S(1)}, u32[]{:S(2)}, u32[]{:S(2)}) async-start(f32[16,8,128]{2,1,0:T(8,128)} %get-tuple-element.44), calls=%async_computation.1 | async-start | bytes 131072 | tf_op jit(solution)/shard_map/all_to_all | solution.py:590
  60.3 0.6 copy-start.18
  74.2 7.2 %copy-start.17 = (bf16[192,192]{1,0:T(8,128)(2,1)S(1)}, bf16[192,192]{1,0:T(8,128)(2,1)}, u32[]{:S(2)}) copy-start(bf16[192,192]{1,0:T(8,128)(2,1)} %get-tuple-element.58) | copy-start | bytes 221188
  74.2 7.4 %copy-start.16 = (bf16[192,192]{1,0:T(8,128)(2,1)S(1)}, bf16[192,192]{1,0:T(8,128)(2,1)}, u32[]{:S(2)}) copy-start(bf16[192,192]{1,0:T(8,128)(2,1)} %get-tuple-element.59) | copy-start | bytes 221188
  74.2 7.5 %copy-start.19 = (bf16[192,4]{1,0:T(8,128)(2,1)S(1)}, bf16[192,4]{1,0:T(8,128)(2,1)}, u32[]{:S(2)}) copy-start(bf16[192,4]{1,0:T(8,128)(2,1)} %get-tuple-element.60) | copy-start | bytes 4612
  74.2 17.3 %all-to-all-start.2 = ((bf16[16,32,384]{2,1,0:T(8,128)(2,1)}), bf16[16,32,384]{2,1,0:T(8,128)(2,1)S(1)}, u32[]{:S(2)}, u32[]{:S(2)}) async-start(bf16[16,32,384]{2,1,0:T(8,128)(2,1)} %bitcast.21), calls=%async_computation.2 | async-start | bytes 786432 | tf_op jit(solution)/shard_map/all_to_all | solution.py:590
  86.2 2.7 %collective-permute-start.1 = (bf16[3456,128]{1,0:T(8,128)(2,1)}, bf16[3456,128]{1,0:T(8,128)(2,1)S(1)}, u32[]{:S(2)}, u32[]{:S(2)}) collective-permute-start(bf16[3456,128]{1,0:T(8,128)(2,1)} %get-tuple-element.77), channel_id=1, source_target_pairs={{0,32},{32,0},{64,96},{96,64},{128,160},{160,128},{192,224},{224,1... | collective-permute-start | bytes 2654216 | tf_op jit(solution)/shard_map/ppermute | solution.py:594
  89.0 1.2 copy-start.8
  90.1 8.6 %copy-start = (bf16[4,32,768]{2,1,0:T(8,128)(2,1)S(1)}, bf16[4,32,768]{2,1,0:T(8,128)(2,1)}, u32[]{:S(2)}) copy-start(bf16[4,32,768]{2,1,0:T(8,128)(2,1)} %copy.27) | copy-start | bytes 589828
  90.1 8.6 %copy-start.1 = (bf16[384,1536]{1,0:T(8,128)(2,1)S(1)}, bf16[384,1536]{1,0:T(8,128)(2,1)}, u32[]{:S(2)}) copy-start(bf16[384,1536]{1,0:T(8,128)(2,1)} %refs_5_.5) | copy-start | bytes 3538948
  90.1 8.6 %copy-start.4 = (bf16[384,384]{1,0:T(8,128)(2,1)S(1)}, bf16[384,384]{1,0:T(8,128)(2,1)}, u32[]{:S(2)}) copy-start(bf16[384,384]{1,0:T(8,128)(2,1)} %refs_4_.7) | copy-start | bytes 884740
  90.1 8.6 %copy-start.5 = (s32[1,32]{1,0:T(1,128)S(1)}, s32[1,32]{1,0:T(1,128)}, u32[]{:S(2)}) copy-start(s32[1,32]{1,0:T(1,128)} %ids.3) | copy-start | bytes 388
  90.1 8.6 %copy-start.10 = (f32[6,128,128]{2,1,0:T(8,128)S(1)}, f32[6,128,128]{2,1,0:T(8,128)}, u32[]{:S(2)}) copy-start(f32[6,128,128]{2,1,0:T(8,128)} %get-tuple-element.63.refs_9_) | copy-start | bytes 1179652
  90.2 8.6 %copy-start.15 = (bf16[128,384]{1,0:T(8,128)(2,1)S(1)}, bf16[128,384]{1,0:T(8,128)(2,1)}, u32[]{:S(2)}) copy-start(bf16[128,384]{1,0:T(8,128)(2,1)} %get-tuple-element.64.refs_10_) | copy-start | bytes 294916
  91.6 23.4 %all-to-all-start.3 = ((bf16[16,224,128]{2,1,0:T(8,128)(2,1)}), bf16[16,224,128]{2,1,0:T(8,128)(2,1)S(1)}, u32[]{:S(2)}, u32[]{:S(2)}) async-start(bf16[16,224,128]{2,1,0:T(8,128)(2,1)} %shard_map.223.refs_14_), calls=%async_computation.3 | async-start | bytes 1835008 | tf_op jit(solution)/shard_map/all_to_all | solution.py:590
  98.8 1.3 copy-start.2
  100.1 1.2 copy-start.3
  101.2 1.1 copy-start.9
  102.4 1.0 copy-start.11
  103.3 0.9 copy-start.12
  104.3 0.9 copy-start.13
  105.2 0.9 copy-start.14
  113.0 1.3 copy-start.6
  114.3 4.4 %collective-permute-start.2 = (bf16[8144,128]{1,0:T(8,128)(2,1)}, bf16[8144,128]{1,0:T(8,128)(2,1)S(1)}, u32[]{:S(2)}, u32[]{:S(2)}) collective-permute-start(bf16[8144,128]{1,0:T(8,128)(2,1)} %get-tuple-element.79), channel_id=1, source_target_pairs={{0,32},{32,0},{64,96},{96,64},{128,160},{160,128},{192,224},{224,1... | collective-permute-start | bytes 6254600 | tf_op jit(solution)/shard_map/ppermute | solution.py:594
  114.9 3.7 %copy-start.7 = (bf16[8144,128]{1,0:T(8,128)(2,1)S(1)}, bf16[8144,128]{1,0:T(8,128)(2,1)}, u32[]{:S(2)}) copy-start(bf16[8144,128]{1,0:T(8,128)(2,1)} %copy-done.6) | copy-start | bytes 6254596

commit v11 on v10

--- a/solution.py
+++ b/solution.py
@@ -443,8 +443,10 @@
 
 
 def tile_backward(core, ids, *refs):
-    ins, _, halves, packed_grad, flat = cut(refs, 14, 1, 2, 1, 1)
-    late = ins
+    near, far, _, halves, bufs, packed_grad, flat, sems = cut(refs, 7, 7, 1, 2, 7, 1, 1, 1)
+    arriving = {i: Late(far[i], bufs[i], sems[0].at[i]) for i in (6, 1, 5, 4, 3, 2, 0)}
+    late = list(near[:3]) + [arriving[0], near[3], near[4], arriving[1], arriving[2], arriving[3], near[5], near[6]]
+    late += [arriving[4], arriving[5], arriving[6]]
     arrived, patches, slide_rows = late[0], late[1], late[2]
     w_qkv, w_out, w_up, w_down = [late[i] for i in range(3, 7)]
     x_ref, res = late[7], [late[i] for i in range(8, 14)]
@@ -708,15 +710,17 @@
     slide_rows = lax.dynamic_slice(slide_flat, (zero, zero, y, zero, x, zero), (4, 2, 1, 2, 1, 1155))
     slide_rows = slide_rows.reshape(4, 2, 2, 1155).transpose(1, 0, 2, 3)
     slide_rows = jnp.pad(slide_rows, ((0, 0), (0, 0), (0, 0), (0, 125))).astype(BF16).reshape(2, 80, LANES)
-    ins = (arrived, tokens, slide_rows, tile_qkv, tile_out, tile_up, tile_down) + tuple(tile_kept)
+    x, packed, attend, mixture, mid, up, out = tile_kept
+    near = (arrived, tokens, slide_rows, tile_out, tile_up, attend, mixture)
+    far = (tile_qkv, tile_down, x, packed, mid, up, out)
     mine, other = call(
         tile_backward,
         13 * US,
         [((8144, LANES), BF16)] * 2,
-        [((128, 3 * D), BF16), ((16128, LANES), F32)],
-        (core, tile_region) + ins + (region_chunks,),
+        like(far) + [((128, 3 * D), BF16), ((16128, LANES), F32), semaphores(7)],
+        (core, tile_region) + near + far + (region_chunks,),
         scalars=1,
-        whole=15,
+        whole=8,
         mebibytes=30,
         direct=(0, 1),
     )

time: 176 us -> 179 us (1.017)
  Pallas kernels: 43.4 us -> 46.7 us
    pallas_call x7, Pallas kernels: 40.9 us -> 44.2 us  [call(): pl.pallas_call(kernel, out_shape=[jax.ShapeDtypeStruct(shape, kind) for s...]
  transfers between devices with their start and end apart: 6 -> 6, of which waited for: 5 -> 4; matrix products, arithmetic and copies ran while one was open for 3% -> 3% of each run, Pallas kernels for 7% -> 9%
where the time goes in v11:
time: 179 us; the launch traced here: 178 us
  blocking collectives  74.3 us (42%)
  Pallas kernels  46.7 us (26%)
  starting transfers between devices  21 us (12%)
  local copies, waits for them, and re-layouts  18.5 us (10%)
  waiting for transfers between devices  14.8 us (8%)
    all_to_all x3, blocking collectives, exchange(): return lax.all_to_all(array, ALL, 0, 0, axis_index_groups=groups)  74.3 us
    pallas_call x7, Pallas kernels, call(): pl.pallas_call(kernel, out_shape=[jax.ShapeDtypeStruct(shape, kind) for s...  44.2 us
    all_to_all x3, starting transfers between devices, exchange(): return lax.all_to_all(array, ALL, 0, 0, axis_index_groups=groups)  14.5 us
    unnamed x45, local copies, waits for them, and re-layouts  10.5 us
    all_to_all x3, waiting for transfers between devices, exchange(): return lax.all_to_all(array, ALL, 0, 0, axis_index_groups=groups)  7.4 us
    ppermute x1, starting transfers between devices, body(): lax.ppermute(message, 'dev', OTHER_PLANE)  6.38 us
    ppermute x2, waiting for transfers between devices, folded(): got = lax.ppermute(other, 'grp', OTHER_CORE)  5.32 us
    reshape x6, local copies, waits for them, and re-layouts, body(): g.astype(F32).reshape(-1)  3.89 us
  transfers between devices with their start and end apart: 6, of which 4 were waited for; matrix products, arithmetic and copies ran while one was open for 3% of the time, Pallas kernels for 9%

profile of v11, /device:TPU:32, one launch (start us, length us, event | category | flops | bytes accessed | tf_op | source)
XLA Modules:
  0.0 178.4 jit_solution(7157263454092032297)
XLA Ops:
  1.3 1.6 copy.27
  2.9 6.9 %shard_map.219 = (bf16[112,128]{1,0:T(8,128)(2,1)}, f32[128,384]{1,0:T(8,128)}, bf16[128,1152]{1,0:T(8,128)(2,1)}, f32[6,128,128]{2,1,0:T(8,128)}, bf16[128,384]...) custom-call(s32[1]{0:T(128)} %bitcast.where, s32[1,32]{1,0:T(1,128)} %ids.3, ...), custom_call_target="tpu_custom_call" | custom-call | flops 7699999744 | bytes 6516872 | tf_op jit(solution)/shard_map/pallas_call | solution.py:550
  9.8 6.4 %collective-permute-start = (bf16[112,128]{1,0:T(8,128)(2,1)}, bf16[112,128]{1,0:T(8,128)(2,1)S(1)}, u32[]{:S(2)}, u32[]{:S(2)}) collective-permute-start(bf16[112,128]{1,0:T(8,128)(2,1)} %get-tuple-element.43), channel_id=1, source_target_pairs={{0,4},{1,5},{2,6},{3,7},{4,0},{5,1},{6,2},{7,3},{8,12},{9,13},{10,... | collective-permute-start | bytes 86024 | tf_op jit(solution)/shard_map/ppermute | solution.py:649
  16.2 2.1 %collective-permute-done = bf16[112,128]{1,0:T(8,128)(2,1)S(1)} collective-permute-done((bf16[112,128]{1,0:T(8,128)(2,1)}, bf16[112,128]{1,0:T(8,128)(2,1)S(1)}, u32[]{:S(2)}, u32[]{:S(2)}) %collective-permute-start) | collective-permute-done | bytes 28704 | tf_op jit(solution)/shard_map/ppermute | solution.py:649
  18.2 0.8 pad_maximum_fusion
  19.0 0.1 broadcast_in_dim.2
  19.1 22.0 %all_to_all.30.refs_0_ = bf16[16,224,128]{2,1,0:T(8,128)(2,1)} all-to-all(bf16[16,224,128]{2,1,0:T(8,128)(2,1)S(1)} %broadcast_in_dim.2), channel_id=1, replica_groups={{0,1,2,3,8,9,10,11,16,17,18,19,24,25,26,27},{4,5,6,7,12,13,14,15,20,21,..., dimensions={0} | all-to-all | bytes 1835008 | tf_op jit(solution)/shard_map/all_to_all | solution.py:592
  41.1 8.1 %shard_map.220 = (f32[16,8,128]{2,1,0:T(8,128)}, bf16[32,16,128]{2,1,0:T(8,128)(2,1)}, f32[128,384]{1,0:T(8,128)}, bf16[128,1152]{1,0:T(8,128)(2,1)}, f32[6,128,...) custom-call(s32[1]{0:T(128)} %bitcast.where, ...), custom_call_target="tpu_custom_call" | custom-call | flops 6600000000 | bytes 6815748 | tf_op jit(solution)/shard_map/pallas_call | solution.py:550
  49.2 3.7 %all-to-all-start.1 = ((f32[16,8,128]{2,1,0:T(8,128)}), f32[16,8,128]{2,1,0:T(8,128)S(1)}, u32[]{:S(2)}, u32[]{:S(2)}) async-start(f32[16,8,128]{2,1,0:T(8,128)} %get-tuple-element.44), calls=%async_computation.1 | async-start | bytes 131072 | tf_op jit(solution)/shard_map/all_to_all | solution.py:592
  52.9 7.4 %all-to-all-done.1.refs_0_ = f32[16,8,128]{2,1,0:T(8,128)S(1)} async-done(((f32[16,8,128]{2,1,0:T(8,128)}), f32[16,8,128]{2,1,0:T(8,128)S(1)}, u32[]{:S(2)}, u32[]{:S(2)}) %all-to-all-start.1) | async-done | bytes 65568 | tf_op jit(solution)/shard_map/all_to_all | solution.py:592
  60.3 0.6 copy-done.18
  60.9 13.3 %shard_map.221 = (f32[1,4]{1,0:T(1,128)}, bf16[4,128,384]{2,1,0:T(8,128)(2,1)}, bf16[128,1536]{1,0:T(8,128)(2,1)}, bf16[128,384]{1,0:T(8,128)(2,1)}, bf16[128,38...) custom-call(s32[1]{0:T(128)} %bitcast.where, ...), custom_call_target="tpu_custom_call" | custom-call | flops 13200000000 | bytes 9047092 | tf_op jit(solution)/shard_map/pallas_call | solution.py:550
  74.2 0.0 copy-start.17
  74.2 0.0 copy-start.16
  74.2 0.0 copy-start.19
  74.2 3.7 %all-to-all-start.2 = ((bf16[16,32,384]{2,1,0:T(8,128)(2,1)}), bf16[16,32,384]{2,1,0:T(8,128)(2,1)S(1)}, u32[]{:S(2)}, u32[]{:S(2)}) async-start(bf16[16,32,384]{2,1,0:T(8,128)(2,1)} %bitcast.21), calls=%async_computation.2 | async-start | bytes 786432 | tf_op jit(solution)/shard_map/all_to_all | solution.py:592
  77.9 1.2 reshape.71
  79.1 1.2 reshape.72
  80.4 1.0 reshape.73
  81.4 0.0 copy-done.17
  81.4 0.2 reshape.74
  81.6 0.0 copy-done.16
  81.6 0.2 reshape.75
  81.8 0.0 copy-done.19
  81.8 0.1 reshape.76
  81.9 4.3 %shard_map.222 = (bf16[3456,128]{1,0:T(8,128)(2,1)}, bf16[3456,128]{1,0:T(8,128)(2,1)}) custom-call(s32[1]{0:T(128)} %bitcast.5.core, s32[1]{0:T(128)} %bitcast.where, bf16[128,1536]{1,0:T(8,128)(2,1)} %get-tuple-element.68.refs_0_, bf16[128,384]{1,0:T(8,128)(2,1)} %get-tuple-element.69.refs_1_, bf16[128,384]{1,0:T(8,128)(2,1)} %get-tuple-element.70.refs_2_, ...), custom_call_target="tpu_custom_call" | custom-call | flops 5500000256 | bytes 3342344 | tf_op jit(solution)/shard_map/pallas_call | solution.py:550
  86.2 0.1 collective-permute-start.1
  86.4 0.9 reshape.85
  87.4 0.1 dynamic-slice_convert_fusion
  87.6 1.4 collective-permute-done.1.got
  89.0 1.2 copy-done.8
  90.1 0.0 copy-start.10
  90.2 0.0 copy-start.15
  90.2 1.4 shard_map.223.refs_14_
  91.6 0.0 all-to-all-done.2.refs_0_
  91.6 7.2 %all-to-all-start.3 = ((bf16[16,224,128]{2,1,0:T(8,128)(2,1)}), bf16[16,224,128]{2,1,0:T(8,128)(2,1)S(1)}, u32[]{:S(2)}, u32[]{:S(2)}) async-start(bf16[16,224,128]{2,1,0:T(8,128)(2,1)} %shard_map.223.refs_14_), calls=%async_computation.3 | async-start | bytes 1835008 | tf_op jit(solution)/shard_map/all_to_all | solution.py:592
  98.7 0.0 copy-done
  98.7 0.0 copy-done.1
  98.8 0.0 copy-done.4
  98.8 0.0 copy-done.5
  98.8 0.0 copy-done.10
  98.8 0.0 copy-done.15
  98.8 0.0 copy-start.2
  98.8 1.3 copy-done.2
  100.1 1.2 copy-done.3
  101.2 1.1 copy-done.9
  102.4 1.0 copy-done.11
  103.3 0.9 copy-done.12
  104.3 0.9 copy-done.13
  105.2 0.9 copy-done.14
  106.1 10.2 %shard_map.224 = (bf16[8144,128]{1,0:T(8,128)(2,1)S(1)}, bf16[8144,128]{1,0:T(8,128)(2,1)}) custom-call(s32[1]{0:T(128)} %bitcast.5.core, s32[1,32]{1,0:T(1,128)S(1)} %copy-done.5, bf16[16,32,384]{2,1,0:T(8,128)(2,1)S(1)} %all-to-all-done.2.refs_0_, bf16[128,768]{1,0:T(8,128)(2,1)S(1)} %bitcast.20, bf16[2,80,128]{2,1,0:T(8,128)(2,1)S(1)} %reshape.80.refs_2_, ...), custom_call_target="tpu_custom_call" | custom-call | flops 14300000256 | bytes 11419780 | tf_op jit(solution)/shard_map/pallas_call | solution.py:550
  116.3 0.0 copy-start.6
  116.3 1.3 copy-done.6
  117.6 0.0 collective-permute-start.2
  117.6 0.0 all-to-all-done.3.parts
  117.6 0.4 shard_map.225.refs_0_.region_in
  118.0 4.0 %collective-permute-done.2.got = bf16[8144,128]{1,0:T(8,128)(2,1)S(1)} collective-permute-done((bf16[8144,128]{1,0:T(8,128)(2,1)}, bf16[8144,128]{1,0:T(8,128)(2,1)S(1)}, u32[]{:S(2)}, u32[]{:S(2)}) %collective-permute-start.2) | collective-permute-done | bytes 2084896 | tf_op jit(solution)/shard_map/ppermute | solution.py:596
  122.0 1.1 shard_map.226
  123.1 35.7 %all_to_all.31.tile_in = bf16[16,512,128]{2,1,0:T(8,128)(2,1)S(1)} all-to-all(bf16[16,512,128]{2,1,0:T(8,128)(2,1)S(1)} %get-tuple-element.80), channel_id=1, replica_groups={{0,1,2,3,8,9,10,11,16,17,18,19,24,25,26,27},{4,5,6,7,12,13,14,15,20,21,..., dimensions={0} | all-to-all | bytes 4194304 | tf_op jit(solution)/shard_map/all_to_all | solution.py:592
  158.8 1.1 shard_map.227
  159.9 16.6 %all_to_all.32 = bf16[8,128,128]{2,1,0:T(8,128)(2,1)S(1)} all-to-all(bf16[8,128,128]{2,1,0:T(8,128)(2,1)S(1)} %shard_map.227), channel_id=1, replica_groups={{0,4,64,68,128,132,192,196},{1,5,65,69,129,133,193,197},{2,6,66,70,130,..., dimensions={0} | all-to-all | bytes 524288 | tf_op jit(solution)/shard_map/all_to_all | solution.py:592
  176.5 0.6 slice_bitcast_fusion
  177.2 0.6 slice_bitcast_fusion.1
  177.8 0.6 slice_multiply_fusion
  (25 shorter events, 0.2 us)
Async XLA Ops:
  9.8 8.4 %collective-permute-start = (bf16[112,128]{1,0:T(8,128)(2,1)}, bf16[112,128]{1,0:T(8,128)(2,1)S(1)}, u32[]{:S(2)}, u32[]{:S(2)}) collective-permute-start(bf16[112,128]{1,0:T(8,128)(2,1)} %get-tuple-element.43), channel_id=1, source_target_pairs={{0,4},{1,5},{2,6},{3,7},{4,0},{5,1},{6,2},{7,3},{8,12},{9,13},{10,... | collective-permute-start | bytes 86024 | tf_op jit(solution)/shard_map/ppermute | solution.py:649
  49.2 11.1 %all-to-all-start.1 = ((f32[16,8,128]{2,1,0:T(8,128)}), f32[16,8,128]{2,1,0:T(8,128)S(1)}, u32[]{:S(2)}, u32[]{:S(2)}) async-start(f32[16,8,128]{2,1,0:T(8,128)} %get-tuple-element.44), calls=%async_computation.1 | async-start | bytes 131072 | tf_op jit(solution)/shard_map/all_to_all | solution.py:592
  60.3 0.6 copy-start.18
  74.2 7.2 %copy-start.17 = (bf16[192,192]{1,0:T(8,128)(2,1)S(1)}, bf16[192,192]{1,0:T(8,128)(2,1)}, u32[]{:S(2)}) copy-start(bf16[192,192]{1,0:T(8,128)(2,1)} %get-tuple-element.58) | copy-start | bytes 221188
  74.2 7.4 %copy-start.16 = (bf16[192,192]{1,0:T(8,128)(2,1)S(1)}, bf16[192,192]{1,0:T(8,128)(2,1)}, u32[]{:S(2)}) copy-start(bf16[192,192]{1,0:T(8,128)(2,1)} %get-tuple-element.59) | copy-start | bytes 221188
  74.2 7.5 %copy-start.19 = (bf16[192,4]{1,0:T(8,128)(2,1)S(1)}, bf16[192,4]{1,0:T(8,128)(2,1)}, u32[]{:S(2)}) copy-start(bf16[192,4]{1,0:T(8,128)(2,1)} %get-tuple-element.60) | copy-start | bytes 4612
  74.2 17.3 %all-to-all-start.2 = ((bf16[16,32,384]{2,1,0:T(8,128)(2,1)}), bf16[16,32,384]{2,1,0:T(8,128)(2,1)S(1)}, u32[]{:S(2)}, u32[]{:S(2)}) async-start(bf16[16,32,384]{2,1,0:T(8,128)(2,1)} %bitcast.21), calls=%async_computation.2 | async-start | bytes 786432 | tf_op jit(solution)/shard_map/all_to_all | solution.py:592
  86.2 2.7 %collective-permute-start.1 = (bf16[3456,128]{1,0:T(8,128)(2,1)}, bf16[3456,128]{1,0:T(8,128)(2,1)S(1)}, u32[]{:S(2)}, u32[]{:S(2)}) collective-permute-start(bf16[3456,128]{1,0:T(8,128)(2,1)} %get-tuple-element.77), channel_id=1, source_target_pairs={{0,32},{32,0},{64,96},{96,64},{128,160},{160,128},{192,224},{224,1... | collective-permute-start | bytes 2654216 | tf_op jit(solution)/shard_map/ppermute | solution.py:596
  89.0 1.2 copy-start.8
  90.1 8.6 %copy-start = (bf16[4,32,768]{2,1,0:T(8,128)(2,1)S(1)}, bf16[4,32,768]{2,1,0:T(8,128)(2,1)}, u32[]{:S(2)}) copy-start(bf16[4,32,768]{2,1,0:T(8,128)(2,1)} %copy.27) | copy-start | bytes 589828
  90.1 8.6 %copy-start.1 = (bf16[384,1536]{1,0:T(8,128)(2,1)S(1)}, bf16[384,1536]{1,0:T(8,128)(2,1)}, u32[]{:S(2)}) copy-start(bf16[384,1536]{1,0:T(8,128)(2,1)} %refs_4_.7) | copy-start | bytes 3538948
  90.1 8.6 %copy-start.4 = (bf16[384,384]{1,0:T(8,128)(2,1)S(1)}, bf16[384,384]{1,0:T(8,128)(2,1)}, u32[]{:S(2)}) copy-start(bf16[384,384]{1,0:T(8,128)(2,1)} %refs_3_.7) | copy-start | bytes 884740
  90.1 8.6 %copy-start.5 = (s32[1,32]{1,0:T(1,128)S(1)}, s32[1,32]{1,0:T(1,128)}, u32[]{:S(2)}) copy-start(s32[1,32]{1,0:T(1,128)} %ids.3) | copy-start | bytes 388
  90.1 8.6 %copy-start.10 = (f32[6,128,128]{2,1,0:T(8,128)S(1)}, f32[6,128,128]{2,1,0:T(8,128)}, u32[]{:S(2)}) copy-start(f32[6,128,128]{2,1,0:T(8,128)} %get-tuple-element.61.refs_5_) | copy-start | bytes 1179652
  90.2 8.6 %copy-start.15 = (bf16[128,384]{1,0:T(8,128)(2,1)S(1)}, bf16[128,384]{1,0:T(8,128)(2,1)}, u32[]{:S(2)}) copy-start(bf16[128,384]{1,0:T(8,128)(2,1)} %get-tuple-element.62.refs_6_) | copy-start | bytes 294916
  91.6 26.0 %all-to-all-start.3 = ((bf16[16,224,128]{2,1,0:T(8,128)(2,1)}), bf16[16,224,128]{2,1,0:T(8,128)(2,1)S(1)}, u32[]{:S(2)}, u32[]{:S(2)}) async-start(bf16[16,224,128]{2,1,0:T(8,128)(2,1)} %shard_map.223.refs_14_), calls=%async_computation.3 | async-start | bytes 1835008 | tf_op jit(solution)/shard_map/all_to_all | solution.py:592
  98.8 1.3 copy-start.2
  100.1 1.2 copy-start.3
  101.2 1.1 copy-start.9
  102.4 1.0 copy-start.11
  103.3 0.9 copy-start.12
  104.3 0.9 copy-start.13
  105.2 0.9 copy-start.14
  116.3 1.3 copy-start.6
  117.6 4.4 %collective-permute-start.2 = (bf16[8144,128]{1,0:T(8,128)(2,1)}, bf16[8144,128]{1,0:T(8,128)(2,1)S(1)}, u32[]{:S(2)}, u32[]{:S(2)}) collective-permute-start(bf16[8144,128]{1,0:T(8,128)(2,1)} %get-tuple-element.79), channel_id=1, source_target_pairs={{0,32},{32,0},{64,96},{96,64},{128,160},{160,128},{192,224},{224,1... | collective-permute-start | bytes 6254600 | tf_op jit(solution)/shard_map/ppermute | solution.py:596
  117.6 4.3 %copy-start.7 = (bf16[8144,128]{1,0:T(8,128)(2,1)S(1)}, bf16[8144,128]{1,0:T(8,128)(2,1)}, u32[]{:S(2)}) copy-start(bf16[8144,128]{1,0:T(8,128)(2,1)} %copy-done.6) | copy-start | bytes 6254596
